TPU v7x, 32 devices: a whole 2x2x4 slice. The times are simulated.
32 devices in a mesh: wide: 8 (over z, x), narrow: 4 (over y, core).
Axes of the slice: x: 2, y: 2, z: 4, core: 2. Of those that a mesh axis runs over, the one named last changes fastest.
Arguments:
- tokens_in: bfloat16 [15680, 768], P(('wide', 'narrow')), may hold values from -6 to 6
- cotangent: float32 [15680, 768], P(('wide', 'narrow')), may hold values from -6 to 6
- norm1_gain: float32 [768], replicated, may hold values from 0.25 to 1.75
- norm1_shift: float32 [768], replicated, may hold values from -2 to 2
- w_query: bfloat16 [768, 768], P('wide', 'narrow'), may hold values from -0.3125 to 0.3125
- w_key: bfloat16 [768, 768], P('wide', 'narrow'), may hold values from -0.3125 to 0.3125
- w_value: bfloat16 [768, 768], P('wide', 'narrow'), may hold values from -0.21875 to 0.21875
- w_out: bfloat16 [768, 768], P('narrow', 'wide'), may hold values from -0.625 to 0.625
- norm2_gain: float32 [768], replicated, may hold values from 0.25 to 1.75
- norm2_shift: float32 [768], replicated, may hold values from -2 to 2
- w_up: bfloat16 [768, 3072], P('wide', 'narrow'), may hold values from -0.21875 to 0.21875
- up_bias: float32 [3072], P('narrow'), may hold values from -2.5 to 2.5
- w_down: bfloat16 [3072, 768], P('narrow', 'wide'), may hold values from -0.15625 to 0.15625
- down_bias: float32 [768], replicated, may hold values from -2.5 to 2.5
Outputs:
- layer_out: float32 [15680, 768], P(('wide', 'narrow'))
- grad_tokens: float32 [15680, 768], P(('wide', 'narrow'))
- grad_norm1_gain: float32 [768], replicated
- grad_norm1_shift: float32 [768], replicated
- grad_query: float32 [768, 768], P('wide', 'narrow')
- grad_key: float32 [768, 768], P('wide', 'narrow')
- grad_value: float32 [768, 768], P('wide', 'narrow')
- grad_out: float32 [768, 768], P('narrow', 'wide')
- grad_norm2_gain: float32 [768], replicated
- grad_norm2_shift: float32 [768], replicated
- grad_up: float32 [768, 3072], P('wide', 'narrow')
- grad_up_bias: float32 [3072], P('narrow')
- grad_down: float32 [3072, 768], P('narrow', 'wide')
- grad_down_bias: float32 [768], replicated
All inputs are finite; a program needn't handle non-finite values.
Results may differ from a plain program's by a relative error of at most 0.013.
The roundings to bfloat16 on the way count: a program that leaves them out, or rounds other values in their place, can miss the bound.
Values may be sent and summed in bfloat16 or wider, within the bound.
No kernel may reach another device: no remote copies, remote signals or barrier semaphores. Data moves between devices by JAX's collectives and lax.ppermute only.
A program may use at most 192 MiB of HBM per device.

v0:
```python
import jax
import jax.numpy as jnp
from jax import lax
from jax.sharding import PartitionSpec as P

HEAD_DIM = 64
PATCHES = 196


EPS = 1e-06


def normalize(value, gain, shift):
    mean = jnp.mean(value, axis=1, keepdims=True)
    centred = value - mean
    rstd = lax.rsqrt(jnp.mean(centred * centred, axis=1, keepdims=True) + EPS)
    normed = centred * rstd
    return (normed, rstd, (normed * gain + shift).astype(jnp.bfloat16))


def norm_back(grad, normed, rstd, gain):
    scaled = grad * gain
    first = jnp.mean(scaled, axis=1, keepdims=True)
    second = jnp.mean(scaled * normed, axis=1, keepdims=True)
    back = rstd * (scaled - first - normed * second)
    return (back, jnp.sum(grad * normed, axis=0), jnp.sum(grad, axis=0))


def widen(value):
    return lax.all_gather(value, "narrow", axis=0, tiled=True)


def widen_grad(value):
    return lax.all_gather(value, "narrow", axis=0, tiled=True)


def cross(left, right):
    return lax.dot_general(
        left, right, (((0,), (0,)), ((), ())), preferred_element_type=jnp.float32
    )


def by_rows(left, right):
    return lax.dot_general(
        left, right, (((1,), (1,)), ((), ())), preferred_element_type=jnp.float32
    )


def gelu_exact(value):
    return jax.nn.gelu(value, approximate=False)


def body(
    tokens_in,
    cotangent,
    norm1_gain,
    norm1_shift,
    w_query,
    w_key,
    w_value,
    w_out,
    norm2_gain,
    norm2_shift,
    w_up,
    up_bias,
    w_down,
    down_bias,
):
    heads = w_query.shape[1] // HEAD_DIM
    scale = HEAD_DIM ** (-0.5)
    full_query, full_key, full_value, full_up = (
        lax.all_gather(w_query, "wide", axis=0, tiled=True),
        lax.all_gather(w_key, "wide", axis=0, tiled=True),
        lax.all_gather(w_value, "wide", axis=0, tiled=True),
        lax.all_gather(w_up, "wide", axis=0, tiled=True),
    )
    full_out, full_down = (
        lax.all_gather(w_out, "wide", axis=1, tiled=True),
        lax.all_gather(w_down, "wide", axis=1, tiled=True),
    )
    x_in = tokens_in.astype(jnp.float32)
    normed_one, rstd_one, h_one = normalize(x_in, norm1_gain, norm1_shift)
    wide_one = widen(h_one)
    group_rows = wide_one.shape[0]
    frames = group_rows // PATCHES
    shape_four = (frames, PATCHES, heads, HEAD_DIM)
    query = (
        jnp.dot(wide_one, full_query, preferred_element_type=jnp.float32)
        .astype(jnp.bfloat16)
        .reshape(shape_four)
    )
    key = (
        jnp.dot(wide_one, full_key, preferred_element_type=jnp.float32)
        .astype(jnp.bfloat16)
        .reshape(shape_four)
    )
    value = (
        jnp.dot(wide_one, full_value, preferred_element_type=jnp.float32)
        .astype(jnp.bfloat16)
        .reshape(shape_four)
    )
    scores = jnp.einsum("fqhd,fkhd->fhqk", query, key, preferred_element_type=jnp.float32) * scale
    top = jnp.max(scores, axis=-1, keepdims=True)
    expo = jnp.exp(scores - top)
    summed = jnp.sum(expo, axis=-1, keepdims=True)
    probs = expo / summed
    log_total = top + jnp.log(summed)
    probs_low = probs.astype(jnp.bfloat16)
    mixed = jnp.einsum("fhqk,fkhd->fqhd", probs_low, value, preferred_element_type=jnp.float32)
    mixed = mixed.reshape(group_rows, heads * HEAD_DIM).astype(jnp.bfloat16)
    attended = lax.psum_scatter(
        jnp.dot(mixed, full_out, preferred_element_type=jnp.float32),
        "narrow",
        scatter_dimension=0,
        tiled=True,
    )
    y_mid = x_in + attended
    normed_two, rstd_two, h_two = normalize(y_mid, norm2_gain, norm2_shift)
    wide_two = widen(h_two)
    hidden = jnp.dot(wide_two, full_up, preferred_element_type=jnp.float32) + up_bias
    active, gelu_pull = jax.vjp(gelu_exact, hidden)
    active_low = active.astype(jnp.bfloat16)
    projected = lax.psum_scatter(
        jnp.dot(active_low, full_down, preferred_element_type=jnp.float32),
        "narrow",
        scatter_dimension=0,
        tiled=True,
    )
    layer_out = y_mid + projected + down_bias
    grad_down_bias = jnp.sum(cotangent, axis=0)
    cot_wide = widen_grad(cotangent.astype(jnp.bfloat16))
    grad_down = cross(active_low, cot_wide)
    grad_active = by_rows(cot_wide, full_down)
    grad_hidden = gelu_pull(grad_active)[0]
    grad_up_bias = jnp.sum(grad_hidden, axis=0)
    hidden_low = grad_hidden.astype(jnp.bfloat16)
    grad_up = cross(wide_two, hidden_low)
    grad_h_two = lax.psum_scatter(
        by_rows(hidden_low, full_up), "narrow", scatter_dimension=0, tiled=True
    )
    back_two, grad_gain_two, grad_shift_two = norm_back(
        grad_h_two, normed_two, rstd_two, norm2_gain
    )
    grad_y = cotangent + back_two
    mix_wide = widen_grad(grad_y.astype(jnp.bfloat16))
    grad_out = cross(mixed, mix_wide)
    grad_mixed = by_rows(mix_wide, full_out).astype(jnp.bfloat16).reshape(shape_four)
    again = jnp.einsum("fqhd,fkhd->fhqk", query, key, preferred_element_type=jnp.float32) * scale
    probs_back = jnp.exp(again - log_total)
    probs_back_low = probs_back.astype(jnp.bfloat16)
    grad_probs = jnp.einsum(
        "fqhd,fkhd->fhqk", grad_mixed, value, preferred_element_type=jnp.float32
    )
    grad_scores = probs_back * (
        grad_probs - jnp.sum(probs_back * grad_probs, axis=-1, keepdims=True)
    )
    scores_low = grad_scores.astype(jnp.bfloat16)
    grad_query = (
        (jnp.einsum("fhqk,fkhd->fqhd", scores_low, key, preferred_element_type=jnp.float32) * scale)
        .astype(jnp.bfloat16)
        .reshape(group_rows, -1)
    )
    grad_key = (
        (
            jnp.einsum("fhqk,fqhd->fkhd", scores_low, query, preferred_element_type=jnp.float32)
            * scale
        )
        .astype(jnp.bfloat16)
        .reshape(group_rows, -1)
    )
    grad_value = (
        jnp.einsum(
            "fhqk,fqhd->fkhd", probs_back_low, grad_mixed, preferred_element_type=jnp.float32
        )
        .astype(jnp.bfloat16)
        .reshape(group_rows, -1)
    )
    weight_query = cross(wide_one, grad_query)
    weight_key = cross(wide_one, grad_key)
    weight_value = cross(wide_one, grad_value)
    grad_h_one = (
        by_rows(grad_query, full_query)
        + by_rows(grad_key, full_key)
        + by_rows(grad_value, full_value)
    )
    grad_h_one = lax.psum_scatter(grad_h_one, "narrow", scatter_dimension=0, tiled=True)
    back_one, grad_gain_one, grad_shift_one = norm_back(
        grad_h_one, normed_one, rstd_one, norm1_gain
    )
    grad_tokens = grad_y + back_one
    gain_one, shift_one, gain_two, shift_two, bias_down = lax.psum(
        (grad_gain_one, grad_shift_one, grad_gain_two, grad_shift_two, grad_down_bias),
        ("wide", "narrow"),
    )
    bias_up = lax.psum(grad_up_bias, "wide")
    sum_query, sum_key, sum_value, sum_up = (
        lax.psum_scatter(weight_query, "wide", scatter_dimension=0, tiled=True),
        lax.psum_scatter(weight_key, "wide", scatter_dimension=0, tiled=True),
        lax.psum_scatter(weight_value, "wide", scatter_dimension=0, tiled=True),
        lax.psum_scatter(grad_up, "wide", scatter_dimension=0, tiled=True),
    )
    sum_out, sum_down = (
        lax.psum_scatter(grad_out, "wide", scatter_dimension=1, tiled=True),
        lax.psum_scatter(grad_down, "wide", scatter_dimension=1, tiled=True),
    )
    return (
        layer_out,
        grad_tokens,
        gain_one,
        shift_one,
        sum_query,
        sum_key,
        sum_value,
        sum_out,
        gain_two,
        shift_two,
        sum_up,
        bias_up,
        sum_down,
        bias_down,
    )


def solution(mesh):
    return jax.shard_map(
        body,
        mesh=mesh,
        in_specs=(
            P(("wide", "narrow"), None),
            P(("wide", "narrow"), None),
            P(),
            P(),
            P("wide", "narrow"),
            P("wide", "narrow"),
            P("wide", "narrow"),
            P("narrow", "wide"),
            P(),
            P(),
            P("wide", "narrow"),
            P("narrow"),
            P("narrow", "wide"),
            P(),
        ),
        out_specs=(
            P(("wide", "narrow"), None),
            P(("wide", "narrow"), None),
            P(),
            P(),
            P("wide", "narrow"),
            P("wide", "narrow"),
            P("wide", "narrow"),
            P("narrow", "wide"),
            P(),
            P(),
            P("wide", "narrow"),
            P("narrow"),
            P("narrow", "wide"),
            P(),
        ),
        check_vma=False,
    )
```

profile of v0, /device:TPU:0, one launch (start us, length us, event | category | flops | bytes accessed | tf_op | source)
XLA Modules:
  0.0 912.4 jit_solution(5790752726869401875)
XLA Ops:
  15.0 33.1 %all_gather.34 = bf16[192,768]{0,1:T(8,128)(2,1)S(1)} all-gather(bf16[192,96]{0,1:T(8,128)(2,1)S(1)} %copy.61), channel_id=1, replica_groups=mesh['wide'=8,'narrow'=4] {'wide'}, dimensions={1}, use_global_device_ids=true | all-gather | bytes 331776 | tf_op jit(solution)/shard_map/all_gather | solution.py:78
  48.1 31.0 %all_gather.32 = bf16[768,192]{1,0:T(8,128)(2,1)S(1)} all-gather(bf16[96,192]{1,0:T(8,128)(2,1)S(1)} %copy-done.36), channel_id=1, replica_groups=mesh['wide'=8,'narrow'=4] {'wide'}, dimensions={0}, use_global_device_ids=true | all-gather | bytes 331776 | tf_op jit(solution)/shard_map/all_gather | solution.py:72
  79.2 31.0 %all_gather.33 = bf16[768,192]{1,0:T(8,128)(2,1)S(1)} all-gather(bf16[96,192]{1,0:T(8,128)(2,1)S(1)} %copy-done.37), channel_id=1, replica_groups=mesh['wide'=8,'narrow'=4] {'wide'}, dimensions={0}, use_global_device_ids=true | all-gather | bytes 331776 | tf_op jit(solution)/shard_map/all_gather | solution.py:73
  110.2 31.0 %all_gather.31 = bf16[768,192]{1,0:T(8,128)(2,1)S(1)} all-gather(bf16[96,192]{1,0:T(8,128)(2,1)S(1)} %copy-done.38), channel_id=1, replica_groups=mesh['wide'=8,'narrow'=4] {'wide'}, dimensions={0}, use_global_device_ids=true | all-gather | bytes 331776 | tf_op jit(solution)/shard_map/all_gather | solution.py:74
  141.2 4.4 reshape.116
  149.4 4.4 reshape.110
  153.8 4.4 convolution_convert_fusion.2
  158.1 4.8 reshape.109
  184.9 55.6 %fusion = f32[496,768]{1,0:T(8,128)S(1)} fusion(f32[1960,768]{1,0:T(8,128)} %fusion.65), kind=kCustom, calls=%all-reduce-scatter | all-reduce-scatter fusion | flops 1523713 | bytes 7545344
  243.2 5.0 concatenate
  257.0 26.9 %all-gather.17.cloned.1.call-done = bf16[4,490,768]{2,1,0:T(8,128)(2,1)} async-done(((bf16[1,490,768]{2,1,0:T(8,128)(2,1)}), bf16[4,490,768]{2,1,0:T(8,128)(2,1)}) %all-gather.17.cloned.1.call-update) | async-done | bytes 3010576 | tf_op jit(solution)/shard_map/all_gather | solution.py:30
  288.2 38.9 %all-gather.11.cloned.1.call-done = bf16[768,768]{1,0:T(8,128)(2,1)} async-done(((bf16[96,768]{1,0:T(8,128)(2,1)}), bf16[768,768]{1,0:T(8,128)(2,1)}) %all-gather.11.cloned.1.call-update) | async-done | bytes 1179664 | tf_op jit(solution)/shard_map/all_gather | solution.py:75
  327.1 7.2 fusion.66
  334.3 34.6 %all-gather.13.cloned.1.call-done = bf16[768,768]{0,1:T(8,128)(2,1)} async-done(((bf16[768,96]{0,1:T(8,128)(2,1)}), bf16[768,768]{0,1:T(8,128)(2,1)}) %all-gather.13.cloned.1.call-update) | async-done | bytes 1179664 | tf_op jit(solution)/shard_map/all_gather | solution.py:79
  369.0 19.8 %fusion.61 = (f32[768]{0:T(1024)}, bf16[1960,768]{1,0:T(8,128)(2,1)S(1)}, f32[1960,768]{1,0:T(8,128)}) fusion(f32[1960,768]{1,0:T(8,128)} %fusion.66, f32[768]{0:T(1024)S(1)} %copy-done.48, bf16[1960,768]{1,0:T(8,128)(2,1)} %reshape.120, bf16[768,768]{0,1:T(8,128)(2,1)} %all-gather.13.cloned.1.call-done), kind=kOutput, calls=%fused_computation.101 | convolution fusion | flops 2423500032 | bytes 19249152 | tf_op jit(solution)/shard_map/dot_general | solution.py:44
  390.5 5.1 fusion.34
  395.6 55.5 %fusion.2 = f32[496,768]{1,0:T(8,128)S(1)} fusion(f32[1960,768]{1,0:T(8,128)} %fusion.34), kind=kCustom, calls=%all-reduce-scatter.2 | all-reduce-scatter fusion | flops 1523713 | bytes 7545344
  453.4 4.9 concatenate.2
  461.9 30.3 %all-gather.21.cloned.1.call-done = bf16[4,490,768]{2,1,0:T(8,128)(2,1)} async-done(((bf16[1,490,768]{2,1,0:T(8,128)(2,1)}), bf16[4,490,768]{2,1,0:T(8,128)(2,1)}) %all-gather.21.cloned.1.call-update) | async-done | bytes 3010576 | tf_op jit(solution)/shard_map/all_gather | solution.py:34
  500.9 5.5 multiply_convert_fusion.1
  512.4 7.0 fusion.32
  519.5 22.2 %psum.46 = f32[768]{0:T(1024)} all-reduce(f32[768]{0:T(1024)S(1)} %copy-done.50), channel_id=1, replica_groups=mesh['wide'=8,'narrow'=4] {'wide'}, use_global_device_ids=true, to_apply=%region_29.0 | all-reduce | flops 768 | bytes 6144 | tf_op jit(solution)/shard_map/psum | solution.py:195
  541.7 7.2 fusion.67
  555.0 4.8 fusion.40
  568.8 6.3 multiply_reduce_fusion
  602.1 8.2 add_add_fusion
  610.3 105.3 %fusion.60 = (f32[496,768]{1,0:T(8,128)}, f32[496,768]{1,0:T(8,128)S(1)}) fusion(f32[1960,768]{1,0:T(8,128)} %fusion.67, f32[1960,768]{1,0:T(8,128)} %add_add_fusion), kind=kCustom, calls=%all-reduce-scatter.4 | all-reduce-scatter fusion | flops 3047425 | bytes 15090176
  725.9 5.7 concatenate.3
  734.0 5.7 concatenate.1
  739.8 37.5 %all-reduce.8 = (f32[768]{0:T(1024)}, f32[768]{0:T(1024)}, f32[768]{0:T(1024)}, f32[768]{0:T(1024)}, f32[768]{0:T(1024)}) all-reduce(f32[768]{0:T(1024)S(1)} %get-tuple-element.16, f32[768]{0:T(1024)S(1)} %get-tuple-element.21, f32[768]{0:T(1024)S(1)} %copy-done.45, ...), channel_id=1, replica_groups=mesh['wide'=8,'narrow'=4] {'wide','narrow'}, use_global_device_ids=true, to_apply=%region_16.0 | all-reduce | flops 3840 | bytes 30720 | tf_op jit(solution)/shard_map/psum | solution.py:191
  783.6 55.9 %reduce-scatter.17.cloned.1.call-done = f32[96,192]{1,0:T(8,128)} async-done(((f32[768,192]{1,0:T(8,128)}), f32[96,192]{1,0:T(8,128)}) %reduce-scatter.17.cloned.1.call-update) | async-done | bytes 73744 | tf_op jit(solution)/shard_map/reduce_scatter | solution.py:197
  839.5 65.6 %reduce-scatter.19.cloned.1.call-done = f32[96,192]{1,0:T(8,128)} async-done(((f32[768,192]{1,0:T(8,128)}), f32[96,192]{1,0:T(8,128)}) %reduce-scatter.19.cloned.1.call-update) | async-done | bytes 73744 | tf_op jit(solution)/shard_map/reduce_scatter | solution.py:198
  (210 shorter events, 131.5 us)
Async XLA Ops:
  7.2 134.0 %all-gather.15.cloned.1.call-start = ((), (), s32[]{:S(2)}) async-start(), calls=%async_computation.13 | async-start | bytes 3809280 | tf_op jit(solution)/shard_map/all_gather | solution.py:30
  10.2 38.0 %copy-start.36 = (bf16[96,192]{1,0:T(8,128)(2,1)S(1)}, bf16[96,192]{1,0:T(8,128)(2,1)}, u32[]{:S(2)}) copy-start(bf16[96,192]{1,0:T(8,128)(2,1)} %param.18) | copy-start | bytes 110596
  10.8 68.4 %copy-start.37 = (bf16[96,192]{1,0:T(8,128)(2,1)S(1)}, bf16[96,192]{1,0:T(8,128)(2,1)}, u32[]{:S(2)}) copy-start(bf16[96,192]{1,0:T(8,128)(2,1)} %param.19) | copy-start | bytes 110596
  10.8 99.4 %copy-start.38 = (bf16[96,192]{1,0:T(8,128)(2,1)S(1)}, bf16[96,192]{1,0:T(8,128)(2,1)}, u32[]{:S(2)}) copy-start(bf16[96,192]{1,0:T(8,128)(2,1)} %param.20) | copy-start | bytes 110596
  13.2 239.6 %all-gather.19.cloned.1.call-start = ((), (), s32[]{:S(2)}) async-start(), calls=%async_computation.15 | async-start | bytes 3809280 | tf_op jit(solution)/shard_map/all_gather | solution.py:34
  14.9 269.1 %all-gather.17.cloned.1.call-start = ((), (), s32[]{:S(2)}) async-start(), calls=%async_computation.14 | async-start | bytes 3809280 | tf_op jit(solution)/shard_map/all_gather | solution.py:30
  79.2 74.6 %copy-start.22 = (bf16[768,192]{1,0:T(8,128)(2,1)}, bf16[768,192]{1,0:T(8,128)(2,1)S(1)}, u32[]{:S(2)}) copy-start(bf16[768,192]{1,0:T(8,128)(2,1)S(1)} %all_gather.32) | copy-start | bytes 884740
  110.2 35.4 %copy-start.20 = (bf16[768,192]{1,0:T(8,128)(2,1)}, bf16[768,192]{1,0:T(8,128)(2,1)S(1)}, u32[]{:S(2)}) copy-start(bf16[768,192]{1,0:T(8,128)(2,1)S(1)} %all_gather.33) | copy-start | bytes 884740
  141.2 21.8 %copy-start.24 = (bf16[768,192]{1,0:T(8,128)(2,1)}, bf16[768,192]{1,0:T(8,128)(2,1)S(1)}, u32[]{:S(2)}) copy-start(bf16[768,192]{1,0:T(8,128)(2,1)S(1)} %all_gather.31) | copy-start | bytes 884740
  153.7 16.1 %copy-start.6 = (bf16[10,196,3,64]{1,0,3,2:T(8,128)(2,1)}, bf16[10,196,3,64]{1,0,3,2:T(8,128)(2,1)S(1)}, u32[]{:S(2)}) copy-start(bf16[10,196,3,64]{1,0,3,2:T(8,128)(2,1)S(1)} %reshape.110) | copy-start | bytes 2257924
  184.9 57.1 %copy-start.51 = (u32[32]{0:T(128)S(1)}, u32[32]{0:T(128)}, u32[]{:S(2)}) copy-start(u32[32]{0:T(128)} %constant.84) | copy-start | bytes 388
  240.6 2.7 collective-permute-start
  251.6 75.5 %all-gather.11.cloned.1.call-start = ((), (), s32[]{:S(2)}) async-start(), calls=%async_computation.6 | async-start | bytes 1327104 | tf_op jit(solution)/shard_map/all_gather | solution.py:75
  252.1 116.8 %all-gather.13.cloned.1.call-start = ((), (), s32[]{:S(2)}) async-start(), calls=%async_computation.7 | async-start | bytes 1327104 | tf_op jit(solution)/shard_map/all_gather | solution.py:79
  252.7 239.5 %all-gather.21.cloned.1.call-start = ((), (), s32[]{:S(2)}) async-start(), calls=%async_computation.16 | async-start | bytes 3809280 | tf_op jit(solution)/shard_map/all_gather | solution.py:34
  288.2 80.8 %copy-start.48 = (f32[768]{0:T(1024)S(1)}, f32[768]{0:T(1024)}, u32[]{:S(2)}) copy-start(f32[768]{0:T(1024)} %param.25) | copy-start | bytes 9220
  334.3 56.2 %copy-start.53 = (bf16[768,768]{1,0:T(8,128)(2,1)S(1)}, bf16[768,768]{1,0:T(8,128)(2,1)}, u32[]{:S(2)}) copy-start(bf16[768,768]{1,0:T(8,128)(2,1)} %all-gather.11.cloned.1.call-done) | copy-start | bytes 3538948
  451.1 2.3 collective-permute-start.2
  461.9 34.6 %copy-start.16 = (bf16[1960,192]{0,1:T(8,128)(2,1)S(1)}, bf16[1960,192]{0,1:T(8,128)(2,1)}, u32[]{:S(2)}) copy-start(bf16[1960,192]{0,1:T(8,128)(2,1)} %copy-done.15) | copy-start | bytes 2257924
  461.9 320.1 %reduce-scatter.27.cloned.1.call-start = ((), (), s32[]{:S(2)}) async-start(), calls=%async_computation.17 | async-start | bytes 884736
  500.6 283.0 %reduce-scatter.25.cloned.1.call-start = ((), (), s32[]{:S(2)}) async-start(), calls=%async_computation.12 | async-start | bytes 2654208 | tf_op jit(solution)/shard_map/reduce_scatter | solution.py:204
  512.3 29.3 %copy-start.52 = (bf16[768,768]{0,1:T(8,128)(2,1)S(1)}, bf16[768,768]{0,1:T(8,128)(2,1)}, u32[]{:S(2)}) copy-start(bf16[768,768]{0,1:T(8,128)(2,1)} %all-gather.13.cloned.1.call-done) | copy-start | bytes 3538948
  512.4 271.3 %reduce-scatter.23.cloned.1.call-start = ((), (), s32[]{:S(2)}) async-start(), calls=%async_computation.11 | async-start | bytes 2654208 | tf_op jit(solution)/shard_map/reduce_scatter | solution.py:200
  519.4 264.3 %reduce-scatter.21.cloned.1.call-start = ((), (), s32[]{:S(2)}) async-start(), calls=%async_computation.10 | async-start | bytes 884736 | tf_op jit(solution)/shard_map/reduce_scatter | solution.py:199
  580.3 259.2 %reduce-scatter.17.cloned.1.call-start = ((), (), s32[]{:S(2)}) async-start(), calls=%async_computation.8 | async-start | bytes 884736 | tf_op jit(solution)/shard_map/reduce_scatter | solution.py:197
  602.1 303.0 %reduce-scatter.19.cloned.1.call-start = ((), (), s32[]{:S(2)}) async-start(), calls=%async_computation.9 | async-start | bytes 884736 | tf_op jit(solution)/shard_map/reduce_scatter | solution.py:198
  715.7 10.3 %collective-permute-start.3 = (f32[18,768]{1,0:T(8,128)S(1)}, f32[18,768]{1,0:T(8,128)S(1)}, u32[]{:S(2)}, u32[]{:S(2)}) collective-permute-start(f32[18,768]{1,0:T(8,128)S(1)} %slice.3), channel_id=1, source_target_pairs={{0,1},{1,2},{2,3},{4,5},{5,6},{6,7},{8,9},{9,10},{10,11},{12,13},{... | collective-permute-start | bytes 165896
  721.0 10.7 %copy-start.35 = (f32[490]{0:T(512)S(1)}, f32[490]{0:T(512)}, u32[]{:S(2)}) copy-start(f32[490]{0:T(512)} %copy-done.34) | copy-start | bytes 5884
  721.0 10.7 %copy-start.41 = (f32[768]{0:T(1024)S(1)}, f32[768]{0:T(1024)}, u32[]{:S(2)}) copy-start(f32[768]{0:T(1024)} %param.16) | copy-start | bytes 9220
  721.0 10.7 %copy-start.43 = (f32[490]{0:T(512)S(1)}, f32[490]{0:T(512)}, u32[]{:S(2)}) copy-start(f32[490]{0:T(512)} %copy-done.42) | copy-start | bytes 5884
  722.0 12.1 %collective-permute-start.1 = (f32[18,768]{1,0:T(8,128)S(1)}, f32[18,768]{1,0:T(8,128)S(1)}, u32[]{:S(2)}, u32[]{:S(2)}) collective-permute-start(f32[18,768]{1,0:T(8,128)S(1)} %slice.1), channel_id=1, source_target_pairs={{0,1},{1,2},{2,3},{4,5},{5,6},{6,7},{8,9},{9,10},{10,11},{12,13},{... | collective-permute-start | bytes 165896
  731.8 45.6 %copy-start.49 = (f32[768]{0:T(1024)S(1)}, f32[768]{0:T(1024)}, u32[]{:S(2)}) copy-start(f32[768]{0:T(1024)} %param.27) | copy-start | bytes 9220
  (41 other events, 172.6 us)
Sparse Core Ops, SparseCore 0:
  13.3 30.6 all-gather.14
  45.5 27.9 all-gather.18
  251.7 32.2 all-gather.16
  286.0 41.0 all-gather.10
  329.1 39.8 all-gather.12
  462.0 30.1 all-gather.20
  500.7 62.4 reduce-scatter.26
  567.7 67.9 reduce-scatter.24
  640.2 67.9 reduce-scatter.22
  712.4 61.5 reduce-scatter.20
  777.9 61.6 reduce-scatter.16
  843.6 61.4 reduce-scatter.18
where the time goes:
time: 918 us; the launch traced here: 912 us
  blocking collectives  402 us (44%)
  waiting for transfers between devices  254 us (28%)
  matrix products  120 us (13%)
  local copies, waits for them, and re-layouts  82.4 us (9%)
  other arithmetic  28.7 us (3%)
  between operations  16.1 us (2%)
  starting transfers between devices  9.23 us (1%)
    unnamed x3, blocking collectives  216 us
    reduce_scatter x1, waiting for transfers between devices, body(): lax.psum_scatter(weight_key, 'wide', scatter_dimension=0, tiled=True)  65.6 us
    reduce_scatter x1, waiting for transfers between devices, body(): lax.psum_scatter(weight_query, 'wide', scatter_dimension=0, tiled=True)  55.9 us
    unnamed x129, local copies, waits for them, and re-layouts  50.1 us
    dot_general x6, matrix products, by_rows(): lax.dot_general(left, right, (((1,), (1,)), ((), ())), preferred_element_...  42.2 us
    all_gather x1, waiting for transfers between devices, body(): lax.all_gather(w_up, 'wide', axis=0, tiled=True)  38.9 us
    psum x1, blocking collectives, body(): lax.psum((grad_gain_one, grad_shift_one, grad_gain_two, grad_shift_two, g...  37.5 us
    all_gather x1, waiting for transfers between devices, body(): lax.all_gather(w_down, 'wide', axis=1, tiled=True)  34.6 us
  transfers between devices with their start and end apart: 16, of which 7 were waited for; matrix products, arithmetic and copies ran while one was open for 37% of the time, Pallas kernels for 0%

commit v1 on v0

v1 whole, which is shorter than its diff:
```python
import functools

import jax
import jax.numpy as jnp
from jax import lax
from jax.experimental import pallas as pl
from jax.experimental.pallas import tpu as pltpu
from jax.sharding import PartitionSpec as P

HEAD_DIM = 64
PATCHES = 196
EPS = 1e-06
D = 768
ROWS = 512
BLOCK = 208
FRAMES_AT = (0, 208)
HALF_AT = 400
HALF_ROWS = 112
HALF = PATCHES // 2
HALF_FIRST = 4
SCALE = HEAD_DIM ** (-0.5)
NEG = -1e30
BF = jnp.bfloat16
F32 = jnp.float32
PARAMS = pltpu.CompilerParams(vmem_limit_bytes=56 * 1024 * 1024)


def nn(left, right):
    return jnp.dot(left, right, preferred_element_type=F32)


def nt(left, right):
    return lax.dot_general(left, right, (((1,), (1,)), ((), ())), preferred_element_type=F32)


def tn(left, right):
    return lax.dot_general(left, right, (((0,), (0,)), ((), ())), preferred_element_type=F32)


def lanes_below(shape, bound):
    return lax.broadcasted_iota(jnp.int32, shape, 1) < bound


def ln_stats(value):
    mean = jnp.mean(value, axis=1, keepdims=True)
    centred = value - mean
    rstd = lax.rsqrt(jnp.mean(centred * centred, axis=1, keepdims=True) + EPS)
    return centred * rstd, rstd


def ln_back(grad, normed, rstd, gain):
    scaled = grad * gain
    first = jnp.mean(scaled, axis=1, keepdims=True)
    second = jnp.mean(scaled * normed, axis=1, keepdims=True)
    return rstd * (scaled - first - normed * second)


def split(block):
    return (
        block[:, 0:128],
        block[:, 128:256],
        block[:, 256:384],
        block[:, 512:640],
        block[:, 640:768],
    )


def masked_pair(pair, low):
    zero = jnp.zeros_like(pair)
    return jnp.where(low, pair, zero), jnp.where(low, zero, pair)


def attend(queries, keys, valid):
    q01, qv2 = queries
    k01, v01, kv2, ko2 = keys
    low = lanes_below(q01.shape, 64)
    q0, q1 = masked_pair(q01, low)
    q2 = jnp.where(low, qv2, jnp.zeros_like(qv2))

    def probs(q, k):
        s = jnp.where(valid, nt(q, k) * SCALE, NEG)
        e = jnp.exp(s - jnp.max(s, axis=1, keepdims=True))
        return (e / jnp.sum(e, axis=1, keepdims=True)).astype(BF)

    o0 = nn(probs(q0, k01), v01)
    o1 = nn(probs(q1, k01), v01)
    o2 = nn(probs(q2, ko2), kv2)
    return jnp.concatenate(
        [jnp.where(low, o0, o1), jnp.where(low, 0.0, o2)], axis=1
    ).astype(BF)


def attend_back(queries, keys, dob, valid):
    q01, qv2 = queries
    k01, v01, kv2, ko2 = keys
    low = lanes_below(q01.shape, 64)
    klow = lanes_below(k01.shape, 64)
    d01, d2 = dob[:, 0:128], dob[:, 128:256]
    zero = jnp.zeros_like(d2)
    d2 = jnp.where(low, zero, d2)
    q0, q1 = masked_pair(q01, low)
    d0, d1 = masked_pair(d01, low)
    q2 = jnp.where(low, qv2, jnp.zeros_like(qv2))

    def one(q, k, d, v):
        st = jnp.where(valid, nt(k, q) * SCALE, NEG)
        e = jnp.exp(st - jnp.max(st, axis=0, keepdims=True))
        p = e / jnp.sum(e, axis=0, keepdims=True)
        dp = nt(v, d)
        ds = p * (dp - jnp.sum(p * dp, axis=0, keepdims=True))
        return p.astype(BF), ds.astype(BF)

    p0, s0 = one(q0, k01, d0, v01)
    p1, s1 = one(q1, k01, d1, v01)
    p2, s2 = one(q2, ko2, d2, kv2)
    dq01 = jnp.where(low, tn(s0, k01), tn(s1, k01)) * SCALE
    dk01 = jnp.where(klow, nn(s0, q01), nn(s1, q01)) * SCALE
    dv01 = jnp.where(klow, nn(p0, d01), nn(p1, d01))
    dq2 = tn(s2, ko2) * SCALE
    dk2 = nn(s2, qv2) * SCALE
    dv2 = nn(p2, d2)
    return dq01, dk01, dv01, dq2, dk2, dv2


def pick(mine_ref, theirs_ref, into):
    n = pl.program_id(0)

    @pl.when(n < 2)
    def _():
        into[...] = mine_ref[0]

    @pl.when(n >= 2)
    def _():
        into[...] = theirs_ref[0]


def pack_kernel(wq_ref, wk_ref, wv_ref, wo_ref, wu_ref, wd_ref, attn_ref, mlp_ref):
    def turned(ref):
        size = ref.shape[0]
        at = lax.broadcasted_iota(jnp.int32, (size, size), 0)
        eye = (at == lax.broadcasted_iota(jnp.int32, (size, size), 1)).astype(BF)
        return tn(ref[...], eye).astype(BF)

    wo = turned(wo_ref)
    attn_ref[:, 0:128] = wq_ref[:, :128]
    attn_ref[:, 128:256] = wk_ref[:, :128]
    attn_ref[:, 256:384] = wv_ref[:, :128]
    attn_ref[:, 384:512] = wo[:, :128]
    attn_ref[:, 512:640] = jnp.concatenate([wq_ref[:, 128:], wv_ref[:, 128:]], axis=1)
    attn_ref[:, 640:768] = jnp.concatenate([wk_ref[:, 128:], wo[:, 128:]], axis=1)
    rows = wu_ref.shape[0]
    mlp_ref[:rows] = wu_ref[...]
    mlp_ref[rows:] = turned(wd_ref)


def spread(into, value, odd):
    zero = jnp.zeros_like(value)
    into[PATCHES:BLOCK] = zero[: BLOCK - PATCHES]
    end = HALF_AT + HALF_FIRST + HALF
    into[end:] = zero[: ROWS - end]

    @pl.when(odd == 0)
    def _():
        into[:PATCHES] = value[:PATCHES]
        into[BLOCK:end] = value[PATCHES:]

    @pl.when(odd == 1)
    def _():
        into[:PATCHES] = value[HALF : HALF + PATCHES]
        into[BLOCK : BLOCK + PATCHES] = value[HALF + PATCHES :]
        into[BLOCK + PATCHES : end] = value[:HALF]


def gather_back(into, value, odd):
    end = HALF_AT + HALF_FIRST + HALF

    @pl.when(odd == 0)
    def _():
        into[:PATCHES] = value[:PATCHES]
        into[PATCHES:] = value[BLOCK:end]

    @pl.when(odd == 1)
    def _():
        into[:HALF] = value[BLOCK + PATCHES : end]
        into[HALF : HALF + PATCHES] = value[:PATCHES]
        into[HALF + PATCHES :] = value[BLOCK : BLOCK + PATCHES]


def prep_kernel(info_ref, x_ref, c_ref, gain_ref, shift_ref, xp_ref, cp_ref, cb_ref, h_ref):
    odd = info_ref[ODD]
    spread(xp_ref, x_ref[...].astype(F32), odd)
    spread(cp_ref, c_ref[...], odd)
    cb_ref[...] = cp_ref[...].astype(BF)
    normed, _ = ln_stats(xp_ref[...])
    h_ref[...] = (normed * gain_ref[...] + shift_ref[...]).astype(BF)


def qkv_kernel(info_ref, h_ref, am_ref, at_ref, out_ref, a):
    pick(am_ref, at_ref, a)
    out_ref[0] = nn(h_ref[...], a[...]).astype(BF)


def whole_kernel(info_ref, qkv_ref, o_ref):
    valid = lanes_below((BLOCK, BLOCK), PATCHES)
    for start in FRAMES_AT:
        q01, k01, v01, qv2, ko2 = split(qkv_ref[0, start : start + BLOCK, :])
        o_ref[0, start : start + BLOCK, :] = attend((q01, qv2), (k01, v01, qv2, ko2), valid)


def half_place(shape, axis):
    at = lax.broadcasted_iota(jnp.int32, shape, axis)
    at = jnp.where(at >= HALF_ROWS, at - HALF_ROWS, at)
    return (at >= HALF_FIRST) & (at < HALF_FIRST + HALF)


def joined(mine, other):
    return tuple(jnp.concatenate([a, b], axis=0) for a, b in zip(split(mine)[1:], split(other)[1:]))


def out_kernel(
    info_ref, half_ref, other_ref, o_ref, am_ref, at_ref, x_ref, gain_ref, shift_ref, oo_ref, y_ref, h_ref, a
):
    n = pl.program_id(0)
    pick(am_ref, at_ref, a)
    q01, _, _, qv2, _ = split(half_ref[0])
    keys = joined(half_ref[0], other_ref[0])
    valid = half_place((HALF_ROWS, 2 * HALF_ROWS), 1)
    part = attend((q01, qv2), keys, valid)
    first = lax.broadcasted_iota(jnp.int32, part.shape, 0) < HALF_FIRST
    part = jnp.where(first, o_ref[0, HALF_AT:, :], part)
    oo_ref[0, :HALF_AT, :] = o_ref[0, :HALF_AT, :]
    oo_ref[0, HALF_AT:, :] = part
    o = oo_ref[0]
    z = nt(o[:, :128], a[:, 384:512]) + nt(o[:, 128:], a[:, 640:768])

    @pl.when(n == 0)
    def _():
        y_ref[...] = x_ref[...] + z

    @pl.when(n > 0)
    def _():
        y_ref[...] += z

    @pl.when(n == pl.num_programs(0) - 1)
    def _():
        normed, _ = ln_stats(y_ref[...])
        h_ref[...] = (normed * gain_ref[...] + shift_ref[...]).astype(BF)


def store_blocks(mine_ref, theirs_ref, value, me, first=0):
    n = pl.program_id(0)
    blocks = mine_ref.shape[1]
    rows = value.shape[0] // blocks
    value = value.astype(BF)

    def put(out_ref):
        for w in range(blocks):
            if blocks == 1:
                place = 0
            else:
                r = jnp.bitwise_xor(w, me)
                place = (r & 1) * (blocks // 2) + lax.shift_right_logical(r, 1)
            out_ref[0, place, first * rows : (first + 1) * rows] = value[w * rows : (w + 1) * rows]

    @pl.when(n < 2)
    def _():
        put(mine_ref)

    @pl.when(n >= 2)
    def _():
        put(theirs_ref)


def mlp_kernel(
    info_ref,
    h_ref,
    cb_ref,
    c_ref,
    y_ref,
    gain_ref,
    u_ref,
    d_ref,
    b_ref,
    act_ref,
    dmm_ref,
    dmt_ref,
    db_ref,
    dy_ref,
    dz_ref,
    sums_ref,
    ht,
    ct,
    acc,
    dub,
):
    n = pl.program_id(0)

    @pl.when(n == 0)
    def _():
        ht[...] = h_ref[...].T
        ct[...] = cb_ref[...].T

    for j in range(3):
        cols = slice(256 * j, 256 * j + 256)
        up = u_ref[:, 0, 0, :, cols].reshape(D, 256)
        down = d_ref[:, 0, 0, :, cols].reshape(D, 256)
        u = nn(h_ref[...], up) + b_ref[0, :, cols]
        big = 0.5 * (1.0 + lax.erf(u * (0.5**0.5)))
        small = jnp.exp(-0.5 * u * u) * 0.3989422804014327
        act_ref[0, :, cols] = (u * big).astype(BF)
        du = nn(cb_ref[...], down) * (big + u * small)
        db_ref[0, :, cols] = jnp.sum(du, axis=0, keepdims=True)
        dub[:, cols] = du.astype(BF)
    dh = nt(dub[...], u_ref[...].reshape(D, D))
    store_blocks(dmm_ref, dmt_ref, nn(ht[...], dub[...]), info_ref[WIDE], 0)
    store_blocks(dmm_ref, dmt_ref, nn(ct[...], act_ref[0]), info_ref[WIDE], 1)

    @pl.when(n == 0)
    def _():
        acc[...] = dh

    @pl.when(n > 0)
    def _():
        acc[...] += dh

    @pl.when(n == pl.num_programs(0) - 1)
    def _():
        normed, rstd = ln_stats(y_ref[...])
        grad = acc[...]
        c = c_ref[...]
        dy = c + ln_back(grad, normed, rstd, gain_ref[...])
        dy_ref[...] = dy
        dz_ref[...] = dy.astype(BF)
        sums_ref[0:1, :] = jnp.sum(grad * normed, axis=0, keepdims=True)
        sums_ref[1:2, :] = jnp.sum(grad, axis=0, keepdims=True)
        sums_ref[2:3, :] = jnp.sum(c, axis=0, keepdims=True)


def half_back_kernel(info_ref, dz_ref, am_ref, at_ref, half_ref, other_ref, dob_ref, own_ref, send_ref, a):
    pick(am_ref, at_ref, a)
    dz = dz_ref[...]
    dob_ref[0, :, 0:128] = nn(dz, a[:, 384:512]).astype(BF)
    dob_ref[0, :, 128:256] = nn(dz, a[:, 640:768]).astype(BF)
    dob = dob_ref[0, HALF_AT:, :]
    dob = jnp.where(half_place(dob.shape, 0), dob, jnp.zeros_like(dob))
    q01, _, _, qv2, _ = split(half_ref[0])
    keys = joined(half_ref[0], other_ref[0])
    valid = half_place((2 * HALF_ROWS, HALF_ROWS), 0)
    dq01, dk01, dv01, dq2, dk2, dv2 = attend_back((q01, qv2), keys, dob, valid)
    low = lanes_below(dq2.shape, 64)
    own_ref[0, :, 0:128] = dq01
    own_ref[0, :, 128:256] = dk01[:HALF_ROWS]
    own_ref[0, :, 256:384] = dv01[:HALF_ROWS]
    own_ref[0, :, 384:512] = jnp.zeros_like(dq01)
    own_ref[0, :, 512:640] = jnp.where(low, dq2, dv2[:HALF_ROWS])
    own_ref[0, :, 640:768] = jnp.where(low, dk2[:HALF_ROWS], 0.0)
    send_ref[0, :, 0:128] = dk01[HALF_ROWS:]
    send_ref[0, :, 128:256] = dv01[HALF_ROWS:]
    send_ref[0, :, 256:384] = jnp.where(low, 0.0, dv2[HALF_ROWS:])
    send_ref[0, :, 384:512] = jnp.where(low, dk2[HALF_ROWS:], 0.0)


def whole_back_kernel(info_ref, qkv_ref, dob_ref, out_ref):
    valid = lax.broadcasted_iota(jnp.int32, (BLOCK, BLOCK), 0) < PATCHES
    for start in FRAMES_AT:
        q01, k01, v01, qv2, ko2 = split(qkv_ref[0, start : start + BLOCK, :])
        dob = dob_ref[0, start : start + BLOCK, :]
        inside = lax.broadcasted_iota(jnp.int32, dob.shape, 0) < PATCHES
        dob = jnp.where(inside, dob, jnp.zeros_like(dob))
        dq01, dk01, dv01, dq2, dk2, dv2 = attend_back(
            (q01, qv2), (k01, v01, qv2, ko2), dob, valid
        )
        low = lanes_below(dq2.shape, 64)
        rows = slice(start, start + BLOCK)
        out_ref[0, rows, 0:128] = dq01.astype(BF)
        out_ref[0, rows, 128:256] = dk01.astype(BF)
        out_ref[0, rows, 256:384] = dv01.astype(BF)
        out_ref[0, rows, 384:512] = jnp.zeros_like(dq01).astype(BF)
        out_ref[0, rows, 512:640] = jnp.where(low, dq2, dv2).astype(BF)
        out_ref[0, rows, 640:768] = jnp.where(low, dk2, 0.0).astype(BF)


def first_kernel(
    info_ref, dqkv_ref, own_ref, recv_ref, o_ref, h_ref, dz_ref, dam_ref, dat_ref, dq_ref, ht, dt
):
    n = pl.program_id(0)

    @pl.when(n == 0)
    def _():
        ht[...] = h_ref[...].T
        dt[...] = dz_ref[...].T

    dq_ref[0, :HALF_AT] = dqkv_ref[0, :HALF_AT, :]
    own = own_ref[0]
    recv = recv_ref[0]
    whole = jnp.concatenate(
        [
            own[:, 0:128],
            own[:, 128:384] + recv[:, 0:256],
            own[:, 384:512],
            own[:, 512:768] + recv[:, 256:512],
        ],
        axis=1,
    ).astype(BF)
    first = lax.broadcasted_iota(jnp.int32, whole.shape, 0) < HALF_FIRST
    dq_ref[0, HALF_AT:] = jnp.where(first, dqkv_ref[0, HALF_AT:, :], whole)
    left = nn(ht[...], dq_ref[0, :, 0:384])
    right = nn(ht[...], dq_ref[0, :, 512:768])
    outs = nn(dt[...], o_ref[0])
    value = jnp.concatenate(
        [left, outs[:, 0:128], right[:, 0:128], right[:, 128:256] + outs[:, 128:256]], axis=1
    )
    store_blocks(dam_ref, dat_ref, value, info_ref[WIDE])


def result_kernel(info_ref, act_ref, d_ref, y_ref, bias_ref, out_ref, acc):
    n = pl.program_id(0)
    y2 = nt(act_ref[0], d_ref[...].reshape(D, D))

    @pl.when(n == 0)
    def _():
        acc[...] = y_ref[...] + y2 + bias_ref[...]

    @pl.when(n > 0)
    def _():
        acc[...] += y2

    @pl.when(n == pl.num_programs(0) - 1)
    def _():
        gather_back(out_ref, acc[...], info_ref[ODD])


def tokens_kernel(
    info_ref, dq_ref, am_ref, at_ref, x_ref, dy_ref, gain_ref, grad_ref, sums_ref, acc, weight
):
    n = pl.program_id(0)
    pick(am_ref, at_ref, weight)
    dh = nt(dq_ref[0], weight[...])

    @pl.when(n == 0)
    def _():
        acc[...] = dh

    @pl.when(n > 0)
    def _():
        acc[...] += dh

    @pl.when(n == pl.num_programs(0) - 1)
    def _():
        normed, rstd = ln_stats(x_ref[...])
        grad = acc[...]
        sums_ref[0:1, :] = jnp.sum(grad * normed, axis=0, keepdims=True)
        sums_ref[1:2, :] = jnp.sum(grad, axis=0, keepdims=True)
        gather_back(grad_ref, dy_ref[...] + ln_back(grad, normed, rstd, gain_ref[...]), info_ref[ODD])


WIDE, ORDER, ODD = 0, 1, 5


def fixed(shape):
    return pl.BlockSpec(shape, lambda n, info: (0,) * len(shape))


def panel(shape):
    return pl.BlockSpec((1,) + tuple(shape[1:]), lambda n, info: (n,) + (0,) * (len(shape) - 1))


def gathered(kind):
    def spec(shape):
        block = (shape[0], 1, 1) + tuple(shape[3:])
        return pl.BlockSpec(block, lambda n, info: (0, info[ORDER + n], kind, 0, 0))

    return spec


def mine(shape):
    return pl.BlockSpec(
        (1,) + tuple(shape[1:]), lambda n, info: (jnp.minimum(n, 1),) + (0,) * (len(shape) - 1)
    )


def theirs(shape):
    return pl.BlockSpec(
        (1,) + tuple(shape[1:]), lambda n, info: (jnp.maximum(n - 2, 0),) + (0,) * (len(shape) - 1)
    )


def crossed(shape):
    return pl.BlockSpec(
        (1,) + tuple(shape[1:]), lambda n, info: (lax.rem(n + 2, 4),) + (0,) * (len(shape) - 1)
    )


KINDS = {
    "fixed": fixed,
    "panel": panel,
    "crossed": crossed,
    "mine": mine,
    "theirs": theirs,
    "up": gathered(0),
    "down": gathered(1),
}
PANELS = 4


def call(kernel, info, ins, outs, scratch=(), flops=0, steps=PANELS):
    moved = sum(a.size * a.dtype.itemsize for a, _ in ins)
    return pl.pallas_call(
        kernel,
        grid_spec=pltpu.PrefetchScalarGridSpec(
            num_scalar_prefetch=1,
            grid=(steps,),
            in_specs=[KINDS[k](a.shape) for a, k in ins],
            out_specs=[KINDS[k](s) for s, _, k in outs],
            scratch_shapes=list(scratch),
        ),
        out_shape=[jax.ShapeDtypeStruct(s, d) for s, d, _ in outs],
        compiler_params=PARAMS,
        cost_estimate=pl.CostEstimate(
            flops=int(flops * steps), bytes_accessed=int(moved * 2), transcendentals=0
        ),
    )(info, *[a for a, _ in ins])


SMEM = pl.BlockSpec(memory_space=pltpu.SMEM)


def assemble_kernel(pieces, me_ref, *refs):
    ins, out, sem = refs[:pieces], refs[pieces], refs[pieces + 1]
    rows = ins[0].shape[1]
    copies = []
    for k in range(pieces):
        y, x, near = k // (pieces // 2), (k // 2) % 2, k % 2
        for z in range(ins[k].shape[0]):
            w = jnp.bitwise_xor(me_ref[WIDE], 2 * (2 * z + near) + x)
            at = pl.ds(pl.multiple_of(w * rows, rows), rows)
            copies.append(pltpu.make_async_copy(ins[k].at[z], out.at[y, at], sem.at[len(copies)]))
    for c in copies:
        c.start()
    for c in copies:
        c.wait()


def assemble(me, pieces):
    count = len(pieces)
    rows = pieces[0].shape[1]
    return pl.pallas_call(
        functools.partial(assemble_kernel, count),
        in_specs=[SMEM] + [pl.BlockSpec(memory_space=pl.ANY)] * count,
        out_specs=pl.BlockSpec(memory_space=pltpu.VMEM),
        out_shape=jax.ShapeDtypeStruct((2, 8 * rows, D), BF),
        scratch_shapes=[pltpu.SemaphoreType.DMA((2 * count,))],
        compiler_params=PARAMS,
        cost_estimate=pl.CostEstimate(flops=0, bytes_accessed=4 * 8 * rows * D * 2, transcendentals=0),
    )(me, *pieces)


CORE, LINE_Y, LINE_X, NEAR_Z, FAR_Z = 1, 2, 4, 8, 16


def make_swap(devices):
    def swap(value, bit):
        return lax.ppermute(value, ("wide", "narrow"), [(i, i ^ bit) for i in range(devices)])

    return swap


def after(value, *others):
    return lax.optimization_barrier((value,) + others)[0]


class Gather:
    def __init__(self, swap, me, own):
        self.swap, self.me, self.own = swap, me, own

    def lines(self):
        self.b0 = jnp.stack([self.own, self.swap(self.own, FAR_Z)])
        self.b1 = self.swap(self.b0, NEAR_Z)

    def planes(self, *wait):
        b0, b1 = self.b0, after(self.b1, *wait)
        self.x0, self.y0 = self.swap(b0, LINE_X), self.swap(b0, LINE_Y)
        self.d0 = self.swap(self.x0, LINE_Y)
        self.x1, self.y1 = self.swap(b1, LINE_X), self.swap(b1, LINE_Y)
        self.d1 = self.swap(self.y1, LINE_X)

    def finish(self, *wait):
        pieces = [self.b0, self.b1, self.x0, self.x1, self.y0, self.y1, self.d0, self.d1]
        if wait:
            pieces[0] = after(pieces[0], *wait)
        own = assemble(self.me, pieces)
        return own, self.swap(own, CORE)


def plus(left, right):
    return (left.astype(F32) + right.astype(F32)).astype(BF)


class Scatter:
    def __init__(self, swap, own, other):
        self.swap, self.own, self.state = swap, own, 0
        self.rows = own.shape[2]
        self.flight = (swap(other, CORE),)

    def step(self, *wait):
        swap = self.swap
        got = tuple(after(f, *wait) for f in self.flight) if wait else self.flight
        self.state += 1
        if self.state == 1:
            s = plus(self.own, got[0]).reshape(2, 2, 2, 2, self.rows, D)
            sa, sb = s[:, :, :, 0], s[:, :, :, 1]
            self.keep = sa[:, 0], sb[0]
            self.flight = swap(sa[:, 1], LINE_X), swap(sb[1], LINE_Y)
            return (s,)
        if self.state == 2:
            ta, tb = plus(self.keep[0], got[0]), plus(self.keep[1], got[1])
            self.keep = ta[0], tb[0]
            self.flight = swap(ta[1], LINE_Y), swap(tb[1], LINE_X)
            return (ta, tb)
        if self.state == 3:
            va, vb = plus(self.keep[0], got[0]), plus(self.keep[1], got[1])
            self.keep = va
            self.flight = (swap(vb, NEAR_Z),)
            return (va, vb)
        if self.state == 4:
            w = self.keep.astype(F32) + got[0].astype(F32)
            self.keep = w[0]
            self.flight = (swap(w[1].astype(BF), FAR_Z),)
            return (w,)
        self.result = self.keep + got[0].astype(F32)
        return (self.result,)


def body(
    tokens_in,
    cotangent,
    norm1_gain,
    norm1_shift,
    w_query,
    w_key,
    w_value,
    w_out,
    norm2_gain,
    norm2_shift,
    w_up,
    up_bias,
    w_down,
    down_bias,
    *,
    wide,
    narrow,
):
    direct = wide == 8 and narrow == 4
    wi, ni = lax.axis_index("wide"), lax.axis_index("narrow")
    twin = "crossed" if direct else "panel"
    swap = make_swap(wide * narrow)
    flipped = jnp.array([0, 2, 1, 3], jnp.int32)
    order = jnp.bitwise_xor(ni, flipped) if direct else jnp.arange(PANELS)
    me = wi if direct else jnp.zeros_like(wi)
    info = jnp.concatenate(
        [v.astype(jnp.int32) for v in (me.reshape(1), order, (ni % 2).reshape(1))]
    )
    count, rows = tokens_in.shape[0], w_up.shape[0]
    row = lambda v: v.reshape(1, D)
    room = pltpu.VMEM((D, D), BF)
    wide_row, turned = pltpu.VMEM((ROWS, D), F32), pltpu.VMEM((D, ROWS), BF)
    unit = 2 * ROWS * D * D
    act = ((PANELS, ROWS, D), BF, "panel")
    outs = ((PANELS, ROWS, 256), BF, "panel")
    tokens32, tokens16 = ((ROWS, D), F32, "fixed"), ((ROWS, D), BF, "fixed")
    result32 = ((count, D), F32, "fixed")
    sums = ((8, D), F32, "fixed")

    attn, mlp = pl.pallas_call(
        pack_kernel,
        out_shape=[jax.ShapeDtypeStruct((rows, D), BF), jax.ShapeDtypeStruct((2 * rows, D), BF)],
        compiler_params=PARAMS,
    )(w_query, w_key, w_value, w_out, w_up, w_down)
    x, c, cb, h1 = call(
        prep_kernel,
        info,
        [(tokens_in, "fixed"), (cotangent, "fixed")]
        + [(row(norm1_gain), "fixed"), (row(norm1_shift), "fixed")],
        [tokens32, tokens32, tokens16, tokens16],
        steps=1,
    )
    if direct:
        full = lax.all_gather(mlp, ("wide", "narrow"), axis=0, tiled=False)
        full = full.reshape(wide, narrow, 2, rows, D)
        ga = Gather(swap, info, attn)
        ga.lines()
        ga.planes(h1)
        a_mine, a_theirs = ga.finish()
        biases = jnp.stack([up_bias, swap(up_bias, LINE_Y)])
        biases = jnp.concatenate([biases, swap(biases, CORE)])
    else:

        def whole(v):
            return lax.all_gather(v, "narrow", axis=0, tiled=False)

        full = lax.all_gather(mlp.reshape(2, rows, D), "wide", axis=1, tiled=True)
        full = whole(full)[None]
        a_mine = whole(lax.all_gather(attn, "wide", axis=0, tiled=True))
        a_mine, a_theirs = a_mine[:2], a_mine[2:]
        biases = whole(up_bias)
    blocks = 8 if direct else 1
    grads = [((2, blocks, D // blocks, D), BF, k) for k in ("mine", "theirs")]
    grads2 = [((2, blocks, 2 * D // blocks, D), BF, k) for k in ("mine", "theirs")]
    weights_a = [(a_mine, "mine"), (a_theirs, "theirs")]

    (qkv,) = call(qkv_kernel, info, [(h1, "fixed")] + weights_a, [act], [room], flops=unit)
    half = qkv[:, HALF_AT:, :]
    other = swap(half, CORE)
    (o_part,) = call(whole_kernel, info, [(qkv, "panel")], [outs], flops=unit)
    o, y, h2 = call(
        out_kernel,
        info,
        [(half, "panel"), (other, twin), (o_part, "panel")]
        + weights_a
        + [(x, "fixed"), (row(norm2_gain), "fixed"), (row(norm2_shift), "fixed")],
        [outs, tokens32, tokens16],
        [room],
        flops=unit,
    )
    a, dm_mine, dm_theirs, grad_b, dy, dz, sums2 = call(
        mlp_kernel,
        info,
        [(h2, "fixed"), (cb, "fixed"), (c, "fixed"), (y, "fixed"), (row(norm2_gain), "fixed")]
        + [(full, "up"), (full, "down"), (biases.reshape(PANELS, 1, D), "panel")],
        [act] + grads2 + [((PANELS, 1, D), F32, "panel"), tokens32, tokens16, sums],
        [turned, turned, wide_row, pltpu.VMEM((ROWS, D), BF)],
        flops=5 * unit,
    )
    if direct:
        sm = Scatter(swap, dm_mine, dm_theirs)
    dob, own, send = call(
        half_back_kernel,
        info,
        [(dz, "fixed")] + weights_a + [(half, "panel"), (other, twin)],
        [outs, ((PANELS, HALF_ROWS, D), F32, "panel"), ((PANELS, HALF_ROWS, 512), F32, "panel")],
        [room],
        flops=unit,
    )
    recv = swap(send, CORE)
    if direct:
        dob = after(dob, *sm.step(dob))
    (dqkv,) = call(whole_back_kernel, info, [(qkv, "panel"), (dob, "panel")], [act], flops=2 * unit)
    da_mine, da_theirs, dq = call(
        first_kernel,
        info,
        [(dqkv, "panel"), (own, "panel"), (recv, twin), (o, "panel")]
        + [(h1, "fixed"), (dz, "fixed")],
        grads + [act],
        [turned, turned],
        flops=2 * unit,
    )
    if direct:
        sa = Scatter(swap, da_mine, da_theirs)
        dq = after(dq, *sm.step(dq))
    grad_x, sums1 = call(
        tokens_kernel,
        info,
        [(dq, "panel")]
        + weights_a
        + [(x, "fixed"), (dy, "fixed"), (row(norm1_gain), "fixed")],
        [result32, sums],
        [wide_row, room],
        flops=unit,
    )
    if direct:
        a = after(a, *sa.step(sums1))
    (out,) = call(
        result_kernel,
        info,
        [(a, "panel"), (full, "down"), (y, "fixed"), (row(down_bias), "fixed")],
        [result32],
        [wide_row],
        flops=unit,
    )
    grad_b = grad_b.reshape(PANELS, D)
    if direct:
        back = flipped[jnp.bitwise_xor(ni, jnp.arange(PANELS))]
        small = jnp.concatenate([sums1[:2], sums2[:3], grad_b[back]])

        def reduced(small, bit, *wait):
            small = after(small, *wait)
            return small + swap(small, bit)

        wait = sa.step(out) + sm.step(out)
        small = reduced(small, CORE, *wait)
        wait = sa.step(small) + sm.step(small)
        small = reduced(reduced(small, LINE_Y, *wait), LINE_X)
        wait = sa.step(small) + sm.step(small)
        small = reduced(reduced(small, NEAR_Z, *wait), FAR_Z)
        sa.step()
        grad_a, grad_u, grad_d = sa.result, sm.result[:rows], sm.result[rows:]
    else:

        def shard(own, other):
            v = jnp.concatenate([own, other]).reshape(PANELS, -1, D, D).astype(F32)
            v = lax.psum_scatter(v, "narrow", scatter_dimension=0, tiled=False)
            return lax.psum_scatter(v, "wide", scatter_dimension=1, tiled=True)

        (grad_a,), (grad_u, grad_d) = shard(da_mine, da_theirs), shard(dm_mine, dm_theirs)
        small = lax.psum(jnp.concatenate([sums1[:2], sums2[:3], grad_b]), ("wide", "narrow"))
    pick = lambda low, high: jnp.concatenate([grad_a[:, low : low + 128], grad_a[:, high : high + 64]], axis=1)
    return (
        out,
        grad_x,
        small[0],
        small[1],
        pick(0, 512),
        pick(128, 640),
        pick(256, 576),
        pick(384, 704).T,
        small[2],
        small[3],
        grad_u,
        lax.dynamic_index_in_dim(small, 5 + ni, 0, keepdims=False),
        grad_d.T,
        small[4],
    )


def solution(mesh):
    rows, cols, copied = P("wide", "narrow"), P("narrow", "wide"), P()
    tokens = P(("wide", "narrow"), None)
    return jax.shard_map(
        functools.partial(body, wide=mesh.shape["wide"], narrow=mesh.shape["narrow"]),
        mesh=mesh,
        in_specs=(tokens, tokens, copied, copied, rows, rows, rows, cols)
        + (copied, copied, rows, P("narrow"), cols, copied),
        out_specs=(tokens, tokens, copied, copied, rows, rows, rows, cols)
        + (copied, copied, rows, P("narrow"), cols, copied),
        check_vma=False,
    )
```

time: 918 us -> 279 us (0.30)
  blocking collectives: 402 us -> 0 us
  waiting for transfers between devices: 254 us -> 74.8 us
  matrix products: 120 us -> 0 us
  Pallas kernels: 0 us -> 114 us
  local copies, waits for them, and re-layouts: 82.4 us -> 23.9 us
  starting transfers between devices: 9.23 us -> 37.4 us
  other arithmetic: 28.7 us -> 13 us
    unnamed x3 -> x0, blocking collectives: 216 us -> none
    all_gather x6 -> x1, waiting for transfers between devices: 131 us -> 0.02 us  [body(): full = lax.all_gather(mlp, ('wide', 'narrow'), axis=0, tiled=False)]
    all_gather x4 -> x0, blocking collectives: 126 us -> none  [the longest x1 33.1 us: body(): lax.all_gather(w_out, 'wide', axis=1, tiled=True)]
    reduce_scatter x5 -> x0, waiting for transfers between devices: 121 us -> none  [the longest x1 65.6 us: body(): lax.psum_scatter(weight_key, 'wide', scatter_dimension=0, tiled=True)]
    dot_general x23 -> x0, matrix products: 116 us -> none  [the longest x6 42.2 us: by_rows(): lax.dot_general(left, right, (((1,), (1,)), ((), ())), preferred_element_...]
    pallas_call x0 -> x12, Pallas kernels: none -> 114 us  [the longest x10 108 us: call(): pl.pallas_call(kernel, grid_spec=pltpu.PrefetchScalarGridSpec(num_scalar_...]
    ppermute x0 -> x32, waiting for transfers between devices: none -> 74.8 us  [swap(): lax.ppermute(value, ('wide', 'narrow'), [(i, i ^ bit) for i in range(devi...]
    psum x2 -> x0, blocking collectives: 59.7 us -> none  [the longest x1 37.5 us: body(): lax.psum((grad_gain_one, grad_shift_one, grad_gain_two, grad_shift_two, g...]
  transfers between devices with their start and end apart: 16 -> 33, of which waited for: 7 -> 19; matrix products, arithmetic and copies ran while one was open for 37% -> 10% of each run, Pallas kernels for 0% -> 31%
where the time goes in v1:
time: 279 us; the launch traced here: 278 us
  Pallas kernels  114 us (41%)
  waiting for transfers between devices  74.8 us (27%)
  starting transfers between devices  37.4 us (13%)
  local copies, waits for them, and re-layouts  23.9 us (9%)
  between operations  14.5 us (5%)
  other arithmetic  13 us (5%)
    pallas_call x10, Pallas kernels, call(): pl.pallas_call(kernel, grid_spec=pltpu.PrefetchScalarGridSpec(num_scalar_...  108 us
    ppermute x32, waiting for transfers between devices, swap(): lax.ppermute(value, ('wide', 'narrow'), [(i, i ^ bit) for i in range(devi...  74.8 us
    ppermute x32, starting transfers between devices, swap(): lax.ppermute(value, ('wide', 'narrow'), [(i, i ^ bit) for i in range(devi...  37.4 us
    convert_element_type x9, other arithmetic, plus(): return (left.astype(F32) + right.astype(F32)).astype(BF)  9.16 us
    unnamed x47, local copies, waits for them, and re-layouts  6.96 us
  transfers between devices with their start and end apart: 33, of which 19 were waited for; matrix products, arithmetic and copies ran while one was open for 10% of the time, Pallas kernels for 31%

profile of v1, /device:TPU:0, one launch (start us, length us, event | category | flops | bytes accessed | tf_op | source)
XLA Modules:
  0.0 277.7 jit_solution(14116975078376529801)
XLA Ops:
  9.0 2.2 shard_map.255
  11.1 4.1 %collective-permute-start = (bf16[96,768]{1,0:T(8,128)(2,1)}, bf16[96,768]{1,0:T(8,128)(2,1)S(1)}, u32[]{:S(2)}, u32[]{:S(2)}) collective-permute-start(bf16[96,768]{1,0:T(8,128)(2,1)} %get-tuple-element.59), channel_id=1, source_target_pairs={{0,16},{1,17},{2,18},{3,19},{4,20},{5,21},{6,22},{7,23},{8,24},{9,... | collective-permute-start | bytes 442376 | tf_op jit(solution)/shard_map/ppermute | solution.py:563
  17.8 4.7 %collective-permute-done = bf16[96,768]{1,0:T(8,128)(2,1)S(1)} collective-permute-done((bf16[96,768]{1,0:T(8,128)(2,1)}, bf16[96,768]{1,0:T(8,128)(2,1)S(1)}, u32[]{:S(2)}, u32[]{:S(2)}) %collective-permute-start) | collective-permute-done | bytes 147488 | tf_op jit(solution)/shard_map/ppermute | solution.py:563
  24.9 4.8 %shard_map.254 = (f32[512,768]{1,0:T(8,128)}, f32[512,768]{1,0:T(8,128)}, bf16[512,768]{1,0:T(8,128)(2,1)}, bf16[512,768]{1,0:T(8,128)(2,1)}) custom-call(s32[6]{0:T(128)} %pad_add_fusion.info_ref.me_ref, bf16[490,768]{1,0:T(8,128)(2,1)} %x_ref.1, f32[490,768]{1,0:T(8,128)} %c_ref.1, f32[1,768]{1,0:T(1,128)} %reshape.123.gain_ref, f32[1,768]{1,0:T(1,128)} %reshape.124.shift_ref), custom_call_target="tpu_custom_call" | custom-call | bytes 4528128 | tf_op jit(solution)/shard_map/pallas_call | solution.py:508
  31.2 6.5 %collective-permute-done.1.refs_1_ = bf16[2,96,768]{2,1,0:T(8,128)(2,1)S(1)} collective-permute-done((bf16[2,96,768]{2,1,0:T(8,128)(2,1)S(1)}, bf16[2,96,768]{2,1,0:T(8,128)(2,1)S(1)}, u32[]{:S(2)}, u32[]{:S(2)}) %collective-permute-start.1) | collective-permute-done | bytes 294944 | tf_op jit(solution)/shard_map/ppermute | solution.py:563
  42.6 6.6 %collective-permute-done.5.refs_5_ = bf16[2,96,768]{2,1,0:T(8,128)(2,1)S(1)} collective-permute-done((bf16[2,96,768]{2,1,0:T(8,128)(2,1)S(1)}, bf16[2,96,768]{2,1,0:T(8,128)(2,1)S(1)}, u32[]{:S(2)}, u32[]{:S(2)}) %collective-permute-start.5) | collective-permute-done | bytes 294944 | tf_op jit(solution)/shard_map/ppermute | solution.py:563
  50.3 7.9 %collective-permute-done.4.refs_4_ = bf16[2,96,768]{2,1,0:T(8,128)(2,1)S(1)} collective-permute-done((bf16[2,96,768]{2,1,0:T(8,128)(2,1)S(1)}, bf16[2,96,768]{2,1,0:T(8,128)(2,1)S(1)}, u32[]{:S(2)}, u32[]{:S(2)}) %collective-permute-start.4) | collective-permute-done | bytes 294944 | tf_op jit(solution)/shard_map/ppermute | solution.py:563
  58.2 4.4 %collective-permute-done.6.refs_6_ = bf16[2,96,768]{2,1,0:T(8,128)(2,1)S(1)} collective-permute-done((bf16[2,96,768]{2,1,0:T(8,128)(2,1)S(1)}, bf16[2,96,768]{2,1,0:T(8,128)(2,1)S(1)}, u32[]{:S(2)}, u32[]{:S(2)}) %collective-permute-start.6) | collective-permute-done | bytes 294944 | tf_op jit(solution)/shard_map/ppermute | solution.py:563
  64.2 3.9 %shard_map.256.am_ref = bf16[2,768,768]{2,1,0:T(8,128)(2,1)} custom-call(s32[6]{0:T(128)} %pad_add_fusion.info_ref.me_ref, bf16[2,96,768]{2,1,0:T(8,128)(2,1)} %copy-done.4, bf16[2,96,768]{2,1,0:T(8,128)(2,1)} %copy-done.6, bf16[2,96,768]{2,1,0:T(8,128)(2,1)} %copy-done.7, bf16[2,96,768]{2,1,0:T(8,128)(2,1)} %copy-done.10, bf16[2,96,768]{2,1,0:T(8,128)(2,1)} %copy-done.9, ...), custom_call_target="tpu_custom_call" | custom-call | bytes 4718592 | tf_op jit(solution)/shard_map/pallas_call | solution.py:547
  68.2 4.7 %collective-permute-done.8.at_ref = bf16[2,768,768]{2,1,0:T(8,128)(2,1)S(1)} collective-permute-done((bf16[2,768,768]{2,1,0:T(8,128)(2,1)}, bf16[2,768,768]{2,1,0:T(8,128)(2,1)S(1)}, u32[]{:S(2)}, u32[]{:S(2)}) %collective-permute-start.8) | collective-permute-done | bytes 2359328 | tf_op jit(solution)/shard_map/ppermute | solution.py:563
  74.3 7.8 %shard_map.257.qkv_ref = bf16[4,512,768]{2,1,0:T(8,128)(2,1)} custom-call(s32[6]{0:T(128)} %pad_add_fusion.info_ref.me_ref, bf16[512,768]{1,0:T(8,128)(2,1)} %get-tuple-element.58.h_ref, bf16[2,768,768]{2,1,0:T(8,128)(2,1)} %shard_map.256.am_ref, bf16[2,768,768]{2,1,0:T(8,128)(2,1)} %copy-done.2), custom_call_target="tpu_custom_call" | custom-call | flops 2415919104 | bytes 11010048 | tf_op jit(solution)/shard_map/pallas_call | solution.py:508
  89.1 7.4 %shard_map.258.o_ref = bf16[4,512,256]{2,1,0:T(8,128)(2,1)} custom-call(s32[6]{0:T(128)} %pad_add_fusion.info_ref.me_ref, bf16[4,512,768]{2,1,0:T(8,128)(2,1)} %shard_map.257.qkv_ref), custom_call_target="tpu_custom_call" | custom-call | flops 2415919104 | bytes 6291456 | tf_op jit(solution)/shard_map/pallas_call | solution.py:508
  97.4 13.3 %shard_map.259 = (bf16[4,512,256]{2,1,0:T(8,128)(2,1)}, f32[512,768]{1,0:T(8,128)}, bf16[512,768]{1,0:T(8,128)(2,1)}) custom-call(s32[6]{0:T(128)} %pad_add_fusion.info_ref.me_ref, bf16[4,112,768]{2,1,0:T(8,128)(2,1)} %copy-done.5, bf16[4,112,768]{2,1,0:T(8,128)(2,1)} %copy-done.19, bf16[4,512,256]{2,1,0:T(8,128)(2,1)} %shard_map.258.o_ref, ...), custom_call_target="tpu_custom_call" | custom-call | flops 2415919104 | bytes 17444864 | tf_op jit(solution)/shard_map/pallas_call | solution.py:508
  110.7 26.6 %shard_map.260 = (bf16[4,512,768]{2,1,0:T(8,128)(2,1)}, bf16[2,8,192,768]{3,2,1,0:T(8,128)(2,1)}, bf16[2,8,192,768]{3,2,1,0:T(8,128)(2,1)}, f32[4,1,768]{2,1,0:T...) custom-call(s32[6]{0:T(128)} %pad_add_fusion.info_ref.me_ref, ...), custom_call_target="tpu_custom_call" | custom-call | flops 12079595520 | bytes 47216640 | tf_op jit(solution)/shard_map/pallas_call | solution.py:508
  137.9 9.0 %shard_map.261 = (bf16[4,512,256]{2,1,0:T(8,128)(2,1)}, f32[4,112,768]{2,1,0:T(8,128)}, f32[4,112,512]{2,1,0:T(8,128)}) custom-call(s32[6]{0:T(128)} %pad_add_fusion.info_ref.me_ref, bf16[512,768]{1,0:T(8,128)(2,1)} %get-tuple-element.68.dz_ref, bf16[2,768,768]{2,1,0:T(8,128)(2,1)} %shard_map.256.am_ref, bf16[2,768,768]{2,1,0:T(8,128)(2,1)} %copy-done.2, ...), custom_call_target="tpu_custom_call" | custom-call | flops 2415919104 | bytes 13762560 | tf_op jit(solution)/shard_map/pallas_call | solution.py:508
  147.0 3.8 %add_convert_fusion = bf16[2,8,192,768]{3,2,1,0:T(8,128)(2,1)S(1)} fusion(bf16[2,8,192,768]{3,2,1,0:T(8,128)(2,1)} %collective-permute-done.12, bf16[2,8,192,768]{3,2,1,0:T(8,128)(2,1)S(1)} %bitcast.110), kind=kLoop, calls=%fused_computation.2 | loop fusion | flops 9437184 | bytes 14155776 | tf_op jit(solution)/shard_map/convert_element_type | solution.py:596
  156.6 9.1 %shard_map.262.dqkv_ref = bf16[4,512,768]{2,1,0:T(8,128)(2,1)} custom-call(s32[6]{0:T(128)} %pad_add_fusion.info_ref.me_ref, bf16[4,512,768]{2,1,0:T(8,128)(2,1)} %shard_map.257.qkv_ref, bf16[4,512,256]{2,1,0:T(8,128)(2,1)} %get-tuple-element.73.dob_ref), custom_call_target="tpu_custom_call" | custom-call | flops 4831838208 | bytes 8388608 | tf_op jit(solution)/shard_map/pallas_call | solution.py:508
  165.7 10.5 %shard_map.263 = (bf16[2,8,96,768]{3,2,1,0:T(8,128)(2,1)}, bf16[2,8,96,768]{3,2,1,0:T(8,128)(2,1)}, bf16[4,512,768]{2,1,0:T(8,128)(2,1)}) custom-call(s32[6]{0:T(128)} %pad_add_fusion.info_ref.me_ref, bf16[4,512,768]{2,1,0:T(8,128)(2,1)} %shard_map.262.dqkv_ref, f32[4,112,768]{2,1,0:T(8,128)} %get-tuple-element.74.own_ref, ...), custom_call_target="tpu_custom_call" | custom-call | flops 4831838208 | bytes 16121856 | tf_op jit(solution)/shard_map/pallas_call | solution.py:508
  180.7 2.9 %collective-permute-done.15 = bf16[2,2,192,768]{3,2,1,0:T(8,128)(2,1)} collective-permute-done((bf16[2,2,192,768]{3,2,1,0:T(8,128)(2,1)}, bf16[2,2,192,768]{3,2,1,0:T(8,128)(2,1)}, u32[]{:S(2)}, u32[]{:S(2)}) %collective-permute-start.15) | collective-permute-done | bytes 1179680 | tf_op jit(solution)/shard_map/ppermute | solution.py:563
  183.5 2.2 fusion
  185.8 10.9 %shard_map.264 = (f32[490,768]{1,0:T(8,128)}, f32[8,768]{1,0:T(8,128)}) custom-call(s32[6]{0:T(128)} %pad_add_fusion.info_ref.me_ref, bf16[4,512,768]{2,1,0:T(8,128)(2,1)} %get-tuple-element.82.dq_ref, bf16[2,768,768]{2,1,0:T(8,128)(2,1)} %shard_map.256.am_ref, bf16[2,768,768]{2,1,0:T(8,128)(2,1)} %copy-done.2, f32[512,768]{1,0:T(8,128)} %get-tuple-element.61.x_ref, ...), custom_call_target="tpu_custom_call" | custom-call | flops 2415919104 | bytes 22026240 | tf_op jit(solution)/shard_map/pallas_call | solution.py:508
  201.6 2.4 add_convert_fusion.1
  206.4 8.5 %shard_map.265 = f32[490,768]{1,0:T(8,128)} custom-call(s32[6]{0:T(128)} %pad_add_fusion.info_ref.me_ref, bf16[4,512,768]{2,1,0:T(8,128)(2,1)} %get-tuple-element.86.act_ref, bf16[8,4,2,96,768]{4,3,2,1,0:T(8,128)(2,1)} %bitcast.108, f32[512,768]{1,0:T(8,128)} %get-tuple-element.65.y_ref, f32[1,768]{1,0:T(1,128)} %reshape.131.bias_ref), custom_call_target="tpu_custom_call" | custom-call | flops 2415919104 | bytes 28317696 | tf_op jit(solution)/shard_map/pallas_call | solution.py:508
  218.2 6.8 %collective-permute-done.18 = bf16[2,2,96,768]{3,2,1,0:T(8,128)(2,1)S(1)} collective-permute-done((bf16[2,2,96,768]{3,2,1,0:T(8,128)(2,1)}, bf16[2,2,96,768]{3,2,1,0:T(8,128)(2,1)S(1)}, u32[]{:S(2)}, u32[]{:S(2)}) %collective-permute-start.18) | collective-permute-done | bytes 589856 | tf_op jit(solution)/shard_map/ppermute | solution.py:563
  225.2 3.7 %collective-permute-done.17 = bf16[2,2,96,768]{3,2,1,0:T(8,128)(2,1)S(1)} collective-permute-done((bf16[2,2,96,768]{3,2,1,0:T(8,128)(2,1)}, bf16[2,2,96,768]{3,2,1,0:T(8,128)(2,1)S(1)}, u32[]{:S(2)}, u32[]{:S(2)}) %collective-permute-start.17) | collective-permute-done | bytes 589856 | tf_op jit(solution)/shard_map/ppermute | solution.py:563
  231.8 4.0 %collective-permute-start.28 = (bf16[192,768]{1,0:T(8,128)(2,1)S(1)}, bf16[192,768]{1,0:T(8,128)(2,1)S(1)}, u32[]{:S(2)}, u32[]{:S(2)}) collective-permute-start(bf16[192,768]{1,0:T(8,128)(2,1)S(1)} %fusion.9), channel_id=1, source_target_pairs={{0,16},{1,17},{2,18},{3,19},{4,20},{5,21},{6,22},{7,23},{8,24},{9,... | collective-permute-start | bytes 884744 | tf_op jit(solution)/shard_map/ppermute | solution.py:563
  235.8 2.9 %collective-permute-done.23 = bf16[2,96,768]{2,1,0:T(8,128)(2,1)S(1)} collective-permute-done((bf16[2,96,768]{2,1,0:T(8,128)(2,1)S(1)}, bf16[2,96,768]{2,1,0:T(8,128)(2,1)S(1)}, u32[]{:S(2)}, u32[]{:S(2)}) %collective-permute-start.23) | collective-permute-done | bytes 294944 | tf_op jit(solution)/shard_map/ppermute | solution.py:563
  244.7 3.5 %collective-permute-done.26 = f32[9,768]{1,0:T(8,128)S(1)} collective-permute-done((f32[9,768]{1,0:T(8,128)S(1)}, f32[9,768]{1,0:T(8,128)S(1)}, u32[]{:S(2)}, u32[]{:S(2)}) %collective-permute-start.26) | collective-permute-done | bytes 27680 | tf_op jit(solution)/shard_map/ppermute | solution.py:563
  249.0 6.2 %collective-permute-done.27 = bf16[2,96,768]{2,1,0:T(8,128)(2,1)S(1)} collective-permute-done((bf16[2,96,768]{2,1,0:T(8,128)(2,1)S(1)}, bf16[2,96,768]{2,1,0:T(8,128)(2,1)S(1)}, u32[]{:S(2)}, u32[]{:S(2)}) %collective-permute-start.27) | collective-permute-done | bytes 294944 | tf_op jit(solution)/shard_map/ppermute | solution.py:563
  255.3 2.7 collective-permute-start.31
  258.0 2.6 collective-permute-done.29
  261.5 5.8 %collective-permute-done.30 = f32[9,768]{1,0:T(8,128)S(1)} collective-permute-done((f32[9,768]{1,0:T(8,128)S(1)}, f32[9,768]{1,0:T(8,128)S(1)}, u32[]{:S(2)}, u32[]{:S(2)}) %collective-permute-start.30) | collective-permute-done | bytes 27680 | tf_op jit(solution)/shard_map/ppermute | solution.py:563
  (156 shorter events, 60.7 us)
Async XLA Ops:
  7.2 103.6 %all-gather.3.cloned.1.call-start = ((), (), s32[]{:S(2)}) async-start(), calls=%async_computation | async-start | bytes 9732096 | tf_op jit(solution)/shard_map/all_gather | solution.py:688
  11.1 11.3 %collective-permute-start = (bf16[96,768]{1,0:T(8,128)(2,1)}, bf16[96,768]{1,0:T(8,128)(2,1)S(1)}, u32[]{:S(2)}, u32[]{:S(2)}) collective-permute-start(bf16[96,768]{1,0:T(8,128)(2,1)} %get-tuple-element.59), channel_id=1, source_target_pairs={{0,16},{1,17},{2,18},{3,19},{4,20},{5,21},{6,22},{7,23},{8,24},{9,... | collective-permute-start | bytes 442376 | tf_op jit(solution)/shard_map/ppermute | solution.py:563
  23.4 14.3 %collective-permute-start.1 = (bf16[2,96,768]{2,1,0:T(8,128)(2,1)S(1)}, bf16[2,96,768]{2,1,0:T(8,128)(2,1)S(1)}, u32[]{:S(2)}, u32[]{:S(2)}) collective-permute-start(bf16[2,96,768]{2,1,0:T(8,128)(2,1)S(1)} %pad_maximum_fusion.refs_0_), channel_id=1, source_target_pairs={{0,8},{1,9},{2,10},{3,11},{4,12},{5,13},{6,14},{7,15},{8,0},{9,1},... | collective-permute-start | bytes 884744 | tf_op jit(solution)/shard_map/ppermute | solution.py:563
  29.7 11.3 %collective-permute-start.2 = (bf16[2,96,768]{2,1,0:T(8,128)(2,1)S(1)}, bf16[2,96,768]{2,1,0:T(8,128)(2,1)S(1)}, u32[]{:S(2)}, u32[]{:S(2)}) collective-permute-start(bf16[2,96,768]{2,1,0:T(8,128)(2,1)S(1)} %pad_maximum_fusion.refs_0_), channel_id=1, source_target_pairs={{0,4},{1,5},{2,6},{3,7},{4,0},{5,1},{6,2},{7,3},{8,12},{9,13},{10,... | collective-permute-start | bytes 884744 | tf_op jit(solution)/shard_map/ppermute | solution.py:563
  37.7 11.4 %collective-permute-start.5 = (bf16[2,96,768]{2,1,0:T(8,128)(2,1)S(1)}, bf16[2,96,768]{2,1,0:T(8,128)(2,1)S(1)}, u32[]{:S(2)}, u32[]{:S(2)}) collective-permute-start(bf16[2,96,768]{2,1,0:T(8,128)(2,1)S(1)} %collective-permute-done.1.refs_1_), channel_id=1, source_target_pairs={{0,2},{1,3},{2,0},{3,1},{4,6},{5,7},{6,4},{7,5},{8,10},{9,11},{10,... | collective-permute-start | bytes 884744 | tf_op jit(solution)/shard_map/ppermute | solution.py:563
  39.1 19.2 %collective-permute-start.4 = (bf16[2,96,768]{2,1,0:T(8,128)(2,1)S(1)}, bf16[2,96,768]{2,1,0:T(8,128)(2,1)S(1)}, u32[]{:S(2)}, u32[]{:S(2)}) collective-permute-start(bf16[2,96,768]{2,1,0:T(8,128)(2,1)S(1)} %pad_maximum_fusion.refs_0_), channel_id=1, source_target_pairs={{0,2},{1,3},{2,0},{3,1},{4,6},{5,7},{6,4},{7,5},{8,10},{9,11},{10,... | collective-permute-start | bytes 884744 | tf_op jit(solution)/shard_map/ppermute | solution.py:563
  39.8 22.9 %collective-permute-start.3 = (bf16[2,96,768]{2,1,0:T(8,128)(2,1)S(1)}, bf16[2,96,768]{2,1,0:T(8,128)(2,1)S(1)}, u32[]{:S(2)}, u32[]{:S(2)}) collective-permute-start(bf16[2,96,768]{2,1,0:T(8,128)(2,1)S(1)} %collective-permute-done.1.refs_1_), channel_id=1, source_target_pairs={{0,4},{1,5},{2,6},{3,7},{4,0},{5,1},{6,2},{7,3},{8,12},{9,13},{10,... | collective-permute-start | bytes 884744 | tf_op jit(solution)/shard_map/ppermute | solution.py:563
  41.0 21.6 %collective-permute-start.6 = (bf16[2,96,768]{2,1,0:T(8,128)(2,1)S(1)}, bf16[2,96,768]{2,1,0:T(8,128)(2,1)S(1)}, u32[]{:S(2)}, u32[]{:S(2)}) collective-permute-start(bf16[2,96,768]{2,1,0:T(8,128)(2,1)S(1)} %collective-permute-done.2.refs_2_), channel_id=1, source_target_pairs={{0,2},{1,3},{2,0},{3,1},{4,6},{5,7},{6,4},{7,5},{8,10},{9,11},{10,... | collective-permute-start | bytes 884744 | tf_op jit(solution)/shard_map/ppermute | solution.py:563
  49.2 13.5 %collective-permute-start.7 = (bf16[2,96,768]{2,1,0:T(8,128)(2,1)S(1)}, bf16[2,96,768]{2,1,0:T(8,128)(2,1)S(1)}, u32[]{:S(2)}, u32[]{:S(2)}) collective-permute-start(bf16[2,96,768]{2,1,0:T(8,128)(2,1)S(1)} %collective-permute-done.5.refs_5_), channel_id=1, source_target_pairs={{0,4},{1,5},{2,6},{3,7},{4,0},{5,1},{6,2},{7,3},{8,12},{9,13},{10,... | collective-permute-start | bytes 884744 | tf_op jit(solution)/shard_map/ppermute | solution.py:563
  68.1 4.8 %collective-permute-start.8 = (bf16[2,768,768]{2,1,0:T(8,128)(2,1)}, bf16[2,768,768]{2,1,0:T(8,128)(2,1)S(1)}, u32[]{:S(2)}, u32[]{:S(2)}) collective-permute-start(bf16[2,768,768]{2,1,0:T(8,128)(2,1)} %shard_map.256.am_ref), channel_id=1, source_target_pairs={{0,1},{1,0},{2,3},{3,2},{4,5},{5,4},{6,7},{7,6},{8,9},{9,8},{10,11... | collective-permute-start | bytes 7077896 | tf_op jit(solution)/shard_map/ppermute | solution.py:563
  83.3 13.2 %collective-permute-start.9 = (bf16[4,112,768]{2,1,0:T(8,128)(2,1)S(1)}, bf16[4,112,768]{2,1,0:T(8,128)(2,1)S(1)}, u32[]{:S(2)}, u32[]{:S(2)}) collective-permute-start(bf16[4,112,768]{2,1,0:T(8,128)(2,1)S(1)} %slice.176.half_ref), channel_id=1, source_target_pairs={{0,1},{1,0},{2,3},{3,2},{4,5},{5,4},{6,7},{7,6},{8,9},{9,8},{10,11... | collective-permute-start | bytes 2064392 | tf_op jit(solution)/shard_map/ppermute | solution.py:563
  83.5 3.7 %collective-permute-start.10 = (f32[768]{0:T(1024)S(1)}, f32[768]{0:T(1024)S(1)}, u32[]{:S(2)}, u32[]{:S(2)}) collective-permute-start(f32[768]{0:T(1024)S(1)} %copy-done.15), channel_id=1, source_target_pairs={{0,2},{1,3},{2,0},{3,1},{4,6},{5,7},{6,4},{7,5},{8,10},{9,11},{10,... | collective-permute-start | bytes 9224 | tf_op jit(solution)/shard_map/ppermute | solution.py:563
  137.3 9.7 %collective-permute-start.12 = (bf16[2,8,192,768]{3,2,1,0:T(8,128)(2,1)}, bf16[2,8,192,768]{3,2,1,0:T(8,128)(2,1)}, u32[]{:S(2)}, u32[]{:S(2)}) collective-permute-start(bf16[2,8,192,768]{3,2,1,0:T(8,128)(2,1)} %get-tuple-element.71), channel_id=1, source_target_pairs={{0,1},{1,0},{2,3},{3,2},{4,5},{5,4},{6,7},{7,6},{8,9},{9,8},{10,11... | collective-permute-start | bytes 14155784 | tf_op jit(solution)/shard_map/ppermute | solution.py:563
  146.9 18.8 %collective-permute-start.13 = (f32[4,112,512]{2,1,0:T(8,128)}, f32[4,112,512]{2,1,0:T(8,128)}, u32[]{:S(2)}, u32[]{:S(2)}) collective-permute-start(f32[4,112,512]{2,1,0:T(8,128)} %get-tuple-element.75), channel_id=1, source_target_pairs={{0,1},{1,0},{2,3},{3,2},{4,5},{5,4},{6,7},{7,6},{8,9},{9,8},{10,11... | collective-permute-start | bytes 2752520 | tf_op jit(solution)/shard_map/ppermute | solution.py:563
  152.0 28.6 %collective-permute-start.16 = (bf16[2,2,192,768]{3,2,1,0:T(8,128)(2,1)}, bf16[2,2,192,768]{3,2,1,0:T(8,128)(2,1)S(1)}, u32[]{:S(2)}, u32[]{:S(2)}) collective-permute-start(bf16[2,2,192,768]{3,2,1,0:T(8,128)(2,1)} %slice_bitcast_fusion), channel_id=1, source_target_pairs={{0,2},{1,3},{2,0},{3,1},{4,6},{5,7},{6,4},{7,5},{8,10},{9,11},{10,... | collective-permute-start | bytes 3538952 | tf_op jit(solution)/shard_map/ppermute | solution.py:563
  155.2 28.4 %collective-permute-start.15 = (bf16[2,2,192,768]{3,2,1,0:T(8,128)(2,1)}, bf16[2,2,192,768]{3,2,1,0:T(8,128)(2,1)}, u32[]{:S(2)}, u32[]{:S(2)}) collective-permute-start(bf16[2,2,192,768]{3,2,1,0:T(8,128)(2,1)} %slice_bitcast_fusion.2), channel_id=1, source_target_pairs={{0,4},{1,5},{2,6},{3,7},{4,0},{5,1},{6,2},{7,3},{8,12},{9,13},{10,... | collective-permute-start | bytes 3538952 | tf_op jit(solution)/shard_map/ppermute | solution.py:563
  176.2 25.4 %collective-permute-start.14 = (bf16[2,8,96,768]{3,2,1,0:T(8,128)(2,1)}, bf16[2,8,96,768]{3,2,1,0:T(8,128)(2,1)}, u32[]{:S(2)}, u32[]{:S(2)}) collective-permute-start(bf16[2,8,96,768]{3,2,1,0:T(8,128)(2,1)} %get-tuple-element.78), channel_id=1, source_target_pairs={{0,1},{1,0},{2,3},{3,2},{4,5},{5,4},{6,7},{7,6},{8,9},{9,8},{10,11... | collective-permute-start | bytes 7077896 | tf_op jit(solution)/shard_map/ppermute | solution.py:563
  197.7 18.9 %collective-permute-start.19 = (bf16[2,192,768]{2,1,0:T(8,128)(2,1)S(1)}, bf16[2,192,768]{2,1,0:T(8,128)(2,1)S(1)}, u32[]{:S(2)}, u32[]{:S(2)}) collective-permute-start(bf16[2,192,768]{2,1,0:T(8,128)(2,1)S(1)} %slice_bitcast_fusion.7), channel_id=1, source_target_pairs={{0,2},{1,3},{2,0},{3,1},{4,6},{5,7},{6,4},{7,5},{8,10},{9,11},{10,... | collective-permute-start | bytes 1769480 | tf_op jit(solution)/shard_map/ppermute | solution.py:563
  200.1 14.8 %collective-permute-start.20 = (bf16[2,192,768]{2,1,0:T(8,128)(2,1)}, bf16[2,192,768]{2,1,0:T(8,128)(2,1)S(1)}, u32[]{:S(2)}, u32[]{:S(2)}) collective-permute-start(bf16[2,192,768]{2,1,0:T(8,128)(2,1)} %slice_bitcast_fusion.5), channel_id=1, source_target_pairs={{0,4},{1,5},{2,6},{3,7},{4,0},{5,1},{6,2},{7,3},{8,12},{9,13},{10,... | collective-permute-start | bytes 1769480 | tf_op jit(solution)/shard_map/ppermute | solution.py:563
  204.9 20.1 %collective-permute-start.18 = (bf16[2,2,96,768]{3,2,1,0:T(8,128)(2,1)}, bf16[2,2,96,768]{3,2,1,0:T(8,128)(2,1)S(1)}, u32[]{:S(2)}, u32[]{:S(2)}) collective-permute-start(bf16[2,2,96,768]{3,2,1,0:T(8,128)(2,1)} %slice_bitcast_fusion.9), channel_id=1, source_target_pairs={{0,2},{1,3},{2,0},{3,1},{4,6},{5,7},{6,4},{7,5},{8,10},{9,11},{10,... | collective-permute-start | bytes 1769480 | tf_op jit(solution)/shard_map/ppermute | solution.py:563
  215.0 14.0 %collective-permute-start.17 = (bf16[2,2,96,768]{3,2,1,0:T(8,128)(2,1)}, bf16[2,2,96,768]{3,2,1,0:T(8,128)(2,1)S(1)}, u32[]{:S(2)}, u32[]{:S(2)}) collective-permute-start(bf16[2,2,96,768]{3,2,1,0:T(8,128)(2,1)} %slice_bitcast_fusion.11), channel_id=1, source_target_pairs={{0,4},{1,5},{2,6},{3,7},{4,0},{5,1},{6,2},{7,3},{8,12},{9,13},{10,... | collective-permute-start | bytes 1769480 | tf_op jit(solution)/shard_map/ppermute | solution.py:563
  216.6 15.0 %collective-permute-start.24 = (bf16[2,192,768]{2,1,0:T(8,128)(2,1)S(1)}, bf16[2,192,768]{2,1,0:T(8,128)(2,1)S(1)}, u32[]{:S(2)}, u32[]{:S(2)}) collective-permute-start(bf16[2,192,768]{2,1,0:T(8,128)(2,1)S(1)} %fusion.2), channel_id=1, source_target_pairs={{0,8},{1,9},{2,10},{3,11},{4,12},{5,13},{6,14},{7,15},{8,0},{9,1},... | collective-permute-start | bytes 1769480 | tf_op jit(solution)/shard_map/ppermute | solution.py:563
  229.1 2.5 collective-permute-start.21
  229.2 9.5 %collective-permute-start.23 = (bf16[2,96,768]{2,1,0:T(8,128)(2,1)S(1)}, bf16[2,96,768]{2,1,0:T(8,128)(2,1)S(1)}, u32[]{:S(2)}, u32[]{:S(2)}) collective-permute-start(bf16[2,96,768]{2,1,0:T(8,128)(2,1)S(1)} %slice_bitcast_fusion.15), channel_id=1, source_target_pairs={{0,4},{1,5},{2,6},{3,7},{4,0},{5,1},{6,2},{7,3},{8,12},{9,13},{10,... | collective-permute-start | bytes 884744 | tf_op jit(solution)/shard_map/ppermute | solution.py:563
  230.7 9.1 %collective-permute-start.22 = (bf16[2,96,768]{2,1,0:T(8,128)(2,1)S(1)}, bf16[2,96,768]{2,1,0:T(8,128)(2,1)S(1)}, u32[]{:S(2)}, u32[]{:S(2)}) collective-permute-start(bf16[2,96,768]{2,1,0:T(8,128)(2,1)S(1)} %slice_bitcast_fusion.17), channel_id=1, source_target_pairs={{0,2},{1,3},{2,0},{3,1},{4,6},{5,7},{6,4},{7,5},{8,10},{9,11},{10,... | collective-permute-start | bytes 884744 | tf_op jit(solution)/shard_map/ppermute | solution.py:563
  231.8 17.2 %collective-permute-start.28 = (bf16[192,768]{1,0:T(8,128)(2,1)S(1)}, bf16[192,768]{1,0:T(8,128)(2,1)S(1)}, u32[]{:S(2)}, u32[]{:S(2)}) collective-permute-start(bf16[192,768]{1,0:T(8,128)(2,1)S(1)} %fusion.9), channel_id=1, source_target_pairs={{0,16},{1,17},{2,18},{3,19},{4,20},{5,21},{6,22},{7,23},{8,24},{9,... | collective-permute-start | bytes 884744 | tf_op jit(solution)/shard_map/ppermute | solution.py:563
  239.9 4.2 %collective-permute-start.25 = (f32[9,768]{1,0:T(8,128)S(1)}, f32[9,768]{1,0:T(8,128)S(1)}, u32[]{:S(2)}, u32[]{:S(2)}) collective-permute-start(f32[9,768]{1,0:T(8,128)S(1)} %add.98), channel_id=1, source_target_pairs={{0,2},{1,3},{2,0},{3,1},{4,6},{5,7},{6,4},{7,5},{8,10},{9,11},{10,... | collective-permute-start | bytes 82952 | tf_op jit(solution)/shard_map/ppermute | solution.py:563
  240.8 14.3 %collective-permute-start.27 = (bf16[2,96,768]{2,1,0:T(8,128)(2,1)S(1)}, bf16[2,96,768]{2,1,0:T(8,128)(2,1)S(1)}, u32[]{:S(2)}, u32[]{:S(2)}) collective-permute-start(bf16[2,96,768]{2,1,0:T(8,128)(2,1)S(1)} %fusion.7), channel_id=1, source_target_pairs={{0,8},{1,9},{2,10},{3,11},{4,12},{5,13},{6,14},{7,15},{8,0},{9,1},... | collective-permute-start | bytes 884744 | tf_op jit(solution)/shard_map/ppermute | solution.py:563
  244.0 4.2 %collective-permute-start.26 = (f32[9,768]{1,0:T(8,128)S(1)}, f32[9,768]{1,0:T(8,128)S(1)}, u32[]{:S(2)}, u32[]{:S(2)}) collective-permute-start(f32[9,768]{1,0:T(8,128)S(1)} %add.102), channel_id=1, source_target_pairs={{0,4},{1,5},{2,6},{3,7},{4,0},{5,1},{6,2},{7,3},{8,12},{9,13},{10,... | collective-permute-start | bytes 82952 | tf_op jit(solution)/shard_map/ppermute | solution.py:563
  255.2 5.4 %collective-permute-start.29 = (f32[9,768]{1,0:T(8,128)S(1)}, f32[9,768]{1,0:T(8,128)S(1)}, u32[]{:S(2)}, u32[]{:S(2)}) collective-permute-start(f32[9,768]{1,0:T(8,128)S(1)} %add.103), channel_id=1, source_target_pairs={{0,8},{1,9},{2,10},{3,11},{4,12},{5,13},{6,14},{7,15},{8,0},{9,1},... | collective-permute-start | bytes 82952 | tf_op jit(solution)/shard_map/ppermute | solution.py:563
  255.3 12.7 %collective-permute-start.31 = (bf16[96,768]{1,0:T(8,128)(2,1)S(1)}, bf16[96,768]{1,0:T(8,128)(2,1)S(1)}, u32[]{:S(2)}, u32[]{:S(2)}) collective-permute-start(bf16[96,768]{1,0:T(8,128)(2,1)S(1)} %fusion.11), channel_id=1, source_target_pairs={{0,16},{1,17},{2,18},{3,19},{4,20},{5,21},{6,22},{7,23},{8,24},{9,... | collective-permute-start | bytes 442376 | tf_op jit(solution)/shard_map/ppermute | solution.py:563
  260.6 6.8 %collective-permute-start.30 = (f32[9,768]{1,0:T(8,128)S(1)}, f32[9,768]{1,0:T(8,128)S(1)}, u32[]{:S(2)}, u32[]{:S(2)}) collective-permute-start(f32[9,768]{1,0:T(8,128)S(1)} %add.106), channel_id=1, source_target_pairs={{0,16},{1,17},{2,18},{3,19},{4,20},{5,21},{6,22},{7,23},{8,24},{9,... | collective-permute-start | bytes 82952 | tf_op jit(solution)/shard_map/ppermute | solution.py:563
  (23 other events, 251.4 us)
Sparse Core Ops, SparseCore 0:
  11.5 95.7 all-gather.2

commit v2 on v1

v2 whole, which is shorter than its diff:
```python
import functools

import jax
import jax.numpy as jnp
from jax import lax
from jax.experimental import pallas as pl
from jax.experimental.pallas import tpu as pltpu
from jax.sharding import PartitionSpec as P

HEAD_DIM = 64
PATCHES = 196
EPS = 1e-06
D = 768
ROWS = 512
BLOCK = 208
FRAMES_AT = (0, 208)
HALF_AT = 400
HALF_ROWS = 112
HALF = PATCHES // 2
HALF_FIRST = 4
SCALE = HEAD_DIM ** (-0.5)
NEG = -1e30
VMEM = {"pack": 8, "prep": 24, "forward": 24, "mlp": 24, "back": 24, "late": 24, "merge": 16}
BF = jnp.bfloat16
F32 = jnp.float32


def nn(left, right):
    return jnp.dot(left, right, preferred_element_type=F32)


def nt(left, right):
    return lax.dot_general(left, right, (((1,), (1,)), ((), ())), preferred_element_type=F32)


def tn(left, right):
    return lax.dot_general(left, right, (((0,), (0,)), ((), ())), preferred_element_type=F32)


def lanes_below(shape, bound):
    return lax.broadcasted_iota(jnp.int32, shape, 1) < bound


def ln_stats(value):
    mean = jnp.mean(value, axis=1, keepdims=True)
    centred = value - mean
    rstd = lax.rsqrt(jnp.mean(centred * centred, axis=1, keepdims=True) + EPS)
    return centred * rstd, rstd


def ln_back(grad, normed, rstd, gain):
    scaled = grad * gain
    first = jnp.mean(scaled, axis=1, keepdims=True)
    second = jnp.mean(scaled * normed, axis=1, keepdims=True)
    return rstd * (scaled - first - normed * second)


def split(block):
    return (
        block[:, 0:128],
        block[:, 128:256],
        block[:, 256:384],
        block[:, 512:640],
        block[:, 640:768],
    )


def masked_pair(pair, low):
    zero = jnp.zeros_like(pair)
    return jnp.where(low, pair, zero), jnp.where(low, zero, pair)


def attend(queries, keys, valid):
    q01, qv2 = queries
    k01, v01, kv2, ko2 = keys
    low = lanes_below(q01.shape, 64)
    q0, q1 = masked_pair(q01, low)
    q2 = jnp.where(low, qv2, jnp.zeros_like(qv2))

    def probs(q, k):
        s = jnp.where(valid, nt(q, k) * SCALE, NEG)
        e = jnp.exp(s - jnp.max(s, axis=1, keepdims=True))
        return (e / jnp.sum(e, axis=1, keepdims=True)).astype(BF)

    o0 = nn(probs(q0, k01), v01)
    o1 = nn(probs(q1, k01), v01)
    o2 = nn(probs(q2, ko2), kv2)
    return jnp.concatenate(
        [jnp.where(low, o0, o1), jnp.where(low, 0.0, o2)], axis=1
    ).astype(BF)


def attend_back(queries, keys, dob, valid, own):
    q01, qv2 = queries
    k01, v01, kv2, ko2 = keys
    low = lanes_below(q01.shape, 64)
    d01, d2 = dob[:, 0:128], dob[:, 128:256]
    d2 = jnp.where(low, jnp.zeros_like(d2), d2)
    q0, q1 = masked_pair(q01, low)
    d0, d1 = masked_pair(d01, low)
    q2 = jnp.where(low, qv2, jnp.zeros_like(qv2))

    def one(q, k, d, v):
        st = jnp.where(valid, nt(k, q) * SCALE, NEG)
        e = jnp.exp(st - jnp.max(st, axis=0, keepdims=True))
        p = e / jnp.sum(e, axis=0, keepdims=True)
        dp = nt(v, d)
        ds = p * (dp - jnp.sum(p * dp, axis=0, keepdims=True))
        return p.astype(BF), ds.astype(BF)

    p0, s0 = one(q0, k01, d0, v01)
    p1, s1 = one(q1, k01, d1, v01)
    p2, s2 = one(q2, ko2, d2, kv2)
    low = low[:own]
    dq01 = jnp.where(low, tn(s0, k01)[:own], tn(s1, k01)[:own]) * SCALE
    dk01 = jnp.where(low, nn(s0[:own], q01), nn(s1[:own], q01)) * SCALE
    dv01 = jnp.where(low, nn(p0[:own], d01), nn(p1[:own], d01))
    dq2 = tn(s2, ko2)[:own] * SCALE
    dk2 = nn(s2[:own], qv2) * SCALE
    dv2 = nn(p2[:own], d2)
    rest = jnp.zeros_like(dq01)
    return jnp.concatenate(
        [dq01, dk01, dv01, rest, jnp.where(low, dq2, dv2), jnp.where(low, dk2, 0.0)], axis=1
    ).astype(BF)


def half_place(shape, axis):
    at = lax.broadcasted_iota(jnp.int32, shape, axis)
    at = jnp.where(at >= HALF_ROWS, at - HALF_ROWS, at)
    return (at >= HALF_FIRST) & (at < HALF_FIRST + HALF)


def pick(mine_ref, theirs_ref, into):
    n = pl.program_id(0)

    @pl.when(n < 2)
    def _():
        into[...] = mine_ref[0]

    @pl.when(n >= 2)
    def _():
        into[...] = theirs_ref[0]


def panel_copies(info_ref, sources, into, sem, start, p):
    if len(sources) == 1:
        return [pltpu.make_async_copy(sources[0].at[start + p], into.at[p], sem.at[p, 0])]
    copies = []
    for k in range(4):
        piece = sources[4 * p + k]
        rows = piece.shape[1]
        x, near = k // 2, k % 2
        for far in range(2):
            w = jnp.bitwise_xor(info_ref[WIDE], 2 * (2 * far + near) + x)
            at = pl.ds(pl.multiple_of(w * rows, rows), rows)
            copies.append(pltpu.make_async_copy(piece.at[far], into.at[p, at], sem.at[p, 2 * k + far]))
    return copies


def bring(info_ref, sources, into, sem, start, steps):
    n = pl.program_id(0)

    @pl.when(n == 0)
    def _():
        for p in range(steps):
            for c in panel_copies(info_ref, sources, into, sem, start, p):
                c.start()

    for p in range(steps):

        @pl.when(n == p)
        def _():
            for c in panel_copies(info_ref, sources, into, sem, start, p):
                c.wait()


def pack_kernel(wq_ref, wk_ref, wv_ref, wo_ref, attn_ref):
    size = wo_ref.shape[0]
    at = lax.broadcasted_iota(jnp.int32, (size, size), 0)
    eye = (at == lax.broadcasted_iota(jnp.int32, (size, size), 1)).astype(BF)
    wo = tn(wo_ref[...], eye).astype(BF)
    attn_ref[:, 0:128] = wq_ref[:, :128]
    attn_ref[:, 128:256] = wk_ref[:, :128]
    attn_ref[:, 256:384] = wv_ref[:, :128]
    attn_ref[:, 384:512] = wo[:, :128]
    attn_ref[:, 512:640] = jnp.concatenate([wq_ref[:, 128:], wv_ref[:, 128:]], axis=1)
    attn_ref[:, 640:768] = jnp.concatenate([wk_ref[:, 128:], wo[:, 128:]], axis=1)


def spread(into, value, odd):
    zero = jnp.zeros_like(value)
    into[PATCHES:BLOCK] = zero[: BLOCK - PATCHES]
    end = HALF_AT + HALF_FIRST + HALF
    into[end:] = zero[: ROWS - end]

    @pl.when(odd == 0)
    def _():
        into[:PATCHES] = value[:PATCHES]
        into[BLOCK:end] = value[PATCHES:]

    @pl.when(odd == 1)
    def _():
        into[:PATCHES] = value[HALF : HALF + PATCHES]
        into[BLOCK : BLOCK + PATCHES] = value[HALF + PATCHES :]
        into[BLOCK + PATCHES : end] = value[:HALF]


def gather_back(into, value, odd):
    end = HALF_AT + HALF_FIRST + HALF

    @pl.when(odd == 0)
    def _():
        into[:PATCHES] = value[:PATCHES]
        into[PATCHES:] = value[BLOCK:end]

    @pl.when(odd == 1)
    def _():
        into[:HALF] = value[BLOCK + PATCHES : end]
        into[HALF : HALF + PATCHES] = value[:PATCHES]
        into[HALF + PATCHES :] = value[BLOCK : BLOCK + PATCHES]


def prep_kernel(info_ref, x_ref, c_ref, xo_ref, vec_ref, xp_ref, cp_ref, cb_ref, h_ref, other):
    odd = info_ref[ODD]
    gain, shift = vec_ref[0:1, :], vec_ref[1:2, :]
    spread(xp_ref, x_ref[...].astype(F32), odd)
    spread(cp_ref, c_ref[...], odd)
    cb_ref[...] = cp_ref[...].astype(BF)
    normed, _ = ln_stats(xp_ref[...])
    h_ref[:ROWS] = (normed * gain + shift).astype(BF)
    other[...] = jnp.zeros_like(other)
    other[HALF_FIRST : HALF_FIRST + HALF] = xo_ref[...].astype(F32)
    normed, _ = ln_stats(other[...])
    h_ref[ROWS:] = (normed * gain + shift).astype(BF)


def forward_kernel(pieces, info_ref, h_ref, x_ref, vec_ref, *refs):
    sources, refs = refs[:pieces], refs[pieces:]
    qkv_ref, o_ref, a_ref, y_ref, h2_ref, w, sem = refs
    n = pl.program_id(0)
    bring(info_ref, sources, w, sem, 0, PANELS)
    a_ref[0] = w[n]
    qkv_ref[0] = nn(h_ref[...], w[n]).astype(BF)
    valid = lanes_below((BLOCK, BLOCK), PATCHES)
    for at in FRAMES_AT:
        q01, k01, v01, qv2, ko2 = split(qkv_ref[0, at : at + BLOCK, :])
        o_ref[0, at : at + BLOCK, :] = attend((q01, qv2), (k01, v01, qv2, ko2), valid)
    q01, k01, v01, qv2, ko2 = split(qkv_ref[0, HALF_AT:, :])
    valid = half_place((HALF_ROWS, 2 * HALF_ROWS), 1)
    part = attend((q01[:HALF_ROWS], qv2[:HALF_ROWS]), (k01, v01, qv2, ko2), valid)
    first = lax.broadcasted_iota(jnp.int32, (16, 256), 0) < HALF_FIRST
    o_ref[0, HALF_AT : HALF_AT + 16] = jnp.where(first, o_ref[0, HALF_AT : HALF_AT + 16], part[:16])
    o_ref[0, HALF_AT + 16 :] = part[16:]
    o = o_ref[0]
    z = nt(o[:, :128], a_ref[0, :, 384:512]) + nt(o[:, 128:], a_ref[0, :, 640:768])

    @pl.when(n == 0)
    def _():
        y_ref[...] = x_ref[...] + z

    @pl.when(n > 0)
    def _():
        y_ref[...] += z

    @pl.when(n == PANELS - 1)
    def _():
        normed, _ = ln_stats(y_ref[...])
        h2_ref[...] = (normed * vec_ref[2:3, :] + vec_ref[3:4, :]).astype(BF)


def store_blocks(out_ref, value, me, part=0):
    blocks = out_ref.shape[1]
    rows = value.shape[0] // blocks
    value = value.astype(BF)
    for w in range(blocks):
        if blocks == 1:
            place = 0
        else:
            r = jnp.bitwise_xor(w, me)
            place = (r & 2) * 2 + (r & 1) * 2 + lax.shift_right_logical(r, 2)
        out_ref[0, place, part * rows : (part + 1) * rows] = value[w * rows : (w + 1) * rows]


def mlp_kernel(last, info_ref, h_ref, cb_ref, b_ref, u_ref, d_ref, *refs):
    if last:
        base_ref, c_ref, y_ref, vec_ref, act_ref, dm_ref, db_ref, dy_ref, dz_ref, sums_ref, *refs = refs
        ht, ct, dub, acc = refs
    else:
        act_ref, dm_ref, db_ref, acc, ht, ct, dub = refs
    n = pl.program_id(0)

    @pl.when(n == 0)
    def _():
        ht[...] = h_ref[...].T
        ct[...] = cb_ref[...].T

    for j in range(3):
        cols = slice(256 * j, 256 * j + 256)
        up = u_ref[:, 0, 0, :, cols].reshape(D, 256)
        down = d_ref[:, 0, 0, :, cols].reshape(D, 256)
        u = nn(h_ref[...], up) + b_ref[0, :, cols]
        big = 0.5 * (1.0 + lax.erf(u * (0.5**0.5)))
        small = jnp.exp(-0.5 * u * u) * 0.3989422804014327
        act_ref[0, :, cols] = (u * big).astype(BF)
        du = nn(cb_ref[...], down) * (big + u * small)
        db_ref[0, :, cols] = jnp.sum(du, axis=0, keepdims=True)
        dub[:, cols] = du.astype(BF)
    dh = nt(dub[...], u_ref[...].reshape(D, D))
    store_blocks(dm_ref, nn(ht[...], dub[...]), info_ref[WIDE], 0)
    store_blocks(dm_ref, nn(ct[...], act_ref[0]), info_ref[WIDE], 1)

    @pl.when(n == 0)
    def _():
        acc[...] = base_ref[...] + dh if last else dh

    @pl.when(n == 1)
    def _():
        acc[...] += dh
        if last:
            normed, rstd = ln_stats(y_ref[...])
            grad = acc[...]
            c = c_ref[...]
            dy = c + ln_back(grad, normed, rstd, vec_ref[2:3, :])
            dy_ref[...] = dy
            dz_ref[...] = dy.astype(BF)
            sums_ref[0:1, :] = jnp.sum(grad * normed, axis=0, keepdims=True)
            sums_ref[1:2, :] = jnp.sum(grad, axis=0, keepdims=True)
            sums_ref[2:3, :] = jnp.sum(c, axis=0, keepdims=True)


def back_kernel(info_ref, dz_ref, dzo_ref, h_ref, qkv_ref, o_ref, a_ref, dam_ref, dat0_ref, dat1_ref, dq_ref, ht, dt, dob):
    n = pl.program_id(0)

    @pl.when(n == 0)
    def _():
        ht[...] = h_ref[:ROWS].T
        dt[...] = dz_ref[...].T

    for into, cols in ((0, 384), (128, 640)):
        weight = a_ref[0, :, cols : cols + 128]
        dob[:ROWS, into : into + 128] = nn(dz_ref[...], weight).astype(BF)
        dob[ROWS:, into : into + 128] = nn(dzo_ref[...], weight).astype(BF)
    valid = lax.broadcasted_iota(jnp.int32, (BLOCK, BLOCK), 0) < PATCHES
    for at in FRAMES_AT:
        q01, k01, v01, qv2, ko2 = split(qkv_ref[0, at : at + BLOCK, :])
        d = dob[at : at + BLOCK]
        inside = lax.broadcasted_iota(jnp.int32, d.shape, 0) < PATCHES
        d = jnp.where(inside, d, jnp.zeros_like(d))
        dq_ref[0, at : at + BLOCK] = attend_back(
            (q01, qv2), (k01, v01, qv2, ko2), d, valid, BLOCK
        )
    q01, k01, v01, qv2, ko2 = split(qkv_ref[0, HALF_AT:, :])
    d = dob[HALF_AT:]
    d = jnp.where(half_place(d.shape, 0), d, jnp.zeros_like(d))
    valid = half_place((2 * HALF_ROWS, 2 * HALF_ROWS), 0)
    part = attend_back((q01, qv2), (k01, v01, qv2, ko2), d, valid, HALF_ROWS)
    first = lax.broadcasted_iota(jnp.int32, (16, D), 0) < HALF_FIRST
    dq_ref[0, HALF_AT : HALF_AT + 16] = jnp.where(first, dq_ref[0, HALF_AT : HALF_AT + 16], part[:16])
    dq_ref[0, HALF_AT + 16 :] = part[16:]
    left = nn(ht[...], dq_ref[0, :, 0:384])
    right = nn(ht[...], dq_ref[0, :, 512:768])
    outs = nn(dt[...], o_ref[0])
    value = jnp.concatenate(
        [left, outs[:, 0:128], right[:, 0:128], right[:, 128:256] + outs[:, 128:256]], axis=1
    )

    @pl.when(n < 2)
    def _():
        store_blocks(dam_ref, value, info_ref[WIDE])

    @pl.when(n == 2)
    def _():
        store_blocks(dat0_ref, value, info_ref[WIDE])

    @pl.when(n == 3)
    def _():
        store_blocks(dat1_ref, value, info_ref[WIDE])


def late_kernel(
    info_ref,
    dq_ref,
    a_ref,
    actm_ref,
    actt_ref,
    d_ref,
    x_ref,
    y_ref,
    dy_ref,
    vec_ref,
    sums_ref,
    dbm_ref,
    dbt_ref,
    out_ref,
    grad_ref,
    small_ref,
    acc,
    acc2,
    left,
):
    n = pl.program_id(0)
    dh = nt(dq_ref[0], a_ref[0])

    @pl.when(n == 0)
    def _():
        acc[...] = dh

    @pl.when(n > 0)
    def _():
        acc[...] += dh

    pick(actm_ref, actt_ref, left)
    y2 = nt(left[...], d_ref[...].reshape(D, D))

    @pl.when(n == 0)
    def _():
        acc2[...] = y_ref[...] + y2 + vec_ref[4:5, :]

    @pl.when(n > 0)
    def _():
        acc2[...] += y2

    @pl.when(n == pl.num_programs(0) - 1)
    def _():
        normed, rstd = ln_stats(x_ref[...])
        grad = acc[...]
        small_ref[0:1, :] = jnp.sum(grad * normed, axis=0, keepdims=True)
        small_ref[1:2, :] = jnp.sum(grad, axis=0, keepdims=True)
        small_ref[2:5, :] = sums_ref[0:3, :]
        for j in range(PANELS):
            at = info_ref[BACK + j]

            @pl.when(at < 2)
            def _():
                small_ref[5 + j : 6 + j, :] = dbm_ref[at]

            @pl.when(at >= 2)
            def _():
                small_ref[5 + j : 6 + j, :] = dbt_ref[at - 2]

        gather_back(grad_ref, dy_ref[...] + ln_back(grad, normed, rstd, vec_ref[0:1, :]), info_ref[ODD])
        gather_back(out_ref, acc2[...], info_ref[ODD])


WIDE, ODD, BACK, ORDER = 0, 1, 2, 6
PANELS = 4


def spec(shape, kind, start):
    tail = (0,) * (len(shape) - 1)
    block = (1,) + tuple(shape[1:])
    if kind == "any":
        return pl.BlockSpec(memory_space=pl.ANY)
    if kind == "fixed":
        return pl.BlockSpec(shape, lambda n, info: (0,) + tail)
    if kind == "panel":
        return pl.BlockSpec(block, lambda n, info: (n + start,) + tail)
    if kind == "local":
        return pl.BlockSpec(block, lambda n, info: (n,) + tail)
    if kind in ("up", "down"):
        which = int(kind == "down")
        block = (shape[0], 1, 1) + tuple(shape[3:])
        return pl.BlockSpec(block, lambda n, info: (0, info[ORDER + n + start], which, 0, 0))
    if kind == "mine":
        return pl.BlockSpec(block, lambda n, info: (jnp.minimum(n, 1),) + tail)
    return pl.BlockSpec(block, lambda n, info: (jnp.maximum(n - 2, 0),) + tail)


def call(kernel, info, ins, outs, scratch=(), units=0, steps=PANELS, start=0, vmem="back"):
    moved = sum(a.size * a.dtype.itemsize for a, _ in ins)
    return pl.pallas_call(
        kernel,
        grid_spec=pltpu.PrefetchScalarGridSpec(
            num_scalar_prefetch=1,
            grid=(steps,),
            in_specs=[spec(a.shape, k, start) for a, k in ins],
            out_specs=[spec(s, k, start) for s, _, k in outs],
            scratch_shapes=list(scratch),
        ),
        out_shape=[jax.ShapeDtypeStruct(s, d) for s, d, _ in outs],
        compiler_params=pltpu.CompilerParams(vmem_limit_bytes=VMEM[vmem] << 20),
        cost_estimate=pl.CostEstimate(
            flops=int(2 * ROWS * D * D * units * steps), bytes_accessed=int(moved * 2), transcendentals=0
        ),
    )(info, *[a for a, _ in ins])


CORE, LINE_Y, LINE_X, NEAR_Z, FAR_Z = 1, 2, 4, 8, 16


def make_swap(devices):
    def swap(value, bit):
        return lax.ppermute(value, ("wide", "narrow"), [(i, i ^ bit) for i in range(devices)])

    return swap


def after(value, *others):
    return lax.optimization_barrier((value,) + others)[0] if others else value


class Gather:
    def __init__(self, swap, own):
        self.swap, self.own = swap, own

    def far(self, *wait):
        own = after(self.own, *wait)
        self.b0 = jnp.stack([own, self.swap(own, FAR_Z)])

    def near(self, *wait):
        self.b1 = self.swap(after(self.b0, *wait), NEAR_Z)

    def planes0(self, *wait):
        b0 = after(self.b0, *wait)
        self.x0, self.y0 = self.swap(b0, LINE_X), self.swap(b0, LINE_Y)

    def planes1(self, *wait):
        b1 = after(self.b1, *wait)
        self.x1, self.y1 = self.swap(b1, LINE_X), self.swap(b1, LINE_Y)

    def corners(self, *wait):
        x0, y1 = after(self.x0, *wait), after(self.y1, *wait)
        self.d0, self.d1 = self.swap(x0, LINE_Y), self.swap(y1, LINE_X)

    def mine(self):
        return [self.b0, self.b1, self.x0, self.x1, self.y0, self.y1, self.d0, self.d1]

    def theirs(self):
        return [self.swap(v, CORE) for v in self.mine()]


def merge_kernel(own_ref, *refs):
    got_refs, (keep_a, send_a, keep_b, send_b) = refs[:-4], refs[-4:]
    y, k = pl.program_id(0), pl.program_id(1)
    got = got_refs[0][...]
    if len(got_refs) == 2:
        got = jnp.where(y == 0, got, got_refs[1][...])
    value = (own_ref[...].astype(F32) + got.astype(F32)).astype(BF)

    @pl.when(k == 0)
    def _():
        keep_a[...] = value

    @pl.when(k == 1)
    def _():
        send_a[...] = value

    @pl.when((k >= 2) & (y == 0))
    def _():
        keep_b[...] = value

    @pl.when((k >= 2) & (y == 1))
    def _():
        send_b[...] = value


def merge(own, *got):
    rows = own.shape[2]
    block = (1, 2, rows, D)
    taken = pl.BlockSpec(block, lambda y, k: (y, k, 0, 0))
    by_y = pl.BlockSpec(block, lambda y, k: (y, 0, 0, 0))
    first = pl.BlockSpec(block, lambda y, k: (jnp.where(y == 0, jnp.maximum(k - 2, 0), 1), 0, 0, 0))
    second = pl.BlockSpec(block, lambda y, k: (jnp.where(y == 0, 0, jnp.maximum(k - 2, 0)), 0, 0, 0))
    size = own.size * 2
    gots = [taken]
    if len(got) == 2:
        gots = [
            pl.BlockSpec(block, lambda y, k: (0, jnp.where(y == 0, k, 3), 0, 0)),
            pl.BlockSpec(block, lambda y, k: (0, jnp.where(y == 0, 0, k), 0, 0)),
        ]
    return pl.pallas_call(
        merge_kernel,
        grid=(2, 4),
        in_specs=[taken] + gots,
        out_specs=[by_y, by_y, first, second],
        out_shape=[jax.ShapeDtypeStruct((2, 2, rows, D), BF)] * 4,
        compiler_params=pltpu.CompilerParams(vmem_limit_bytes=VMEM["merge"] << 20),
        cost_estimate=pl.CostEstimate(flops=0, bytes_accessed=3 * size, transcendentals=0),
    )(own, *got)


def total(*parts):
    value = parts[0].astype(F32)
    for p in parts[1:]:
        value = value + p.astype(F32)
    return value


class Scatter:
    def __init__(self, swap, *other):
        self.swap, self.state = swap, 0
        self.flight = tuple(swap(v, CORE) for v in other)

    def step(self, *wait, own=None):
        swap = self.swap
        got = tuple(after(f, *wait) for f in self.flight)
        self.state += 1
        if self.state == 1:
            self.a, send_a, self.b, send_b = merge(own, *got)
            self.flight = swap(send_a, LINE_X), swap(send_b, LINE_Y)
            return (send_a, send_b)
        if self.state == 2:
            send_a = total(self.a[1], got[0][1]).astype(BF)
            send_b = total(self.b[1], got[1][1]).astype(BF)
            self.a, self.b = (self.a[0], got[0][0]), (self.b[0], got[1][0])
            self.flight = swap(send_a, LINE_Y), swap(send_b, LINE_X)
            return (send_a, send_b)
        if self.state == 3:
            self.a = self.a + (got[0],)
            send = total(*self.b, got[1]).astype(BF)
            self.flight = (swap(send, NEAR_Z),)
            return (send,)
        if self.state == 4:
            self.a = self.a + (got[0],)
            send = total(*(p[1] for p in self.a)).astype(BF)
            self.flight = (swap(send, FAR_Z),)
            return (send,)
        self.result = total(*(p[0] for p in self.a), got[0])
        return (self.result,)


def body(
    tokens_in,
    cotangent,
    norm1_gain,
    norm1_shift,
    w_query,
    w_key,
    w_value,
    w_out,
    norm2_gain,
    norm2_shift,
    w_up,
    up_bias,
    w_down,
    down_bias,
    *,
    wide,
    narrow,
):
    direct = wide == 8 and narrow == 4
    wi, ni = lax.axis_index("wide"), lax.axis_index("narrow")
    swap = make_swap(wide * narrow)
    flipped = jnp.array([0, 2, 1, 3], jnp.int32)
    places = jnp.arange(PANELS, dtype=jnp.int32)
    back = flipped[jnp.bitwise_xor(ni, places)] if direct else places
    order = jnp.bitwise_xor(ni, flipped) if direct else places
    me = wi if direct else jnp.zeros_like(wi)
    info = jnp.concatenate(
        [v.astype(jnp.int32) for v in (me.reshape(1), (ni % 2).reshape(1), back, order)]
    )
    count, rows = tokens_in.shape[0], w_up.shape[0]
    vecs = jnp.stack([norm1_gain, norm1_shift, norm2_gain, norm2_shift, down_bias] + [down_bias] * 3)
    wide_row, turned = pltpu.VMEM((ROWS, D), F32), pltpu.VMEM((D, ROWS), BF)
    tokens32, tokens16 = ((ROWS, D), F32, "fixed"), ((ROWS, D), BF, "fixed")
    result32 = ((count, D), F32, "fixed")
    sums = ((8, D), F32, "fixed")
    blocks = 8 if direct else 1
    grads_a, grads_m = (2, blocks, D // blocks, D), (2, blocks, 2 * D // blocks, D)

    mlp = jnp.concatenate([w_up, w_down.T])
    if direct:
        full = lax.all_gather(mlp, ("wide", "narrow"), axis=0, tiled=False)
        full = full.reshape(wide, narrow, 2, rows, D)
    (attn,) = pl.pallas_call(
        pack_kernel,
        out_shape=[jax.ShapeDtypeStruct((rows, D), BF)],
        compiler_params=pltpu.CompilerParams(vmem_limit_bytes=VMEM["pack"] << 20),
    )(w_query, w_key, w_value, w_out)
    shared = jnp.where(ni % 2 == 1, tokens_in[:HALF], tokens_in[count - HALF :])
    shared = swap(shared, CORE)
    x, c, cb, h1 = call(
        prep_kernel,
        info,
        [(tokens_in, "fixed"), (cotangent, "fixed"), (shared, "fixed"), (vecs, "fixed")],
        [tokens32, tokens32, tokens16, ((ROWS + HALF_ROWS, D), BF, "fixed")],
        [pltpu.VMEM((HALF_ROWS, D), F32)],
        steps=1,
        vmem="prep",
    )
    if direct:
        ga = Gather(swap, attn)
        ga.far()
        ga.near()
        ga.planes0()
        ga.planes1(h1)
        ga.corners()
        sources = ga.mine() + ga.theirs()
        b_y, b_c = swap(after(up_bias, ga.d0, ga.d1), LINE_Y), swap(up_bias, CORE)
    else:

        def whole(v):
            return lax.all_gather(v, "narrow", axis=0, tiled=False)

        sources = [whole(lax.all_gather(attn, "wide", axis=0, tiled=True))]
        full = lax.all_gather(mlp.reshape(2, rows, D), "wide", axis=1, tiled=True)
        full = whole(full)[None]
        biases = whole(up_bias)
    qkv, o, a, y, h2 = call(
        functools.partial(forward_kernel, len(sources)),
        info,
        [(h1, "fixed"), (x, "fixed"), (vecs, "fixed")] + [(v, "any") for v in sources],
        [((PANELS, ROWS + HALF_ROWS, D), BF, "panel"), ((PANELS, ROWS, 256), BF, "panel")]
        + [((PANELS, D, D), BF, "panel"), tokens32, tokens16],
        [pltpu.VMEM((PANELS, D, D), BF), pltpu.SemaphoreType.DMA((PANELS, 8))],
        units=2,
        vmem="forward",
    )

    if direct:
        b_y = after(b_y, h2)
        biases = jnp.stack([up_bias, b_y, b_c, swap(b_y, CORE)])
    biases = biases.reshape(PANELS, 1, D)

    def mlp_part(start, more_in, more_out, more_scratch):
        return call(
            functools.partial(mlp_kernel, not start),
            info,
            [(h2, "fixed"), (cb, "fixed"), (biases, "panel"), (full, "up"), (full, "down")] + more_in,
            [((2, ROWS, D), BF, "local"), (grads_m, BF, "local"), ((2, 1, D), F32, "local")] + more_out,
            [turned, turned, pltpu.VMEM((ROWS, D), BF)] + more_scratch,
            units=5,
            steps=2,
            start=start,
            vmem="mlp",
        )

    act_t, dm_t, db_t, acc = mlp_part(2, [], [tokens32], [])
    if direct:
        sm = Scatter(swap, dm_t)
    act_m, dm_m, db_m, dy, dz, sums2 = mlp_part(
        0,
        [(acc, "fixed"), (c, "fixed"), (y, "fixed"), (vecs, "fixed")],
        [tokens32, tokens16, sums],
        [wide_row],
    )
    dzo = swap(dz[HALF_AT:], CORE)
    if direct:
        dz = after(dz, *sm.step(dz, own=dm_m))

    grads_one = ((1,) + grads_a[1:], BF, "fixed")
    da_m, *da_t, dq = call(
        back_kernel,
        info,
        [(dz, "fixed"), (dzo, "fixed"), (h1, "fixed"), (qkv, "panel"), (o, "panel"), (a, "panel")],
        [(grads_a, BF, "mine"), grads_one, grads_one, ((PANELS, ROWS, D), BF, "panel")],
        [turned, turned, pltpu.VMEM((ROWS + HALF_ROWS, 256), BF)],
        units=4,
    )
    if direct:
        sa = Scatter(swap, *da_t)
        sent = sm.step(dq)
        dq = after(dq, *sent, *sa.step(*sent, own=da_m))
    out, grad_x, small = call(
        late_kernel,
        info,
        [(dq, "panel"), (a, "panel"), (act_m, "mine"), (act_t, "theirs")]
        + [(full, "down"), (x, "fixed"), (y, "fixed"), (dy, "fixed")]
        + [(vecs, "fixed"), (sums2, "fixed"), (db_m, "fixed"), (db_t, "fixed")],
        [result32, result32, ((16, D), F32, "fixed")],
        [wide_row, wide_row, pltpu.VMEM((ROWS, D), BF)],
        units=2,
        vmem="late",
    )
    if direct:

        def reduced(small, bit, *wait):
            small = after(small, *wait)
            return small + swap(small, bit)

        wait = sa.step(small)
        small = reduced(reduced(small, CORE, *wait), FAR_Z)
        wait = sm.step(small)
        small = reduced(small, LINE_X, *sa.step(small, *wait))
        wait = sm.step(small)
        small = reduced(reduced(small, LINE_Y, *sa.step(small, *wait)), NEAR_Z)
        sm.step(), sa.step()
        grad_a, grad_u, grad_d = sa.result, sm.result[:rows], sm.result[rows:]
    else:

        def shard(own, other):
            v = jnp.concatenate([own, other]).reshape(PANELS, -1, D, D).astype(F32)
            v = lax.psum_scatter(v, "narrow", scatter_dimension=0, tiled=False)
            return lax.psum_scatter(v, "wide", scatter_dimension=1, tiled=True)

        (grad_a,), (grad_u, grad_d) = shard(da_m, jnp.concatenate(da_t)), shard(dm_m, dm_t)
        small = lax.psum(small, ("wide", "narrow"))
    pick_lanes = lambda low, high: jnp.concatenate(
        [grad_a[:, low : low + 128], grad_a[:, high : high + 64]], axis=1
    )
    return (
        out,
        grad_x,
        small[0],
        small[1],
        pick_lanes(0, 512),
        pick_lanes(128, 640),
        pick_lanes(256, 576),
        pick_lanes(384, 704).T,
        small[2],
        small[3],
        grad_u,
        lax.dynamic_index_in_dim(small, 5 + ni, 0, keepdims=False),
        grad_d.T,
        small[4],
    )


def solution(mesh):
    rows, cols, copied = P("wide", "narrow"), P("narrow", "wide"), P()
    tokens = P(("wide", "narrow"), None)
    return jax.shard_map(
        functools.partial(body, wide=mesh.shape["wide"], narrow=mesh.shape["narrow"]),
        mesh=mesh,
        in_specs=(tokens, tokens, copied, copied, rows, rows, rows, cols)
        + (copied, copied, rows, P("narrow"), cols, copied),
        out_specs=(tokens, tokens, copied, copied, rows, rows, rows, cols)
        + (copied, copied, rows, P("narrow"), cols, copied),
        check_vma=False,
    )
```

time: 279 us -> 253 us (0.907)
  Pallas kernels: 114 us -> 79.3 us
  waiting for transfers between devices: 74.8 us -> 84.7 us
  local copies, waits for them, and re-layouts: 23.9 us -> 30.3 us
  other arithmetic: 13 us -> 7.65 us
    pallas_call x10 -> x6, Pallas kernels: 108 us -> 75.1 us  [call(): pl.pallas_call(kernel, grid_spec=pltpu.PrefetchScalarGridSpec(num_scalar_...]
    unnamed x47 -> x91, local copies, waits for them, and re-layouts: 6.96 us -> 27.9 us
    all_gather x1, waiting for transfers between devices: 0.02 us -> 13.3 us  [body(): full = lax.all_gather(mlp, ('wide', 'narrow'), axis=0, tiled=False)]
    convert_element_type x9 -> x8, other arithmetic: 9.16 us -> 1.01 us  [the longest x2 0.34 us: step(): send = total(*self.b, got[1]).astype(BF)]
    squeeze x10 -> x0, local copies, waits for them, and re-layouts: 5.21 us -> none  [the longest x4 4.05 us: step(): self.flight = (swap(sa[:, 1], LINE_X), swap(sb[1], LINE_Y))]
    reshape x6 -> x1, local copies, waits for them, and re-layouts: 4.88 us -> 0.01 us  [body(): biases = biases.reshape(PANELS, 1, D)]
    slice x3 -> x1, local copies, waits for them, and re-layouts: 3.38 us -> 0.01 us  [body(): dzo = swap(dz[HALF_AT:], CORE)]
    ppermute x32 -> x41, waiting for transfers between devices: 74.8 us -> 71.4 us  [swap(): lax.ppermute(value, ('wide', 'narrow'), [(i, i ^ bit) for i in range(devi...]
  transfers between devices with their start and end apart: 33 -> 42, of which waited for: 19 -> 22; matrix products, arithmetic and copies ran while one was open for 10% -> 3% of each run, Pallas kernels for 31% -> 27%
where the time goes in v2:
time: 253 us
  waiting for transfers between devices  84.7 us (33%)
  Pallas kernels  79.3 us (31%)
  starting transfers between devices  36.4 us (14%)
  local copies, waits for them, and re-layouts  30.3 us (12%)
  between operations  14.5 us (6%)
  other arithmetic  7.65 us (3%)
    pallas_call x6, Pallas kernels, call(): pl.pallas_call(kernel, grid_spec=pltpu.PrefetchScalarGridSpec(num_scalar_...  75.1 us
    ppermute x41, waiting for transfers between devices, swap(): lax.ppermute(value, ('wide', 'narrow'), [(i, i ^ bit) for i in range(devi...  71.4 us
    ppermute x41, starting transfers between devices, swap(): lax.ppermute(value, ('wide', 'narrow'), [(i, i ^ bit) for i in range(devi...  36.4 us
    unnamed x91, local copies, waits for them, and re-layouts  27.9 us
    all_gather x1, waiting for transfers between devices, body(): full = lax.all_gather(mlp, ('wide', 'narrow'), axis=0, tiled=False)  13.3 us
  transfers between devices with their start and end apart: 42, of which 22 were waited for; matrix products, arithmetic and copies ran while one was open for 3% of the time, Pallas kernels for 27%

profile of v2, /device:TPU:0, one launch (start us, length us, event | category | flops | bytes accessed | tf_op | source)
XLA Modules:
  0.0 252.9 jit_solution(14527023113220928261)
XLA Ops:
  7.3 1.7 pad_maximum_fusion.1
  11.0 3.7 %collective-permute-start.1 = (bf16[96,768]{1,0:T(8,128)(2,1)S(1)}, bf16[96,768]{1,0:T(8,128)(2,1)S(1)}, u32[]{:S(2)}, u32[]{:S(2)}) collective-permute-start(bf16[96,768]{1,0:T(8,128)(2,1)S(1)} %shard_map.255), channel_id=1, source_target_pairs={{0,16},{1,17},{2,18},{3,19},{4,20},{5,21},{6,22},{7,23},{8,24},{9,... | collective-permute-start | bytes 442376 | tf_op jit(solution)/shard_map/ppermute | solution.py:493
  14.7 7.6 %collective-permute-done.1 = bf16[96,768]{1,0:T(8,128)(2,1)S(1)} collective-permute-done((bf16[96,768]{1,0:T(8,128)(2,1)S(1)}, bf16[96,768]{1,0:T(8,128)(2,1)S(1)}, u32[]{:S(2)}, u32[]{:S(2)}) %collective-permute-start.1) | collective-permute-done | bytes 147488 | tf_op jit(solution)/shard_map/ppermute | solution.py:493
  28.5 1.6 shard_map.254
  32.2 4.3 %collective-permute-done.2.refs_1_ = bf16[2,96,768]{2,1,0:T(8,128)(2,1)S(1)} collective-permute-done((bf16[2,96,768]{2,1,0:T(8,128)(2,1)S(1)}, bf16[2,96,768]{2,1,0:T(8,128)(2,1)S(1)}, u32[]{:S(2)}, u32[]{:S(2)}) %collective-permute-start.2) | collective-permute-done | bytes 294944 | tf_op jit(solution)/shard_map/ppermute | solution.py:493
  40.9 5.8 %collective-permute-done.6.refs_5_ = bf16[2,96,768]{2,1,0:T(8,128)(2,1)S(1)} collective-permute-done((bf16[2,96,768]{2,1,0:T(8,128)(2,1)S(1)}, bf16[2,96,768]{2,1,0:T(8,128)(2,1)S(1)}, u32[]{:S(2)}, u32[]{:S(2)}) %collective-permute-start.6) | collective-permute-done | bytes 294944 | tf_op jit(solution)/shard_map/ppermute | solution.py:493
  47.8 6.6 %collective-permute-done.7.refs_6_ = bf16[2,96,768]{2,1,0:T(8,128)(2,1)S(1)} collective-permute-done((bf16[2,96,768]{2,1,0:T(8,128)(2,1)S(1)}, bf16[2,96,768]{2,1,0:T(8,128)(2,1)S(1)}, u32[]{:S(2)}, u32[]{:S(2)}) %collective-permute-start.7) | collective-permute-done | bytes 294944 | tf_op jit(solution)/shard_map/ppermute | solution.py:493
  55.0 4.6 %collective-permute-done.8.refs_7_ = bf16[2,96,768]{2,1,0:T(8,128)(2,1)S(1)} collective-permute-done((bf16[2,96,768]{2,1,0:T(8,128)(2,1)S(1)}, bf16[2,96,768]{2,1,0:T(8,128)(2,1)S(1)}, u32[]{:S(2)}, u32[]{:S(2)}) %collective-permute-start.8) | collective-permute-done | bytes 294944 | tf_op jit(solution)/shard_map/ppermute | solution.py:493
  62.1 23.9 %shard_map.256 = (bf16[4,624,768]{2,1,0:T(8,128)(2,1)S(1)}, bf16[4,512,256]{2,1,0:T(8,128)(2,1)S(1)}, bf16[4,768,768]{2,1,0:T(8,128)(2,1)S(1)}, f32[512,768]{1,0:T(8,128)S(1)}, bf16[512,768]{1,0:T(8,128)(2,1)S(1)}) custom-call(s32[10]{0:T(128)S(1)} %pad_add_fusion.info_ref, bf16[624,768]{1,0:T(8,128)(2,1)S(1)} %get-tuple-element.69.h_ref, ...), custom_call_target="tpu_custom_call" | custom-call | flops 4831838208 | bytes 14548992 | tf_op jit(solution)/shard_map/pallas_call | solution.py:471
  86.1 2.2 copy-done.2
  89.2 1.9 copy-done.32
  93.3 13.3 %all-gather.3.cloned.1.call-done = bf16[6144,768]{1,0:T(8,128)(2,1)} async-done(((bf16[192,768]{1,0:T(8,128)(2,1)}), bf16[6144,768]{1,0:T(8,128)(2,1)}) %all-gather.3.cloned.1.call-update) | async-done | bytes 9437200 | tf_op jit(solution)/shard_map/all_gather | solution.py:663
  106.5 3.7 %copy-done = bf16[6144,768]{1,0:T(8,128)(2,1)S(1)} copy-done((bf16[6144,768]{1,0:T(8,128)(2,1)S(1)}, bf16[6144,768]{1,0:T(8,128)(2,1)}, u32[]{:S(2)}) %copy-start) | copy-done | bytes 9437208
  112.5 10.1 %shard_map.257 = (bf16[2,512,768]{2,1,0:T(8,128)(2,1)S(1)}, bf16[2,8,192,768]{3,2,1,0:T(8,128)(2,1)}, f32[2,1,768]{2,1,0:T(1,128)S(1)}, f32[512,768]{1,0:T(8,128)S(1)}) custom-call(s32[10]{0:T(128)S(1)} %pad_add_fusion.info_ref, bf16[512,768]{1,0:T(8,128)(2,1)S(1)} %copy-done.21, bf16[512,768]{1,0:T(8,128)(2,1)S(1)} %copy-done.18, ...), custom_call_target="tpu_custom_call" | custom-call | flops 6039797760 | bytes 40919040 | tf_op jit(solution)/shard_map/pallas_call | solution.py:471
  122.9 10.0 %shard_map.258 = (bf16[2,512,768]{2,1,0:T(8,128)(2,1)S(1)}, bf16[2,8,192,768]{3,2,1,0:T(8,128)(2,1)S(1)}, f32[2,1,768]{2,1,0:T(1,128)S(1)}, f32[512,768]{1,0:T(8...) custom-call(s32[10]{0:T(128)S(1)} %pad_add_fusion.info_ref, bf16[512,768]{1,0:T(8,128)(2,1)S(1)} %copy-done.22, ...), custom_call_target="tpu_custom_call" | custom-call | flops 6039797760 | bytes 50405376 | tf_op jit(solution)/shard_map/pallas_call | solution.py:471
  135.7 2.2 copy-done.4
  137.9 2.3 copy-done.5
  140.2 2.6 %shard_map.259 = (bf16[2,2,192,768]{3,2,1,0:T(8,128)(2,1)S(1)}, bf16[2,2,192,768]{3,2,1,0:T(8,128)(2,1)S(1)}, bf16[2,2,192,768]{3,2,1,0:T(8,128)(2,1)S(1)}, bf16[2,2,192,768]{3,2,1,0:T(8,128)(2,1)S(1)}) custom-call(bf16[2,8,192,768]{3,2,1,0:T(8,128)(2,1)S(1)} %get-tuple-element.80.own_ref, bf16[2,8,192,768]{3,2,1,0:T(8,128)(2,1)S(1)} %copy-done.5), custom_call_target="tpu_custom_call" | custom-call | bytes 14155776 | tf_op jit(solution)/shard_map/pallas_call | solution.py:571
  145.8 2.1 copy-done.33
  147.9 15.8 %shard_map.260 = (bf16[2,8,96,768]{3,2,1,0:T(8,128)(2,1)S(1)}, bf16[1,8,96,768]{3,2,1,0:T(8,128)(2,1)S(1)}, bf16[1,8,96,768]{3,2,1,0:T(8,128)(2,1)S(1)}, bf16[4,512,768]{2,1,0:T(8,128)(2,1)S(1)}) custom-call(s32[10]{0:T(128)S(1)} %pad_add_fusion.info_ref, bf16[512,768]{1,0:T(8,128)(2,1)S(1)} %get-tuple-element.85.dz_ref, ...), custom_call_target="tpu_custom_call" | custom-call | flops 9663676416 | bytes 23035904 | tf_op jit(solution)/shard_map/pallas_call | solution.py:471
  164.3 7.6 %collective-permute-done.23 = bf16[2,2,192,768]{3,2,1,0:T(8,128)(2,1)S(1)} collective-permute-done((bf16[2,2,192,768]{3,2,1,0:T(8,128)(2,1)S(1)}, bf16[2,2,192,768]{3,2,1,0:T(8,128)(2,1)S(1)}, u32[]{:S(2)}, u32[]{:S(2)}) %collective-permute-start.23) | collective-permute-done | bytes 1179680 | tf_op jit(solution)/shard_map/ppermute | solution.py:493
  177.6 13.5 %shard_map.262 = (f32[490,768]{1,0:T(8,128)}, f32[490,768]{1,0:T(8,128)}, f32[16,768]{1,0:T(8,128)S(1)}) custom-call(s32[10]{0:T(128)S(1)} %pad_add_fusion.info_ref, bf16[4,512,768]{2,1,0:T(8,128)(2,1)S(1)} %get-tuple-element.101.dq_ref, bf16[4,768,768]{2,1,0:T(8,128)(2,1)S(1)} %copy-done.3, bf16[2,512,768]{2,1,0:T(8,128)(2,1)S(1)} %copy-done.9, ...), custom_call_target="tpu_custom_call" | custom-call | flops 4831838208 | bytes 50454528 | tf_op jit(solution)/shard_map/pallas_call | solution.py:471
  193.3 1.9 collective-permute-start.29
  197.2 2.1 collective-permute-done.29
  199.4 5.1 %collective-permute-done.31 = bf16[2,192,768]{2,1,0:T(8,128)(2,1)S(1)} collective-permute-done((bf16[2,192,768]{2,1,0:T(8,128)(2,1)S(1)}, bf16[2,192,768]{2,1,0:T(8,128)(2,1)S(1)}, u32[]{:S(2)}, u32[]{:S(2)}) %collective-permute-start.31) | collective-permute-done | bytes 589856 | tf_op jit(solution)/shard_map/ppermute | solution.py:493
  211.6 5.0 %collective-permute-done.33 = bf16[2,96,768]{2,1,0:T(8,128)(2,1)S(1)} collective-permute-done((bf16[2,96,768]{2,1,0:T(8,128)(2,1)S(1)}, bf16[2,96,768]{2,1,0:T(8,128)(2,1)S(1)}, u32[]{:S(2)}, u32[]{:S(2)}) %collective-permute-start.33) | collective-permute-done | bytes 294944 | tf_op jit(solution)/shard_map/ppermute | solution.py:493
  216.6 2.3 collective-permute-done.36
  219.1 3.0 %collective-permute-done.34 = bf16[2,96,768]{2,1,0:T(8,128)(2,1)S(1)} collective-permute-done((bf16[2,96,768]{2,1,0:T(8,128)(2,1)S(1)}, bf16[2,96,768]{2,1,0:T(8,128)(2,1)S(1)}, u32[]{:S(2)}, u32[]{:S(2)}) %collective-permute-start.34) | collective-permute-done | bytes 294944 | tf_op jit(solution)/shard_map/ppermute | solution.py:493
  223.6 2.7 %collective-permute-done.37 = f32[16,768]{1,0:T(8,128)S(1)} collective-permute-done((f32[16,768]{1,0:T(8,128)S(1)}, f32[16,768]{1,0:T(8,128)S(1)}, u32[]{:S(2)}, u32[]{:S(2)}) %collective-permute-start.37) | collective-permute-done | bytes 49184 | tf_op jit(solution)/shard_map/ppermute | solution.py:493
  228.9 1.9 collective-permute-start.40
  230.8 2.1 collective-permute-done.38
  233.5 6.8 %collective-permute-done.39 = bf16[96,768]{1,0:T(8,128)(2,1)S(1)} collective-permute-done((bf16[96,768]{1,0:T(8,128)(2,1)S(1)}, bf16[96,768]{1,0:T(8,128)(2,1)S(1)}, u32[]{:S(2)}, u32[]{:S(2)}) %collective-permute-start.39) | collective-permute-done | bytes 147488 | tf_op jit(solution)/shard_map/ppermute | solution.py:493
  (195 shorter events, 58.3 us)
Async XLA Ops:
  7.2 99.3 %all-gather.3.cloned.1.call-start = ((), (), s32[]{:S(2)}) async-start(), calls=%async_computation | async-start | bytes 9732096 | tf_op jit(solution)/shard_map/all_gather | solution.py:663
  10.2 16.9 %collective-permute-start = (bf16[98,768]{1,0:T(8,128)(2,1)S(1)}, bf16[98,768]{1,0:T(8,128)(2,1)S(1)}, u32[]{:S(2)}, u32[]{:S(2)}) collective-permute-start(bf16[98,768]{1,0:T(8,128)(2,1)S(1)} %slice_select_fusion), channel_id=1, source_target_pairs={{0,1},{1,0},{2,3},{3,2},{4,5},{5,4},{6,7},{7,6},{8,9},{9,8},{10,11... | collective-permute-start | bytes 451592 | tf_op jit(solution)/shard_map/ppermute | solution.py:493
  11.0 11.3 %collective-permute-start.1 = (bf16[96,768]{1,0:T(8,128)(2,1)S(1)}, bf16[96,768]{1,0:T(8,128)(2,1)S(1)}, u32[]{:S(2)}, u32[]{:S(2)}) collective-permute-start(bf16[96,768]{1,0:T(8,128)(2,1)S(1)} %shard_map.255), channel_id=1, source_target_pairs={{0,16},{1,17},{2,18},{3,19},{4,20},{5,21},{6,22},{7,23},{8,24},{9,... | collective-permute-start | bytes 442376 | tf_op jit(solution)/shard_map/ppermute | solution.py:493
  22.3 14.1 %collective-permute-start.2 = (bf16[2,96,768]{2,1,0:T(8,128)(2,1)S(1)}, bf16[2,96,768]{2,1,0:T(8,128)(2,1)S(1)}, u32[]{:S(2)}, u32[]{:S(2)}) collective-permute-start(bf16[2,96,768]{2,1,0:T(8,128)(2,1)S(1)} %pad_maximum_fusion.refs_0_), channel_id=1, source_target_pairs={{0,8},{1,9},{2,10},{3,11},{4,12},{5,13},{6,14},{7,15},{8,0},{9,1},... | collective-permute-start | bytes 884744 | tf_op jit(solution)/shard_map/ppermute | solution.py:493
  24.0 15.2 %collective-permute-start.3 = (bf16[2,96,768]{2,1,0:T(8,128)(2,1)S(1)}, bf16[2,96,768]{2,1,0:T(8,128)(2,1)S(1)}, u32[]{:S(2)}, u32[]{:S(2)}) collective-permute-start(bf16[2,96,768]{2,1,0:T(8,128)(2,1)S(1)} %pad_maximum_fusion.refs_0_), channel_id=1, source_target_pairs={{0,4},{1,5},{2,6},{3,7},{4,0},{5,1},{6,2},{7,3},{8,12},{9,13},{10,... | collective-permute-start | bytes 884744 | tf_op jit(solution)/shard_map/ppermute | solution.py:493
  25.5 14.2 %collective-permute-start.5 = (bf16[2,96,768]{2,1,0:T(8,128)(2,1)S(1)}, bf16[2,96,768]{2,1,0:T(8,128)(2,1)S(1)}, u32[]{:S(2)}, u32[]{:S(2)}) collective-permute-start(bf16[2,96,768]{2,1,0:T(8,128)(2,1)S(1)} %pad_maximum_fusion.refs_0_), channel_id=1, source_target_pairs={{0,2},{1,3},{2,0},{3,1},{4,6},{5,7},{6,4},{7,5},{8,10},{9,11},{10,... | collective-permute-start | bytes 884744 | tf_op jit(solution)/shard_map/ppermute | solution.py:493
  27.0 13.4 %collective-permute-start.9 = (bf16[2,96,768]{2,1,0:T(8,128)(2,1)S(1)}, bf16[2,96,768]{2,1,0:T(8,128)(2,1)S(1)}, u32[]{:S(2)}, u32[]{:S(2)}) collective-permute-start(bf16[2,96,768]{2,1,0:T(8,128)(2,1)S(1)} %pad_maximum_fusion.refs_0_), channel_id=1, source_target_pairs={{0,1},{1,0},{2,3},{3,2},{4,5},{5,4},{6,7},{7,6},{8,9},{9,8},{10,11... | collective-permute-start | bytes 884744 | tf_op jit(solution)/shard_map/ppermute | solution.py:493
  36.5 10.2 %collective-permute-start.6 = (bf16[2,96,768]{2,1,0:T(8,128)(2,1)S(1)}, bf16[2,96,768]{2,1,0:T(8,128)(2,1)S(1)}, u32[]{:S(2)}, u32[]{:S(2)}) collective-permute-start(bf16[2,96,768]{2,1,0:T(8,128)(2,1)S(1)} %collective-permute-done.2.refs_1_), channel_id=1, source_target_pairs={{0,2},{1,3},{2,0},{3,1},{4,6},{5,7},{6,4},{7,5},{8,10},{9,11},{10,... | collective-permute-start | bytes 884744 | tf_op jit(solution)/shard_map/ppermute | solution.py:493
  37.7 10.1 %collective-permute-start.4 = (bf16[2,96,768]{2,1,0:T(8,128)(2,1)S(1)}, bf16[2,96,768]{2,1,0:T(8,128)(2,1)S(1)}, u32[]{:S(2)}, u32[]{:S(2)}) collective-permute-start(bf16[2,96,768]{2,1,0:T(8,128)(2,1)S(1)} %collective-permute-done.2.refs_1_), channel_id=1, source_target_pairs={{0,4},{1,5},{2,6},{3,7},{4,0},{5,1},{6,2},{7,3},{8,12},{9,13},{10,... | collective-permute-start | bytes 884744 | tf_op jit(solution)/shard_map/ppermute | solution.py:493
  39.3 15.1 %collective-permute-start.7 = (bf16[2,96,768]{2,1,0:T(8,128)(2,1)S(1)}, bf16[2,96,768]{2,1,0:T(8,128)(2,1)S(1)}, u32[]{:S(2)}, u32[]{:S(2)}) collective-permute-start(bf16[2,96,768]{2,1,0:T(8,128)(2,1)S(1)} %collective-permute-done.3.refs_2_), channel_id=1, source_target_pairs={{0,2},{1,3},{2,0},{3,1},{4,6},{5,7},{6,4},{7,5},{8,10},{9,11},{10,... | collective-permute-start | bytes 884744 | tf_op jit(solution)/shard_map/ppermute | solution.py:493
  39.7 14.7 %collective-permute-start.10 = (bf16[2,96,768]{2,1,0:T(8,128)(2,1)S(1)}, bf16[2,96,768]{2,1,0:T(8,128)(2,1)S(1)}, u32[]{:S(2)}, u32[]{:S(2)}) collective-permute-start(bf16[2,96,768]{2,1,0:T(8,128)(2,1)S(1)} %collective-permute-done.2.refs_1_), channel_id=1, source_target_pairs={{0,1},{1,0},{2,3},{3,2},{4,5},{5,4},{6,7},{7,6},{8,9},{9,8},{10,11... | collective-permute-start | bytes 884744 | tf_op jit(solution)/shard_map/ppermute | solution.py:493
  40.4 14.5 %collective-permute-start.11 = (bf16[2,96,768]{2,1,0:T(8,128)(2,1)S(1)}, bf16[2,96,768]{2,1,0:T(8,128)(2,1)S(1)}, u32[]{:S(2)}, u32[]{:S(2)}) collective-permute-start(bf16[2,96,768]{2,1,0:T(8,128)(2,1)S(1)} %collective-permute-done.3.refs_2_), channel_id=1, source_target_pairs={{0,1},{1,0},{2,3},{3,2},{4,5},{5,4},{6,7},{7,6},{8,9},{9,8},{10,11... | collective-permute-start | bytes 884744 | tf_op jit(solution)/shard_map/ppermute | solution.py:493
  46.7 12.9 %collective-permute-start.8 = (bf16[2,96,768]{2,1,0:T(8,128)(2,1)S(1)}, bf16[2,96,768]{2,1,0:T(8,128)(2,1)S(1)}, u32[]{:S(2)}, u32[]{:S(2)}) collective-permute-start(bf16[2,96,768]{2,1,0:T(8,128)(2,1)S(1)} %collective-permute-done.6.refs_5_), channel_id=1, source_target_pairs={{0,4},{1,5},{2,6},{3,7},{4,0},{5,1},{6,2},{7,3},{8,12},{9,13},{10,... | collective-permute-start | bytes 884744 | tf_op jit(solution)/shard_map/ppermute | solution.py:493
  47.8 11.8 %collective-permute-start.13 = (bf16[2,96,768]{2,1,0:T(8,128)(2,1)S(1)}, bf16[2,96,768]{2,1,0:T(8,128)(2,1)S(1)}, u32[]{:S(2)}, u32[]{:S(2)}) collective-permute-start(bf16[2,96,768]{2,1,0:T(8,128)(2,1)S(1)} %collective-permute-done.5.refs_4_), channel_id=1, source_target_pairs={{0,1},{1,0},{2,3},{3,2},{4,5},{5,4},{6,7},{7,6},{8,9},{9,8},{10,11... | collective-permute-start | bytes 884744 | tf_op jit(solution)/shard_map/ppermute | solution.py:493
  59.6 32.6 %collective-permute-start.18 = (f32[768]{0:T(1024)S(1)}, f32[768]{0:T(1024)S(1)}, u32[]{:S(2)}, u32[]{:S(2)}) collective-permute-start(f32[768]{0:T(1024)S(1)} %copy-done.44), channel_id=1, source_target_pairs={{0,1},{1,0},{2,3},{3,2},{4,5},{5,4},{6,7},{7,6},{8,9},{9,8},{10,11... | collective-permute-start | bytes 9224 | tf_op jit(solution)/shard_map/ppermute | solution.py:493
  60.1 31.9 %collective-permute-start.17 = (f32[768]{0:T(1024)S(1)}, f32[768]{0:T(1024)S(1)}, u32[]{:S(2)}, u32[]{:S(2)}) collective-permute-start(f32[768]{0:T(1024)S(1)} %copy-done.44), channel_id=1, source_target_pairs={{0,2},{1,3},{2,0},{3,1},{4,6},{5,7},{6,4},{7,5},{8,10},{9,11},{10,... | collective-permute-start | bytes 9224 | tf_op jit(solution)/shard_map/ppermute | solution.py:493
  122.6 13.1 %collective-permute-start.20 = (bf16[2,8,192,768]{3,2,1,0:T(8,128)(2,1)}, bf16[2,8,192,768]{3,2,1,0:T(8,128)(2,1)S(1)}, u32[]{:S(2)}, u32[]{:S(2)}) collective-permute-start(bf16[2,8,192,768]{3,2,1,0:T(8,128)(2,1)} %get-tuple-element.81), channel_id=1, source_target_pairs={{0,1},{1,0},{2,3},{3,2},{4,5},{5,4},{6,7},{7,6},{8,9},{9,8},{10,11... | collective-permute-start | bytes 14155784 | tf_op jit(solution)/shard_map/ppermute | solution.py:493
  135.4 10.4 %collective-permute-start.21 = (bf16[112,768]{1,0:T(8,128)(2,1)S(1)}, bf16[112,768]{1,0:T(8,128)(2,1)S(1)}, u32[]{:S(2)}, u32[]{:S(2)}) collective-permute-start(bf16[112,768]{1,0:T(8,128)(2,1)S(1)} %slice.160), channel_id=1, source_target_pairs={{0,1},{1,0},{2,3},{3,2},{4,5},{5,4},{6,7},{7,6},{8,9},{9,8},{10,11... | collective-permute-start | bytes 516104 | tf_op jit(solution)/shard_map/ppermute | solution.py:493
  143.8 28.1 %collective-permute-start.23 = (bf16[2,2,192,768]{3,2,1,0:T(8,128)(2,1)S(1)}, bf16[2,2,192,768]{3,2,1,0:T(8,128)(2,1)S(1)}, u32[]{:S(2)}, u32[]{:S(2)}) collective-permute-start(bf16[2,2,192,768]{3,2,1,0:T(8,128)(2,1)S(1)} %get-tuple-element.84), channel_id=1, source_target_pairs={{0,2},{1,3},{2,0},{3,1},{4,6},{5,7},{6,4},{7,5},{8,10},{9,11},{10,... | collective-permute-start | bytes 3538952 | tf_op jit(solution)/shard_map/ppermute | solution.py:493
  145.2 27.9 %collective-permute-start.22 = (bf16[2,2,192,768]{3,2,1,0:T(8,128)(2,1)S(1)}, bf16[2,2,192,768]{3,2,1,0:T(8,128)(2,1)S(1)}, u32[]{:S(2)}, u32[]{:S(2)}) collective-permute-start(bf16[2,2,192,768]{3,2,1,0:T(8,128)(2,1)S(1)} %get-tuple-element.83), channel_id=1, source_target_pairs={{0,4},{1,5},{2,6},{3,7},{4,0},{5,1},{6,2},{7,3},{8,12},{9,13},{10,... | collective-permute-start | bytes 3538952 | tf_op jit(solution)/shard_map/ppermute | solution.py:493
  163.8 9.6 %collective-permute-start.25 = (bf16[1,8,96,768]{3,2,1,0:T(8,128)(2,1)S(1)}, bf16[1,8,96,768]{3,2,1,0:T(8,128)(2,1)S(1)}, u32[]{:S(2)}, u32[]{:S(2)}) collective-permute-start(bf16[1,8,96,768]{3,2,1,0:T(8,128)(2,1)S(1)} %get-tuple-element.97), channel_id=1, source_target_pairs={{0,1},{1,0},{2,3},{3,2},{4,5},{5,4},{6,7},{7,6},{8,9},{9,8},{10,11... | collective-permute-start | bytes 3538952 | tf_op jit(solution)/shard_map/ppermute | solution.py:493
  163.8 9.6 %collective-permute-start.24 = (bf16[1,8,96,768]{3,2,1,0:T(8,128)(2,1)S(1)}, bf16[1,8,96,768]{3,2,1,0:T(8,128)(2,1)S(1)}, u32[]{:S(2)}, u32[]{:S(2)}) collective-permute-start(bf16[1,8,96,768]{3,2,1,0:T(8,128)(2,1)S(1)} %get-tuple-element.95), channel_id=1, source_target_pairs={{0,1},{1,0},{2,3},{3,2},{4,5},{5,4},{6,7},{7,6},{8,9},{9,8},{10,11... | collective-permute-start | bytes 3538952 | tf_op jit(solution)/shard_map/ppermute | solution.py:493
  174.9 16.3 %collective-permute-start.27 = (bf16[2,2,96,768]{3,2,1,0:T(8,128)(2,1)S(1)}, bf16[2,2,96,768]{3,2,1,0:T(8,128)(2,1)S(1)}, u32[]{:S(2)}, u32[]{:S(2)}) collective-permute-start(bf16[2,2,96,768]{3,2,1,0:T(8,128)(2,1)S(1)} %get-tuple-element.100), channel_id=1, source_target_pairs={{0,2},{1,3},{2,0},{3,1},{4,6},{5,7},{6,4},{7,5},{8,10},{9,11},{10,... | collective-permute-start | bytes 1769480 | tf_op jit(solution)/shard_map/ppermute | solution.py:493
  175.6 16.3 %collective-permute-start.26 = (bf16[2,2,96,768]{3,2,1,0:T(8,128)(2,1)S(1)}, bf16[2,2,96,768]{3,2,1,0:T(8,128)(2,1)S(1)}, u32[]{:S(2)}, u32[]{:S(2)}) collective-permute-start(bf16[2,2,96,768]{3,2,1,0:T(8,128)(2,1)S(1)} %get-tuple-element.99), channel_id=1, source_target_pairs={{0,4},{1,5},{2,6},{3,7},{4,0},{5,1},{6,2},{7,3},{8,12},{9,13},{10,... | collective-permute-start | bytes 1769480 | tf_op jit(solution)/shard_map/ppermute | solution.py:493
  176.9 27.6 %collective-permute-start.31 = (bf16[2,192,768]{2,1,0:T(8,128)(2,1)S(1)}, bf16[2,192,768]{2,1,0:T(8,128)(2,1)S(1)}, u32[]{:S(2)}, u32[]{:S(2)}) collective-permute-start(bf16[2,192,768]{2,1,0:T(8,128)(2,1)S(1)} %fusion.2), channel_id=1, source_target_pairs={{0,4},{1,5},{2,6},{3,7},{4,0},{5,1},{6,2},{7,3},{8,12},{9,13},{10,... | collective-permute-start | bytes 1769480 | tf_op jit(solution)/shard_map/ppermute | solution.py:493
  195.2 16.4 %collective-permute-start.35 = (bf16[2,192,768]{2,1,0:T(8,128)(2,1)S(1)}, bf16[2,192,768]{2,1,0:T(8,128)(2,1)S(1)}, u32[]{:S(2)}, u32[]{:S(2)}) collective-permute-start(bf16[2,192,768]{2,1,0:T(8,128)(2,1)S(1)} %fusion.1), channel_id=1, source_target_pairs={{0,2},{1,3},{2,0},{3,1},{4,6},{5,7},{6,4},{7,5},{8,10},{9,11},{10,... | collective-permute-start | bytes 1769480 | tf_op jit(solution)/shard_map/ppermute | solution.py:493
  196.7 11.9 %collective-permute-start.30 = (bf16[2,96,768]{2,1,0:T(8,128)(2,1)S(1)}, bf16[2,96,768]{2,1,0:T(8,128)(2,1)S(1)}, u32[]{:S(2)}, u32[]{:S(2)}) collective-permute-start(bf16[2,96,768]{2,1,0:T(8,128)(2,1)S(1)} %fusion.7), channel_id=1, source_target_pairs={{0,4},{1,5},{2,6},{3,7},{4,0},{5,1},{6,2},{7,3},{8,12},{9,13},{10,... | collective-permute-start | bytes 884744 | tf_op jit(solution)/shard_map/ppermute | solution.py:493
  204.7 14.2 %collective-permute-start.36 = (bf16[2,192,768]{2,1,0:T(8,128)(2,1)S(1)}, bf16[2,192,768]{2,1,0:T(8,128)(2,1)S(1)}, u32[]{:S(2)}, u32[]{:S(2)}) collective-permute-start(bf16[2,192,768]{2,1,0:T(8,128)(2,1)S(1)} %fusion), channel_id=1, source_target_pairs={{0,8},{1,9},{2,10},{3,11},{4,12},{5,13},{6,14},{7,15},{8,0},{9,1},... | collective-permute-start | bytes 1769480 | tf_op jit(solution)/shard_map/ppermute | solution.py:493
  206.2 10.4 %collective-permute-start.33 = (bf16[2,96,768]{2,1,0:T(8,128)(2,1)S(1)}, bf16[2,96,768]{2,1,0:T(8,128)(2,1)S(1)}, u32[]{:S(2)}, u32[]{:S(2)}) collective-permute-start(bf16[2,96,768]{2,1,0:T(8,128)(2,1)S(1)} %fusion.6), channel_id=1, source_target_pairs={{0,2},{1,3},{2,0},{3,1},{4,6},{5,7},{6,4},{7,5},{8,10},{9,11},{10,... | collective-permute-start | bytes 884744 | tf_op jit(solution)/shard_map/ppermute | solution.py:493
  210.2 11.9 %collective-permute-start.34 = (bf16[2,96,768]{2,1,0:T(8,128)(2,1)S(1)}, bf16[2,96,768]{2,1,0:T(8,128)(2,1)S(1)}, u32[]{:S(2)}, u32[]{:S(2)}) collective-permute-start(bf16[2,96,768]{2,1,0:T(8,128)(2,1)S(1)} %fusion.5), channel_id=1, source_target_pairs={{0,8},{1,9},{2,10},{3,11},{4,12},{5,13},{6,14},{7,15},{8,0},{9,1},... | collective-permute-start | bytes 884744 | tf_op jit(solution)/shard_map/ppermute | solution.py:493
  227.9 12.4 %collective-permute-start.39 = (bf16[96,768]{1,0:T(8,128)(2,1)S(1)}, bf16[96,768]{1,0:T(8,128)(2,1)S(1)}, u32[]{:S(2)}, u32[]{:S(2)}) collective-permute-start(bf16[96,768]{1,0:T(8,128)(2,1)S(1)} %fusion.9), channel_id=1, source_target_pairs={{0,16},{1,17},{2,18},{3,19},{4,20},{5,21},{6,22},{7,23},{8,24},{9,... | collective-permute-start | bytes 442376 | tf_op jit(solution)/shard_map/ppermute | solution.py:493
  228.9 15.1 %collective-permute-start.40 = (bf16[192,768]{1,0:T(8,128)(2,1)S(1)}, bf16[192,768]{1,0:T(8,128)(2,1)S(1)}, u32[]{:S(2)}, u32[]{:S(2)}) collective-permute-start(bf16[192,768]{1,0:T(8,128)(2,1)S(1)} %fusion.4), channel_id=1, source_target_pairs={{0,16},{1,17},{2,18},{3,19},{4,20},{5,21},{6,22},{7,23},{8,24},{9,... | collective-permute-start | bytes 884744 | tf_op jit(solution)/shard_map/ppermute | solution.py:493
  (55 other events, 567.3 us)
Sparse Core Ops, SparseCore 0:
  11.6 94.9 all-gather.2

commit v3 on v2

--- a/solution.py
+++ b/solution.py
@@ -20,7 +20,7 @@
 HALF_FIRST = 4
 SCALE = HEAD_DIM ** (-0.5)
 NEG = -1e30
-VMEM = {"pack": 8, "prep": 24, "forward": 24, "mlp": 24, "back": 24, "late": 24, "merge": 16}
+VMEM = {"pack": 4, "prep": 8, "forward": 16, "mlp": 16, "back": 16, "late": 16, "merge": 8}
 BF = jnp.bfloat16
 F32 = jnp.float32
 

time: 253 us -> 244 us (0.964)
  local copies, waits for them, and re-layouts: 30.3 us -> 20.2 us
    unnamed x91 -> x79, local copies, waits for them, and re-layouts: 27.9 us -> 17.8 us
  transfers between devices with their start and end apart: 42 -> 42, of which waited for: 22 -> 22; matrix products, arithmetic and copies ran while one was open for 3% -> 3% of each run, Pallas kernels for 27% -> 28%
where the time goes in v3:
time: 244 us
  waiting for transfers between devices  86.4 us (35%)
  Pallas kernels  78.5 us (32%)
  starting transfers between devices  36.6 us (15%)
  local copies, waits for them, and re-layouts  20.2 us (8%)
  between operations  14.6 us (6%)
  other arithmetic  7.62 us (3%)
    pallas_call x6, Pallas kernels, call(): pl.pallas_call(kernel, grid_spec=pltpu.PrefetchScalarGridSpec(num_scalar_...  74.2 us
    ppermute x41, waiting for transfers between devices, swap(): lax.ppermute(value, ('wide', 'narrow'), [(i, i ^ bit) for i in range(devi...  73.3 us
    ppermute x41, starting transfers between devices, swap(): lax.ppermute(value, ('wide', 'narrow'), [(i, i ^ bit) for i in range(devi...  36.6 us
    unnamed x79, local copies, waits for them, and re-layouts  17.8 us
    all_gather x1, waiting for transfers between devices, body(): full = lax.all_gather(mlp, ('wide', 'narrow'), axis=0, tiled=False)  13.1 us
  transfers between devices with their start and end apart: 42, of which 22 were waited for; matrix products, arithmetic and copies ran while one was open for 3% of the time, Pallas kernels for 28%

profile of v3, /device:TPU:0, one launch (start us, length us, event | category | flops | bytes accessed | tf_op | source)
XLA Modules:
  0.0 243.9 jit_solution(1022520653654783408)
XLA Ops:
  7.3 1.7 pad_maximum_fusion.1
  11.0 3.7 %collective-permute-start.1 = (bf16[96,768]{1,0:T(8,128)(2,1)S(1)}, bf16[96,768]{1,0:T(8,128)(2,1)S(1)}, u32[]{:S(2)}, u32[]{:S(2)}) collective-permute-start(bf16[96,768]{1,0:T(8,128)(2,1)S(1)} %shard_map.255), channel_id=1, source_target_pairs={{0,16},{1,17},{2,18},{3,19},{4,20},{5,21},{6,22},{7,23},{8,24},{9,... | collective-permute-start | bytes 442376 | tf_op jit(solution)/shard_map/ppermute | solution.py:493
  14.7 7.6 %collective-permute-done.1 = bf16[96,768]{1,0:T(8,128)(2,1)S(1)} collective-permute-done((bf16[96,768]{1,0:T(8,128)(2,1)S(1)}, bf16[96,768]{1,0:T(8,128)(2,1)S(1)}, u32[]{:S(2)}, u32[]{:S(2)}) %collective-permute-start.1) | collective-permute-done | bytes 147488 | tf_op jit(solution)/shard_map/ppermute | solution.py:493
  25.5 1.5 collective-permute-start.5
  28.5 1.6 shard_map.254
  32.1 4.3 %collective-permute-done.2.refs_1_ = bf16[2,96,768]{2,1,0:T(8,128)(2,1)S(1)} collective-permute-done((bf16[2,96,768]{2,1,0:T(8,128)(2,1)S(1)}, bf16[2,96,768]{2,1,0:T(8,128)(2,1)S(1)}, u32[]{:S(2)}, u32[]{:S(2)}) %collective-permute-start.2) | collective-permute-done | bytes 294944 | tf_op jit(solution)/shard_map/ppermute | solution.py:493
  37.7 1.6 collective-permute-start.4
  40.9 5.8 %collective-permute-done.6.refs_5_ = bf16[2,96,768]{2,1,0:T(8,128)(2,1)S(1)} collective-permute-done((bf16[2,96,768]{2,1,0:T(8,128)(2,1)S(1)}, bf16[2,96,768]{2,1,0:T(8,128)(2,1)S(1)}, u32[]{:S(2)}, u32[]{:S(2)}) %collective-permute-start.6) | collective-permute-done | bytes 294944 | tf_op jit(solution)/shard_map/ppermute | solution.py:493
  47.8 6.6 %collective-permute-done.7.refs_6_ = bf16[2,96,768]{2,1,0:T(8,128)(2,1)S(1)} collective-permute-done((bf16[2,96,768]{2,1,0:T(8,128)(2,1)S(1)}, bf16[2,96,768]{2,1,0:T(8,128)(2,1)S(1)}, u32[]{:S(2)}, u32[]{:S(2)}) %collective-permute-start.7) | collective-permute-done | bytes 294944 | tf_op jit(solution)/shard_map/ppermute | solution.py:493
  55.0 4.6 %collective-permute-done.8.refs_7_ = bf16[2,96,768]{2,1,0:T(8,128)(2,1)S(1)} collective-permute-done((bf16[2,96,768]{2,1,0:T(8,128)(2,1)S(1)}, bf16[2,96,768]{2,1,0:T(8,128)(2,1)S(1)}, u32[]{:S(2)}, u32[]{:S(2)}) %collective-permute-start.8) | collective-permute-done | bytes 294944 | tf_op jit(solution)/shard_map/ppermute | solution.py:493
  62.1 24.2 %shard_map.256 = (bf16[4,624,768]{2,1,0:T(8,128)(2,1)S(1)}, bf16[4,512,256]{2,1,0:T(8,128)(2,1)S(1)}, bf16[4,768,768]{2,1,0:T(8,128)(2,1)S(1)}, f32[512,768]{1,0:T(8,128)S(1)}, bf16[512,768]{1,0:T(8,128)(2,1)S(1)}) custom-call(s32[10]{0:T(128)S(1)} %pad_add_fusion.info_ref, bf16[624,768]{1,0:T(8,128)(2,1)S(1)} %get-tuple-element.69.h_ref, ...), custom_call_target="tpu_custom_call" | custom-call | flops 4831838208 | bytes 14548992 | tf_op jit(solution)/shard_map/pallas_call | solution.py:471
  86.3 2.2 copy-done.2
  89.5 1.8 copy-done.24
  93.5 13.1 %all-gather.3.cloned.1.call-done = bf16[6144,768]{1,0:T(8,128)(2,1)} async-done(((bf16[192,768]{1,0:T(8,128)(2,1)}), bf16[6144,768]{1,0:T(8,128)(2,1)}) %all-gather.3.cloned.1.call-update) | async-done | bytes 9437200 | tf_op jit(solution)/shard_map/all_gather | solution.py:663
  106.5 3.7 %copy-done = bf16[6144,768]{1,0:T(8,128)(2,1)S(1)} copy-done((bf16[6144,768]{1,0:T(8,128)(2,1)S(1)}, bf16[6144,768]{1,0:T(8,128)(2,1)}, u32[]{:S(2)}) %copy-start) | copy-done | bytes 9437208
  112.5 8.8 %shard_map.257 = (bf16[2,512,768]{2,1,0:T(8,128)(2,1)S(1)}, bf16[2,8,192,768]{3,2,1,0:T(8,128)(2,1)S(1)}, f32[2,1,768]{2,1,0:T(1,128)S(1)}, f32[512,768]{1,0:T(8,128)S(1)}) custom-call(s32[10]{0:T(128)S(1)} %pad_add_fusion.info_ref, bf16[512,768]{1,0:T(8,128)(2,1)S(1)} %copy-done.14, bf16[512,768]{1,0:T(8,128)(2,1)S(1)} %copy-done.11, ...), custom_call_target="tpu_custom_call" | custom-call | flops 6039797760 | bytes 40919040 | tf_op jit(solution)/shard_map/pallas_call | solution.py:471
  121.7 10.1 %shard_map.258 = (bf16[2,512,768]{2,1,0:T(8,128)(2,1)S(1)}, bf16[2,8,192,768]{3,2,1,0:T(8,128)(2,1)S(1)}, f32[2,1,768]{2,1,0:T(1,128)S(1)}, f32[512,768]{1,0:T(8...) custom-call(s32[10]{0:T(128)S(1)} %pad_add_fusion.info_ref, bf16[512,768]{1,0:T(8,128)(2,1)S(1)} %copy-done.14, ...), custom_call_target="tpu_custom_call" | custom-call | flops 6039797760 | bytes 50405376 | tf_op jit(solution)/shard_map/pallas_call | solution.py:471
  132.2 2.6 %shard_map.259 = (bf16[2,2,192,768]{3,2,1,0:T(8,128)(2,1)S(1)}, bf16[2,2,192,768]{3,2,1,0:T(8,128)(2,1)S(1)}, bf16[2,2,192,768]{3,2,1,0:T(8,128)(2,1)S(1)}, bf16[2,2,192,768]{3,2,1,0:T(8,128)(2,1)S(1)}) custom-call(bf16[2,8,192,768]{3,2,1,0:T(8,128)(2,1)S(1)} %get-tuple-element.80.own_ref, bf16[2,8,192,768]{3,2,1,0:T(8,128)(2,1)S(1)} %collective-permute-done.20.refs_0_), custom_call_target="tpu_custom_call" | custom-call | bytes 14155776 | tf_op jit(solution)/shard_map/pallas_call | solution.py:571
  136.9 15.8 %shard_map.260 = (bf16[2,8,96,768]{3,2,1,0:T(8,128)(2,1)S(1)}, bf16[1,8,96,768]{3,2,1,0:T(8,128)(2,1)S(1)}, bf16[1,8,96,768]{3,2,1,0:T(8,128)(2,1)S(1)}, bf16[4,512,768]{2,1,0:T(8,128)(2,1)S(1)}) custom-call(s32[10]{0:T(128)S(1)} %pad_add_fusion.info_ref, bf16[512,768]{1,0:T(8,128)(2,1)S(1)} %get-tuple-element.85.dz_ref, ...), custom_call_target="tpu_custom_call" | custom-call | flops 9663676416 | bytes 23035904 | tf_op jit(solution)/shard_map/pallas_call | solution.py:471
  153.3 9.7 %collective-permute-done.23 = bf16[2,2,192,768]{3,2,1,0:T(8,128)(2,1)S(1)} collective-permute-done((bf16[2,2,192,768]{3,2,1,0:T(8,128)(2,1)S(1)}, bf16[2,2,192,768]{3,2,1,0:T(8,128)(2,1)S(1)}, u32[]{:S(2)}, u32[]{:S(2)}) %collective-permute-start.23) | collective-permute-done | bytes 1179680 | tf_op jit(solution)/shard_map/ppermute | solution.py:493
  168.6 13.7 %shard_map.262 = (f32[490,768]{1,0:T(8,128)}, f32[490,768]{1,0:T(8,128)}, f32[16,768]{1,0:T(8,128)S(1)}) custom-call(s32[10]{0:T(128)S(1)} %pad_add_fusion.info_ref, bf16[4,512,768]{2,1,0:T(8,128)(2,1)S(1)} %get-tuple-element.101.dq_ref, bf16[4,768,768]{2,1,0:T(8,128)(2,1)S(1)} %bitcast.66, bf16[2,512,768]{2,1,0:T(8,128)(2,1)S(1)} %get-tuple-element.102.actm_ref, ...), custom_call_target="tpu_custom_call" | custom-call | flops 4831838208 | bytes 50454528 | tf_op jit(solution)/shard_map/pallas_call | solution.py:471
  184.3 1.9 collective-permute-start.29
  188.2 2.1 collective-permute-done.29
  190.3 5.1 %collective-permute-done.31 = bf16[2,192,768]{2,1,0:T(8,128)(2,1)S(1)} collective-permute-done((bf16[2,192,768]{2,1,0:T(8,128)(2,1)S(1)}, bf16[2,192,768]{2,1,0:T(8,128)(2,1)S(1)}, u32[]{:S(2)}, u32[]{:S(2)}) %collective-permute-start.31) | collective-permute-done | bytes 589856 | tf_op jit(solution)/shard_map/ppermute | solution.py:493
  202.6 5.0 %collective-permute-done.33 = bf16[2,96,768]{2,1,0:T(8,128)(2,1)S(1)} collective-permute-done((bf16[2,96,768]{2,1,0:T(8,128)(2,1)S(1)}, bf16[2,96,768]{2,1,0:T(8,128)(2,1)S(1)}, u32[]{:S(2)}, u32[]{:S(2)}) %collective-permute-start.33) | collective-permute-done | bytes 294944 | tf_op jit(solution)/shard_map/ppermute | solution.py:493
  207.6 2.3 collective-permute-done.36
  210.0 3.0 %collective-permute-done.34 = bf16[2,96,768]{2,1,0:T(8,128)(2,1)S(1)} collective-permute-done((bf16[2,96,768]{2,1,0:T(8,128)(2,1)S(1)}, bf16[2,96,768]{2,1,0:T(8,128)(2,1)S(1)}, u32[]{:S(2)}, u32[]{:S(2)}) %collective-permute-start.34) | collective-permute-done | bytes 294944 | tf_op jit(solution)/shard_map/ppermute | solution.py:493
  214.6 2.7 %collective-permute-done.37 = f32[16,768]{1,0:T(8,128)S(1)} collective-permute-done((f32[16,768]{1,0:T(8,128)S(1)}, f32[16,768]{1,0:T(8,128)S(1)}, u32[]{:S(2)}, u32[]{:S(2)}) %collective-permute-start.37) | collective-permute-done | bytes 49184 | tf_op jit(solution)/shard_map/ppermute | solution.py:493
  217.3 1.6 collective-permute-start.38
  219.9 1.9 collective-permute-start.40
  221.8 2.0 collective-permute-done.38
  224.4 6.8 %collective-permute-done.39 = bf16[96,768]{1,0:T(8,128)(2,1)S(1)} collective-permute-done((bf16[96,768]{1,0:T(8,128)(2,1)S(1)}, bf16[96,768]{1,0:T(8,128)(2,1)S(1)}, u32[]{:S(2)}, u32[]{:S(2)}) %collective-permute-start.39) | collective-permute-done | bytes 147488 | tf_op jit(solution)/shard_map/ppermute | solution.py:493
  (184 shorter events, 50.1 us)
Async XLA Ops:
  7.2 99.3 %all-gather.3.cloned.1.call-start = ((), (), s32[]{:S(2)}) async-start(), calls=%async_computation | async-start | bytes 9732096 | tf_op jit(solution)/shard_map/all_gather | solution.py:663
  10.2 16.9 %collective-permute-start = (bf16[98,768]{1,0:T(8,128)(2,1)S(1)}, bf16[98,768]{1,0:T(8,128)(2,1)S(1)}, u32[]{:S(2)}, u32[]{:S(2)}) collective-permute-start(bf16[98,768]{1,0:T(8,128)(2,1)S(1)} %slice_select_fusion), channel_id=1, source_target_pairs={{0,1},{1,0},{2,3},{3,2},{4,5},{5,4},{6,7},{7,6},{8,9},{9,8},{10,11... | collective-permute-start | bytes 451592 | tf_op jit(solution)/shard_map/ppermute | solution.py:493
  11.0 11.3 %collective-permute-start.1 = (bf16[96,768]{1,0:T(8,128)(2,1)S(1)}, bf16[96,768]{1,0:T(8,128)(2,1)S(1)}, u32[]{:S(2)}, u32[]{:S(2)}) collective-permute-start(bf16[96,768]{1,0:T(8,128)(2,1)S(1)} %shard_map.255), channel_id=1, source_target_pairs={{0,16},{1,17},{2,18},{3,19},{4,20},{5,21},{6,22},{7,23},{8,24},{9,... | collective-permute-start | bytes 442376 | tf_op jit(solution)/shard_map/ppermute | solution.py:493
  22.3 14.1 %collective-permute-start.2 = (bf16[2,96,768]{2,1,0:T(8,128)(2,1)S(1)}, bf16[2,96,768]{2,1,0:T(8,128)(2,1)S(1)}, u32[]{:S(2)}, u32[]{:S(2)}) collective-permute-start(bf16[2,96,768]{2,1,0:T(8,128)(2,1)S(1)} %pad_maximum_fusion.refs_0_), channel_id=1, source_target_pairs={{0,8},{1,9},{2,10},{3,11},{4,12},{5,13},{6,14},{7,15},{8,0},{9,1},... | collective-permute-start | bytes 884744 | tf_op jit(solution)/shard_map/ppermute | solution.py:493
  24.0 15.2 %collective-permute-start.3 = (bf16[2,96,768]{2,1,0:T(8,128)(2,1)S(1)}, bf16[2,96,768]{2,1,0:T(8,128)(2,1)S(1)}, u32[]{:S(2)}, u32[]{:S(2)}) collective-permute-start(bf16[2,96,768]{2,1,0:T(8,128)(2,1)S(1)} %pad_maximum_fusion.refs_0_), channel_id=1, source_target_pairs={{0,4},{1,5},{2,6},{3,7},{4,0},{5,1},{6,2},{7,3},{8,12},{9,13},{10,... | collective-permute-start | bytes 884744 | tf_op jit(solution)/shard_map/ppermute | solution.py:493
  25.5 14.2 %collective-permute-start.5 = (bf16[2,96,768]{2,1,0:T(8,128)(2,1)S(1)}, bf16[2,96,768]{2,1,0:T(8,128)(2,1)S(1)}, u32[]{:S(2)}, u32[]{:S(2)}) collective-permute-start(bf16[2,96,768]{2,1,0:T(8,128)(2,1)S(1)} %pad_maximum_fusion.refs_0_), channel_id=1, source_target_pairs={{0,2},{1,3},{2,0},{3,1},{4,6},{5,7},{6,4},{7,5},{8,10},{9,11},{10,... | collective-permute-start | bytes 884744 | tf_op jit(solution)/shard_map/ppermute | solution.py:493
  27.0 13.4 %collective-permute-start.9 = (bf16[2,96,768]{2,1,0:T(8,128)(2,1)S(1)}, bf16[2,96,768]{2,1,0:T(8,128)(2,1)S(1)}, u32[]{:S(2)}, u32[]{:S(2)}) collective-permute-start(bf16[2,96,768]{2,1,0:T(8,128)(2,1)S(1)} %pad_maximum_fusion.refs_0_), channel_id=1, source_target_pairs={{0,1},{1,0},{2,3},{3,2},{4,5},{5,4},{6,7},{7,6},{8,9},{9,8},{10,11... | collective-permute-start | bytes 884744 | tf_op jit(solution)/shard_map/ppermute | solution.py:493
  36.5 10.2 %collective-permute-start.6 = (bf16[2,96,768]{2,1,0:T(8,128)(2,1)S(1)}, bf16[2,96,768]{2,1,0:T(8,128)(2,1)S(1)}, u32[]{:S(2)}, u32[]{:S(2)}) collective-permute-start(bf16[2,96,768]{2,1,0:T(8,128)(2,1)S(1)} %collective-permute-done.2.refs_1_), channel_id=1, source_target_pairs={{0,2},{1,3},{2,0},{3,1},{4,6},{5,7},{6,4},{7,5},{8,10},{9,11},{10,... | collective-permute-start | bytes 884744 | tf_op jit(solution)/shard_map/ppermute | solution.py:493
  37.7 10.1 %collective-permute-start.4 = (bf16[2,96,768]{2,1,0:T(8,128)(2,1)S(1)}, bf16[2,96,768]{2,1,0:T(8,128)(2,1)S(1)}, u32[]{:S(2)}, u32[]{:S(2)}) collective-permute-start(bf16[2,96,768]{2,1,0:T(8,128)(2,1)S(1)} %collective-permute-done.2.refs_1_), channel_id=1, source_target_pairs={{0,4},{1,5},{2,6},{3,7},{4,0},{5,1},{6,2},{7,3},{8,12},{9,13},{10,... | collective-permute-start | bytes 884744 | tf_op jit(solution)/shard_map/ppermute | solution.py:493
  39.3 15.1 %collective-permute-start.7 = (bf16[2,96,768]{2,1,0:T(8,128)(2,1)S(1)}, bf16[2,96,768]{2,1,0:T(8,128)(2,1)S(1)}, u32[]{:S(2)}, u32[]{:S(2)}) collective-permute-start(bf16[2,96,768]{2,1,0:T(8,128)(2,1)S(1)} %collective-permute-done.3.refs_2_), channel_id=1, source_target_pairs={{0,2},{1,3},{2,0},{3,1},{4,6},{5,7},{6,4},{7,5},{8,10},{9,11},{10,... | collective-permute-start | bytes 884744 | tf_op jit(solution)/shard_map/ppermute | solution.py:493
  39.7 14.7 %collective-permute-start.10 = (bf16[2,96,768]{2,1,0:T(8,128)(2,1)S(1)}, bf16[2,96,768]{2,1,0:T(8,128)(2,1)S(1)}, u32[]{:S(2)}, u32[]{:S(2)}) collective-permute-start(bf16[2,96,768]{2,1,0:T(8,128)(2,1)S(1)} %collective-permute-done.2.refs_1_), channel_id=1, source_target_pairs={{0,1},{1,0},{2,3},{3,2},{4,5},{5,4},{6,7},{7,6},{8,9},{9,8},{10,11... | collective-permute-start | bytes 884744 | tf_op jit(solution)/shard_map/ppermute | solution.py:493
  40.4 14.5 %collective-permute-start.11 = (bf16[2,96,768]{2,1,0:T(8,128)(2,1)S(1)}, bf16[2,96,768]{2,1,0:T(8,128)(2,1)S(1)}, u32[]{:S(2)}, u32[]{:S(2)}) collective-permute-start(bf16[2,96,768]{2,1,0:T(8,128)(2,1)S(1)} %collective-permute-done.3.refs_2_), channel_id=1, source_target_pairs={{0,1},{1,0},{2,3},{3,2},{4,5},{5,4},{6,7},{7,6},{8,9},{9,8},{10,11... | collective-permute-start | bytes 884744 | tf_op jit(solution)/shard_map/ppermute | solution.py:493
  46.7 12.9 %collective-permute-start.8 = (bf16[2,96,768]{2,1,0:T(8,128)(2,1)S(1)}, bf16[2,96,768]{2,1,0:T(8,128)(2,1)S(1)}, u32[]{:S(2)}, u32[]{:S(2)}) collective-permute-start(bf16[2,96,768]{2,1,0:T(8,128)(2,1)S(1)} %collective-permute-done.6.refs_5_), channel_id=1, source_target_pairs={{0,4},{1,5},{2,6},{3,7},{4,0},{5,1},{6,2},{7,3},{8,12},{9,13},{10,... | collective-permute-start | bytes 884744 | tf_op jit(solution)/shard_map/ppermute | solution.py:493
  47.8 11.8 %collective-permute-start.13 = (bf16[2,96,768]{2,1,0:T(8,128)(2,1)S(1)}, bf16[2,96,768]{2,1,0:T(8,128)(2,1)S(1)}, u32[]{:S(2)}, u32[]{:S(2)}) collective-permute-start(bf16[2,96,768]{2,1,0:T(8,128)(2,1)S(1)} %collective-permute-done.5.refs_4_), channel_id=1, source_target_pairs={{0,1},{1,0},{2,3},{3,2},{4,5},{5,4},{6,7},{7,6},{8,9},{9,8},{10,11... | collective-permute-start | bytes 884744 | tf_op jit(solution)/shard_map/ppermute | solution.py:493
  59.6 32.8 %collective-permute-start.18 = (f32[768]{0:T(1024)S(1)}, f32[768]{0:T(1024)S(1)}, u32[]{:S(2)}, u32[]{:S(2)}) collective-permute-start(f32[768]{0:T(1024)S(1)} %copy-done.36), channel_id=1, source_target_pairs={{0,1},{1,0},{2,3},{3,2},{4,5},{5,4},{6,7},{7,6},{8,9},{9,8},{10,11... | collective-permute-start | bytes 9224 | tf_op jit(solution)/shard_map/ppermute | solution.py:493
  60.1 32.2 %collective-permute-start.17 = (f32[768]{0:T(1024)S(1)}, f32[768]{0:T(1024)S(1)}, u32[]{:S(2)}, u32[]{:S(2)}) collective-permute-start(f32[768]{0:T(1024)S(1)} %copy-done.36), channel_id=1, source_target_pairs={{0,2},{1,3},{2,0},{3,1},{4,6},{5,7},{6,4},{7,5},{8,10},{9,11},{10,... | collective-permute-start | bytes 9224 | tf_op jit(solution)/shard_map/ppermute | solution.py:493
  121.3 10.8 %collective-permute-start.20 = (bf16[2,8,192,768]{3,2,1,0:T(8,128)(2,1)S(1)}, bf16[2,8,192,768]{3,2,1,0:T(8,128)(2,1)S(1)}, u32[]{:S(2)}, u32[]{:S(2)}) collective-permute-start(bf16[2,8,192,768]{3,2,1,0:T(8,128)(2,1)S(1)} %get-tuple-element.81), channel_id=1, source_target_pairs={{0,1},{1,0},{2,3},{3,2},{4,5},{5,4},{6,7},{7,6},{8,9},{9,8},{10,11... | collective-permute-start | bytes 14155784 | tf_op jit(solution)/shard_map/ppermute | solution.py:493
  134.8 28.2 %collective-permute-start.23 = (bf16[2,2,192,768]{3,2,1,0:T(8,128)(2,1)S(1)}, bf16[2,2,192,768]{3,2,1,0:T(8,128)(2,1)S(1)}, u32[]{:S(2)}, u32[]{:S(2)}) collective-permute-start(bf16[2,2,192,768]{3,2,1,0:T(8,128)(2,1)S(1)} %get-tuple-element.84), channel_id=1, source_target_pairs={{0,2},{1,3},{2,0},{3,1},{4,6},{5,7},{6,4},{7,5},{8,10},{9,11},{10,... | collective-permute-start | bytes 3538952 | tf_op jit(solution)/shard_map/ppermute | solution.py:493
  136.2 27.9 %collective-permute-start.22 = (bf16[2,2,192,768]{3,2,1,0:T(8,128)(2,1)S(1)}, bf16[2,2,192,768]{3,2,1,0:T(8,128)(2,1)S(1)}, u32[]{:S(2)}, u32[]{:S(2)}) collective-permute-start(bf16[2,2,192,768]{3,2,1,0:T(8,128)(2,1)S(1)} %get-tuple-element.83), channel_id=1, source_target_pairs={{0,4},{1,5},{2,6},{3,7},{4,0},{5,1},{6,2},{7,3},{8,12},{9,13},{10,... | collective-permute-start | bytes 3538952 | tf_op jit(solution)/shard_map/ppermute | solution.py:493
  152.7 11.7 %collective-permute-start.25 = (bf16[1,8,96,768]{3,2,1,0:T(8,128)(2,1)S(1)}, bf16[1,8,96,768]{3,2,1,0:T(8,128)(2,1)S(1)}, u32[]{:S(2)}, u32[]{:S(2)}) collective-permute-start(bf16[1,8,96,768]{3,2,1,0:T(8,128)(2,1)S(1)} %get-tuple-element.97), channel_id=1, source_target_pairs={{0,1},{1,0},{2,3},{3,2},{4,5},{5,4},{6,7},{7,6},{8,9},{9,8},{10,11... | collective-permute-start | bytes 3538952 | tf_op jit(solution)/shard_map/ppermute | solution.py:493
  152.8 11.6 %collective-permute-start.24 = (bf16[1,8,96,768]{3,2,1,0:T(8,128)(2,1)S(1)}, bf16[1,8,96,768]{3,2,1,0:T(8,128)(2,1)S(1)}, u32[]{:S(2)}, u32[]{:S(2)}) collective-permute-start(bf16[1,8,96,768]{3,2,1,0:T(8,128)(2,1)S(1)} %get-tuple-element.95), channel_id=1, source_target_pairs={{0,1},{1,0},{2,3},{3,2},{4,5},{5,4},{6,7},{7,6},{8,9},{9,8},{10,11... | collective-permute-start | bytes 3538952 | tf_op jit(solution)/shard_map/ppermute | solution.py:493
  165.9 16.4 %collective-permute-start.27 = (bf16[2,2,96,768]{3,2,1,0:T(8,128)(2,1)S(1)}, bf16[2,2,96,768]{3,2,1,0:T(8,128)(2,1)S(1)}, u32[]{:S(2)}, u32[]{:S(2)}) collective-permute-start(bf16[2,2,96,768]{3,2,1,0:T(8,128)(2,1)S(1)} %get-tuple-element.100), channel_id=1, source_target_pairs={{0,2},{1,3},{2,0},{3,1},{4,6},{5,7},{6,4},{7,5},{8,10},{9,11},{10,... | collective-permute-start | bytes 1769480 | tf_op jit(solution)/shard_map/ppermute | solution.py:493
  166.6 16.3 %collective-permute-start.26 = (bf16[2,2,96,768]{3,2,1,0:T(8,128)(2,1)S(1)}, bf16[2,2,96,768]{3,2,1,0:T(8,128)(2,1)S(1)}, u32[]{:S(2)}, u32[]{:S(2)}) collective-permute-start(bf16[2,2,96,768]{3,2,1,0:T(8,128)(2,1)S(1)} %get-tuple-element.99), channel_id=1, source_target_pairs={{0,4},{1,5},{2,6},{3,7},{4,0},{5,1},{6,2},{7,3},{8,12},{9,13},{10,... | collective-permute-start | bytes 1769480 | tf_op jit(solution)/shard_map/ppermute | solution.py:493
  167.9 27.6 %collective-permute-start.31 = (bf16[2,192,768]{2,1,0:T(8,128)(2,1)S(1)}, bf16[2,192,768]{2,1,0:T(8,128)(2,1)S(1)}, u32[]{:S(2)}, u32[]{:S(2)}) collective-permute-start(bf16[2,192,768]{2,1,0:T(8,128)(2,1)S(1)} %fusion.2), channel_id=1, source_target_pairs={{0,4},{1,5},{2,6},{3,7},{4,0},{5,1},{6,2},{7,3},{8,12},{9,13},{10,... | collective-permute-start | bytes 1769480 | tf_op jit(solution)/shard_map/ppermute | solution.py:493
  186.2 16.4 %collective-permute-start.35 = (bf16[2,192,768]{2,1,0:T(8,128)(2,1)S(1)}, bf16[2,192,768]{2,1,0:T(8,128)(2,1)S(1)}, u32[]{:S(2)}, u32[]{:S(2)}) collective-permute-start(bf16[2,192,768]{2,1,0:T(8,128)(2,1)S(1)} %fusion.1), channel_id=1, source_target_pairs={{0,2},{1,3},{2,0},{3,1},{4,6},{5,7},{6,4},{7,5},{8,10},{9,11},{10,... | collective-permute-start | bytes 1769480 | tf_op jit(solution)/shard_map/ppermute | solution.py:493
  187.7 11.9 %collective-permute-start.30 = (bf16[2,96,768]{2,1,0:T(8,128)(2,1)S(1)}, bf16[2,96,768]{2,1,0:T(8,128)(2,1)S(1)}, u32[]{:S(2)}, u32[]{:S(2)}) collective-permute-start(bf16[2,96,768]{2,1,0:T(8,128)(2,1)S(1)} %fusion.7), channel_id=1, source_target_pairs={{0,4},{1,5},{2,6},{3,7},{4,0},{5,1},{6,2},{7,3},{8,12},{9,13},{10,... | collective-permute-start | bytes 884744 | tf_op jit(solution)/shard_map/ppermute | solution.py:493
  195.7 14.2 %collective-permute-start.36 = (bf16[2,192,768]{2,1,0:T(8,128)(2,1)S(1)}, bf16[2,192,768]{2,1,0:T(8,128)(2,1)S(1)}, u32[]{:S(2)}, u32[]{:S(2)}) collective-permute-start(bf16[2,192,768]{2,1,0:T(8,128)(2,1)S(1)} %fusion), channel_id=1, source_target_pairs={{0,8},{1,9},{2,10},{3,11},{4,12},{5,13},{6,14},{7,15},{8,0},{9,1},... | collective-permute-start | bytes 1769480 | tf_op jit(solution)/shard_map/ppermute | solution.py:493
  197.1 10.4 %collective-permute-start.33 = (bf16[2,96,768]{2,1,0:T(8,128)(2,1)S(1)}, bf16[2,96,768]{2,1,0:T(8,128)(2,1)S(1)}, u32[]{:S(2)}, u32[]{:S(2)}) collective-permute-start(bf16[2,96,768]{2,1,0:T(8,128)(2,1)S(1)} %fusion.6), channel_id=1, source_target_pairs={{0,2},{1,3},{2,0},{3,1},{4,6},{5,7},{6,4},{7,5},{8,10},{9,11},{10,... | collective-permute-start | bytes 884744 | tf_op jit(solution)/shard_map/ppermute | solution.py:493
  199.7 7.9 %collective-permute-start.32 = (f32[16,768]{1,0:T(8,128)S(1)}, f32[16,768]{1,0:T(8,128)S(1)}, u32[]{:S(2)}, u32[]{:S(2)}) collective-permute-start(f32[16,768]{1,0:T(8,128)S(1)} %add.131), channel_id=1, source_target_pairs={{0,4},{1,5},{2,6},{3,7},{4,0},{5,1},{6,2},{7,3},{8,12},{9,13},{10,... | collective-permute-start | bytes 147464 | tf_op jit(solution)/shard_map/ppermute | solution.py:493
  201.1 11.9 %collective-permute-start.34 = (bf16[2,96,768]{2,1,0:T(8,128)(2,1)S(1)}, bf16[2,96,768]{2,1,0:T(8,128)(2,1)S(1)}, u32[]{:S(2)}, u32[]{:S(2)}) collective-permute-start(bf16[2,96,768]{2,1,0:T(8,128)(2,1)S(1)} %fusion.5), channel_id=1, source_target_pairs={{0,8},{1,9},{2,10},{3,11},{4,12},{5,13},{6,14},{7,15},{8,0},{9,1},... | collective-permute-start | bytes 884744 | tf_op jit(solution)/shard_map/ppermute | solution.py:493
  218.9 12.4 %collective-permute-start.39 = (bf16[96,768]{1,0:T(8,128)(2,1)S(1)}, bf16[96,768]{1,0:T(8,128)(2,1)S(1)}, u32[]{:S(2)}, u32[]{:S(2)}) collective-permute-start(bf16[96,768]{1,0:T(8,128)(2,1)S(1)} %fusion.9), channel_id=1, source_target_pairs={{0,16},{1,17},{2,18},{3,19},{4,20},{5,21},{6,22},{7,23},{8,24},{9,... | collective-permute-start | bytes 442376 | tf_op jit(solution)/shard_map/ppermute | solution.py:493
  219.9 15.1 %collective-permute-start.40 = (bf16[192,768]{1,0:T(8,128)(2,1)S(1)}, bf16[192,768]{1,0:T(8,128)(2,1)S(1)}, u32[]{:S(2)}, u32[]{:S(2)}) collective-permute-start(bf16[192,768]{1,0:T(8,128)(2,1)S(1)} %fusion.4), channel_id=1, source_target_pairs={{0,16},{1,17},{2,18},{3,19},{4,20},{5,21},{6,22},{7,23},{8,24},{9,... | collective-permute-start | bytes 884744 | tf_op jit(solution)/shard_map/ppermute | solution.py:493
  (49 other events, 558.3 us)
Sparse Core Ops, SparseCore 0:
  11.6 94.9 all-gather.2

commit v4 on v3

--- a/solution.py
+++ b/solution.py
@@ -593,7 +593,7 @@
 
     def step(self, *wait, own=None):
         swap = self.swap
-        got = tuple(after(f, *wait) for f in self.flight)
+        got = lax.optimization_barrier(self.flight + wait)[: len(self.flight)]
         self.state += 1
         if self.state == 1:
             self.a, send_a, self.b, send_b = merge(own, *got)
@@ -768,13 +768,13 @@
             small = after(small, *wait)
             return small + swap(small, bit)
 
-        wait = sa.step(small)
-        small = reduced(reduced(small, CORE, *wait), FAR_Z)
-        wait = sm.step(small)
-        small = reduced(small, LINE_X, *sa.step(small, *wait))
-        wait = sm.step(small)
-        small = reduced(reduced(small, LINE_Y, *sa.step(small, *wait)), NEAR_Z)
-        sm.step(), sa.step()
+        near = sm.step(small)
+        small = reduced(reduced(small, CORE), LINE_X, *near)
+        small = reduced(small, FAR_Z, *sa.step(small))
+        far = sm.step()
+        small = reduced(small, NEAR_Z, *sa.step(small, *far))
+        small = reduced(small, LINE_Y, *sa.step(small, *sm.step()))
+        sa.step()
         grad_a, grad_u, grad_d = sa.result, sm.result[:rows], sm.result[rows:]
     else:
 

time: 244 us -> 239 us (0.980)
  waiting for transfers between devices: 86.4 us -> 76.3 us
    ppermute x41, waiting for transfers between devices: 73.3 us -> 61.8 us  [swap(): lax.ppermute(value, ('wide', 'narrow'), [(i, i ^ bit) for i in range(devi...]
    unnamed x79 -> x87, local copies, waits for them, and re-layouts: 17.8 us -> 19.9 us
  transfers between devices with their start and end apart: 42 -> 42, of which waited for: 22 -> 19; matrix products, arithmetic and copies ran while one was open for 3% -> 3% of each run, Pallas kernels for 28% -> 30%
where the time goes in v4:
time: 239 us; the launch traced here: 238 us
  Pallas kernels  79.3 us (33%)
  waiting for transfers between devices  76.3 us (32%)
  starting transfers between devices  36.8 us (15%)
  local copies, waits for them, and re-layouts  22.2 us (9%)
  between operations  14.6 us (6%)
  other arithmetic  8.83 us (4%)
    pallas_call x6, Pallas kernels, call(): pl.pallas_call(kernel, grid_spec=pltpu.PrefetchScalarGridSpec(num_scalar_...  73.4 us
    ppermute x41, waiting for transfers between devices, swap(): lax.ppermute(value, ('wide', 'narrow'), [(i, i ^ bit) for i in range(devi...  61.8 us
    ppermute x41, starting transfers between devices, swap(): lax.ppermute(value, ('wide', 'narrow'), [(i, i ^ bit) for i in range(devi...  36.7 us
    unnamed x87, local copies, waits for them, and re-layouts  19.9 us
    all_gather x1, waiting for transfers between devices, body(): full = lax.all_gather(mlp, ('wide', 'narrow'), axis=0, tiled=False)  14.5 us
    pallas_call x2, Pallas kernels, merge(): pl.pallas_call(merge_kernel, grid=(2, 4), in_specs=[taken] + gots, out_sp...  5.65 us
  transfers between devices with their start and end apart: 42, of which 19 were waited for; matrix products, arithmetic and copies ran while one was open for 3% of the time, Pallas kernels for 30%

profile of v4, /device:TPU:0, one launch (start us, length us, event | category | flops | bytes accessed | tf_op | source)
XLA Modules:
  0.0 238.1 jit_solution(15434489475312990268)
XLA Ops:
  7.3 1.7 pad_maximum_fusion.1
  11.0 3.7 %collective-permute-start.1 = (bf16[96,768]{1,0:T(8,128)(2,1)S(1)}, bf16[96,768]{1,0:T(8,128)(2,1)S(1)}, u32[]{:S(2)}, u32[]{:S(2)}) collective-permute-start(bf16[96,768]{1,0:T(8,128)(2,1)S(1)} %shard_map.255), channel_id=1, source_target_pairs={{0,16},{1,17},{2,18},{3,19},{4,20},{5,21},{6,22},{7,23},{8,24},{9,... | collective-permute-start | bytes 442376 | tf_op jit(solution)/shard_map/ppermute | solution.py:493
  14.7 7.6 %collective-permute-done.1 = bf16[96,768]{1,0:T(8,128)(2,1)S(1)} collective-permute-done((bf16[96,768]{1,0:T(8,128)(2,1)S(1)}, bf16[96,768]{1,0:T(8,128)(2,1)S(1)}, u32[]{:S(2)}, u32[]{:S(2)}) %collective-permute-start.1) | collective-permute-done | bytes 147488 | tf_op jit(solution)/shard_map/ppermute | solution.py:493
  25.5 1.5 collective-permute-start.5
  30.0 1.6 shard_map.254
  33.7 2.9 %collective-permute-done.2.refs_1_ = bf16[2,96,768]{2,1,0:T(8,128)(2,1)} collective-permute-done((bf16[2,96,768]{2,1,0:T(8,128)(2,1)S(1)}, bf16[2,96,768]{2,1,0:T(8,128)(2,1)}, u32[]{:S(2)}, u32[]{:S(2)}) %collective-permute-start.2) | collective-permute-done | bytes 294944 | tf_op jit(solution)/shard_map/ppermute | solution.py:493
  37.8 1.5 collective-permute-start.4
  40.3 7.0 %collective-permute-done.6.refs_5_ = bf16[2,96,768]{2,1,0:T(8,128)(2,1)S(1)} collective-permute-done((bf16[2,96,768]{2,1,0:T(8,128)(2,1)}, bf16[2,96,768]{2,1,0:T(8,128)(2,1)S(1)}, u32[]{:S(2)}, u32[]{:S(2)}) %collective-permute-start.6) | collective-permute-done | bytes 294944 | tf_op jit(solution)/shard_map/ppermute | solution.py:493
  48.4 6.3 %collective-permute-done.7.refs_6_ = bf16[2,96,768]{2,1,0:T(8,128)(2,1)S(1)} collective-permute-done((bf16[2,96,768]{2,1,0:T(8,128)(2,1)S(1)}, bf16[2,96,768]{2,1,0:T(8,128)(2,1)S(1)}, u32[]{:S(2)}, u32[]{:S(2)}) %collective-permute-start.7) | collective-permute-done | bytes 294944 | tf_op jit(solution)/shard_map/ppermute | solution.py:493
  55.3 4.5 %collective-permute-done.8.refs_7_ = bf16[2,96,768]{2,1,0:T(8,128)(2,1)S(1)} collective-permute-done((bf16[2,96,768]{2,1,0:T(8,128)(2,1)S(1)}, bf16[2,96,768]{2,1,0:T(8,128)(2,1)S(1)}, u32[]{:S(2)}, u32[]{:S(2)}) %collective-permute-start.8) | collective-permute-done | bytes 294944 | tf_op jit(solution)/shard_map/ppermute | solution.py:493
  61.4 23.5 %shard_map.256 = (bf16[4,624,768]{2,1,0:T(8,128)(2,1)S(1)}, bf16[4,512,256]{2,1,0:T(8,128)(2,1)S(1)}, bf16[4,768,768]{2,1,0:T(8,128)(2,1)S(1)}, f32[512,768]{1,0:T(8,128)S(1)}, bf16[512,768]{1,0:T(8,128)(2,1)S(1)}) custom-call(s32[10]{0:T(128)S(1)} %pad_add_fusion.info_ref, bf16[624,768]{1,0:T(8,128)(2,1)S(1)} %get-tuple-element.69.h_ref, ...), custom_call_target="tpu_custom_call" | custom-call | flops 4831838208 | bytes 14548992 | tf_op jit(solution)/shard_map/pallas_call | solution.py:471
  84.9 2.2 copy-done.2
  88.0 1.9 copy-done.25
  92.1 14.5 %all-gather.3.cloned.1.call-done = bf16[6144,768]{1,0:T(8,128)(2,1)} async-done(((bf16[192,768]{1,0:T(8,128)(2,1)}), bf16[6144,768]{1,0:T(8,128)(2,1)}) %all-gather.3.cloned.1.call-update) | async-done | bytes 9437200 | tf_op jit(solution)/shard_map/all_gather | solution.py:663
  106.6 3.7 %copy-done = bf16[6144,768]{1,0:T(8,128)(2,1)S(1)} copy-done((bf16[6144,768]{1,0:T(8,128)(2,1)S(1)}, bf16[6144,768]{1,0:T(8,128)(2,1)}, u32[]{:S(2)}) %copy-start) | copy-done | bytes 9437208
  112.6 8.8 %shard_map.257 = (bf16[2,512,768]{2,1,0:T(8,128)(2,1)S(1)}, bf16[2,8,192,768]{3,2,1,0:T(8,128)(2,1)S(1)}, f32[2,1,768]{2,1,0:T(1,128)S(1)}, f32[512,768]{1,0:T(8,128)S(1)}) custom-call(s32[10]{0:T(128)S(1)} %pad_add_fusion.info_ref, bf16[512,768]{1,0:T(8,128)(2,1)S(1)} %copy-done.14, bf16[512,768]{1,0:T(8,128)(2,1)S(1)} %copy-done.11, ...), custom_call_target="tpu_custom_call" | custom-call | flops 6039797760 | bytes 40919040 | tf_op jit(solution)/shard_map/pallas_call | solution.py:471
  121.7 10.1 %shard_map.258 = (bf16[2,512,768]{2,1,0:T(8,128)(2,1)S(1)}, bf16[2,8,192,768]{3,2,1,0:T(8,128)(2,1)S(1)}, f32[2,1,768]{2,1,0:T(1,128)S(1)}, f32[512,768]{1,0:T(8...) custom-call(s32[10]{0:T(128)S(1)} %pad_add_fusion.info_ref, bf16[512,768]{1,0:T(8,128)(2,1)S(1)} %copy-done.14, ...), custom_call_target="tpu_custom_call" | custom-call | flops 6039797760 | bytes 50405376 | tf_op jit(solution)/shard_map/pallas_call | solution.py:471
  132.2 4.2 %shard_map.259 = (bf16[2,2,192,768]{3,2,1,0:T(8,128)(2,1)S(1)}, bf16[2,2,192,768]{3,2,1,0:T(8,128)(2,1)}, bf16[2,2,192,768]{3,2,1,0:T(8,128)(2,1)S(1)}, bf16[2,2,192,768]{3,2,1,0:T(8,128)(2,1)}) custom-call(bf16[2,8,192,768]{3,2,1,0:T(8,128)(2,1)S(1)} %get-tuple-element.80.own_ref, bf16[2,8,192,768]{3,2,1,0:T(8,128)(2,1)S(1)} %collective-permute-done.20.refs_0_), custom_call_target="tpu_custom_call" | custom-call | bytes 14155776 | tf_op jit(solution)/shard_map/pallas_call | solution.py:571
  138.5 2.1 copy-done.26
  140.6 15.8 %shard_map.260 = (bf16[2,8,96,768]{3,2,1,0:T(8,128)(2,1)S(1)}, bf16[1,8,96,768]{3,2,1,0:T(8,128)(2,1)S(1)}, bf16[1,8,96,768]{3,2,1,0:T(8,128)(2,1)S(1)}, bf16[4,512,768]{2,1,0:T(8,128)(2,1)S(1)}) custom-call(s32[10]{0:T(128)S(1)} %pad_add_fusion.info_ref, bf16[512,768]{1,0:T(8,128)(2,1)S(1)} %get-tuple-element.85.dz_ref, ...), custom_call_target="tpu_custom_call" | custom-call | flops 9663676416 | bytes 23035904 | tf_op jit(solution)/shard_map/pallas_call | solution.py:471
  157.0 7.8 %collective-permute-done.22 = bf16[2,2,192,768]{3,2,1,0:T(8,128)(2,1)S(1)} collective-permute-done((bf16[2,2,192,768]{3,2,1,0:T(8,128)(2,1)}, bf16[2,2,192,768]{3,2,1,0:T(8,128)(2,1)S(1)}, u32[]{:S(2)}, u32[]{:S(2)}) %collective-permute-start.22) | collective-permute-done | bytes 1179680 | tf_op jit(solution)/shard_map/ppermute | solution.py:493
  166.9 1.6 collective-permute-start.27
  171.9 13.6 %shard_map.262 = (f32[490,768]{1,0:T(8,128)}, f32[490,768]{1,0:T(8,128)}, f32[16,768]{1,0:T(8,128)S(1)}) custom-call(s32[10]{0:T(128)S(1)} %pad_add_fusion.info_ref, bf16[4,512,768]{2,1,0:T(8,128)(2,1)S(1)} %get-tuple-element.101.dq_ref, bf16[4,768,768]{2,1,0:T(8,128)(2,1)S(1)} %bitcast.70, bf16[2,512,768]{2,1,0:T(8,128)(2,1)S(1)} %get-tuple-element.102.actm_ref, ...), custom_call_target="tpu_custom_call" | custom-call | flops 4831838208 | bytes 50454528 | tf_op jit(solution)/shard_map/pallas_call | solution.py:471
  189.1 5.1 %collective-permute-done.29 = f32[16,768]{1,0:T(8,128)S(1)} collective-permute-done((f32[16,768]{1,0:T(8,128)S(1)}, f32[16,768]{1,0:T(8,128)S(1)}, u32[]{:S(2)}, u32[]{:S(2)}) %collective-permute-start.29) | collective-permute-done | bytes 49184 | tf_op jit(solution)/shard_map/ppermute | solution.py:493
  194.4 2.0 collective-permute-start.32
  198.5 4.3 %collective-permute-done.32 = f32[16,768]{1,0:T(8,128)S(1)} collective-permute-done((f32[16,768]{1,0:T(8,128)S(1)}, f32[16,768]{1,0:T(8,128)S(1)}, u32[]{:S(2)}, u32[]{:S(2)}) %collective-permute-start.32) | collective-permute-done | bytes 49184 | tf_op jit(solution)/shard_map/ppermute | solution.py:493
  204.0 3.1 %collective-permute-start.38 = (bf16[192,768]{1,0:T(8,128)(2,1)S(1)}, bf16[192,768]{1,0:T(8,128)(2,1)S(1)}, u32[]{:S(2)}, u32[]{:S(2)}) collective-permute-start(bf16[192,768]{1,0:T(8,128)(2,1)S(1)} %fusion.4), channel_id=1, source_target_pairs={{0,16},{1,17},{2,18},{3,19},{4,20},{5,21},{6,22},{7,23},{8,24},{9,... | collective-permute-start | bytes 884744 | tf_op jit(solution)/shard_map/ppermute | solution.py:493
  208.0 2.0 collective-permute-start.37
  210.0 5.8 %collective-permute-done.36 = f32[16,768]{1,0:T(8,128)} collective-permute-done((f32[16,768]{1,0:T(8,128)}, f32[16,768]{1,0:T(8,128)}, u32[]{:S(2)}, u32[]{:S(2)}) %collective-permute-start.36) | collective-permute-done | bytes 49184 | tf_op jit(solution)/shard_map/ppermute | solution.py:493
  216.6 2.9 %collective-permute-done.38 = bf16[192,768]{1,0:T(8,128)(2,1)S(1)} collective-permute-done((bf16[192,768]{1,0:T(8,128)(2,1)S(1)}, bf16[192,768]{1,0:T(8,128)(2,1)S(1)}, u32[]{:S(2)}, u32[]{:S(2)}) %collective-permute-start.38) | collective-permute-done | bytes 294944 | tf_op jit(solution)/shard_map/ppermute | solution.py:493
  221.2 1.5 collective-permute-start.40
  225.1 1.8 collective-permute-done.39
  (192 shorter events, 47.0 us)
Async XLA Ops:
  7.2 99.4 %all-gather.3.cloned.1.call-start = ((), (), s32[]{:S(2)}) async-start(), calls=%async_computation | async-start | bytes 9732096 | tf_op jit(solution)/shard_map/all_gather | solution.py:663
  10.2 16.9 %collective-permute-start = (bf16[98,768]{1,0:T(8,128)(2,1)S(1)}, bf16[98,768]{1,0:T(8,128)(2,1)S(1)}, u32[]{:S(2)}, u32[]{:S(2)}) collective-permute-start(bf16[98,768]{1,0:T(8,128)(2,1)S(1)} %slice_select_fusion), channel_id=1, source_target_pairs={{0,1},{1,0},{2,3},{3,2},{4,5},{5,4},{6,7},{7,6},{8,9},{9,8},{10,11... | collective-permute-start | bytes 451592 | tf_op jit(solution)/shard_map/ppermute | solution.py:493
  11.0 11.3 %collective-permute-start.1 = (bf16[96,768]{1,0:T(8,128)(2,1)S(1)}, bf16[96,768]{1,0:T(8,128)(2,1)S(1)}, u32[]{:S(2)}, u32[]{:S(2)}) collective-permute-start(bf16[96,768]{1,0:T(8,128)(2,1)S(1)} %shard_map.255), channel_id=1, source_target_pairs={{0,16},{1,17},{2,18},{3,19},{4,20},{5,21},{6,22},{7,23},{8,24},{9,... | collective-permute-start | bytes 442376 | tf_op jit(solution)/shard_map/ppermute | solution.py:493
  22.3 14.2 %collective-permute-start.2 = (bf16[2,96,768]{2,1,0:T(8,128)(2,1)S(1)}, bf16[2,96,768]{2,1,0:T(8,128)(2,1)}, u32[]{:S(2)}, u32[]{:S(2)}) collective-permute-start(bf16[2,96,768]{2,1,0:T(8,128)(2,1)S(1)} %pad_maximum_fusion.refs_0_), channel_id=1, source_target_pairs={{0,8},{1,9},{2,10},{3,11},{4,12},{5,13},{6,14},{7,15},{8,0},{9,1},... | collective-permute-start | bytes 884744 | tf_op jit(solution)/shard_map/ppermute | solution.py:493
  24.0 15.3 %collective-permute-start.3 = (bf16[2,96,768]{2,1,0:T(8,128)(2,1)S(1)}, bf16[2,96,768]{2,1,0:T(8,128)(2,1)S(1)}, u32[]{:S(2)}, u32[]{:S(2)}) collective-permute-start(bf16[2,96,768]{2,1,0:T(8,128)(2,1)S(1)} %pad_maximum_fusion.refs_0_), channel_id=1, source_target_pairs={{0,4},{1,5},{2,6},{3,7},{4,0},{5,1},{6,2},{7,3},{8,12},{9,13},{10,... | collective-permute-start | bytes 884744 | tf_op jit(solution)/shard_map/ppermute | solution.py:493
  25.5 14.3 %collective-permute-start.5 = (bf16[2,96,768]{2,1,0:T(8,128)(2,1)S(1)}, bf16[2,96,768]{2,1,0:T(8,128)(2,1)S(1)}, u32[]{:S(2)}, u32[]{:S(2)}) collective-permute-start(bf16[2,96,768]{2,1,0:T(8,128)(2,1)S(1)} %pad_maximum_fusion.refs_0_), channel_id=1, source_target_pairs={{0,2},{1,3},{2,0},{3,1},{4,6},{5,7},{6,4},{7,5},{8,10},{9,11},{10,... | collective-permute-start | bytes 884744 | tf_op jit(solution)/shard_map/ppermute | solution.py:493
  27.0 12.8 %collective-permute-start.9 = (bf16[2,96,768]{2,1,0:T(8,128)(2,1)S(1)}, bf16[2,96,768]{2,1,0:T(8,128)(2,1)S(1)}, u32[]{:S(2)}, u32[]{:S(2)}) collective-permute-start(bf16[2,96,768]{2,1,0:T(8,128)(2,1)S(1)} %pad_maximum_fusion.refs_0_), channel_id=1, source_target_pairs={{0,1},{1,0},{2,3},{3,2},{4,5},{5,4},{6,7},{7,6},{8,9},{9,8},{10,11... | collective-permute-start | bytes 884744 | tf_op jit(solution)/shard_map/ppermute | solution.py:493
  36.6 10.8 %collective-permute-start.6 = (bf16[2,96,768]{2,1,0:T(8,128)(2,1)}, bf16[2,96,768]{2,1,0:T(8,128)(2,1)S(1)}, u32[]{:S(2)}, u32[]{:S(2)}) collective-permute-start(bf16[2,96,768]{2,1,0:T(8,128)(2,1)} %collective-permute-done.2.refs_1_), channel_id=1, source_target_pairs={{0,2},{1,3},{2,0},{3,1},{4,6},{5,7},{6,4},{7,5},{8,10},{9,11},{10,... | collective-permute-start | bytes 884744 | tf_op jit(solution)/shard_map/ppermute | solution.py:493
  37.8 10.6 %collective-permute-start.4 = (bf16[2,96,768]{2,1,0:T(8,128)(2,1)}, bf16[2,96,768]{2,1,0:T(8,128)(2,1)S(1)}, u32[]{:S(2)}, u32[]{:S(2)}) collective-permute-start(bf16[2,96,768]{2,1,0:T(8,128)(2,1)} %collective-permute-done.2.refs_1_), channel_id=1, source_target_pairs={{0,4},{1,5},{2,6},{3,7},{4,0},{5,1},{6,2},{7,3},{8,12},{9,13},{10,... | collective-permute-start | bytes 884744 | tf_op jit(solution)/shard_map/ppermute | solution.py:493
  39.3 15.4 %collective-permute-start.7 = (bf16[2,96,768]{2,1,0:T(8,128)(2,1)S(1)}, bf16[2,96,768]{2,1,0:T(8,128)(2,1)S(1)}, u32[]{:S(2)}, u32[]{:S(2)}) collective-permute-start(bf16[2,96,768]{2,1,0:T(8,128)(2,1)S(1)} %collective-permute-done.3.refs_2_), channel_id=1, source_target_pairs={{0,2},{1,3},{2,0},{3,1},{4,6},{5,7},{6,4},{7,5},{8,10},{9,11},{10,... | collective-permute-start | bytes 884744 | tf_op jit(solution)/shard_map/ppermute | solution.py:493
  39.8 14.9 %collective-permute-start.10 = (bf16[2,96,768]{2,1,0:T(8,128)(2,1)}, bf16[2,96,768]{2,1,0:T(8,128)(2,1)S(1)}, u32[]{:S(2)}, u32[]{:S(2)}) collective-permute-start(bf16[2,96,768]{2,1,0:T(8,128)(2,1)} %collective-permute-done.2.refs_1_), channel_id=1, source_target_pairs={{0,1},{1,0},{2,3},{3,2},{4,5},{5,4},{6,7},{7,6},{8,9},{9,8},{10,11... | collective-permute-start | bytes 884744 | tf_op jit(solution)/shard_map/ppermute | solution.py:493
  39.8 15.4 %collective-permute-start.11 = (bf16[2,96,768]{2,1,0:T(8,128)(2,1)S(1)}, bf16[2,96,768]{2,1,0:T(8,128)(2,1)S(1)}, u32[]{:S(2)}, u32[]{:S(2)}) collective-permute-start(bf16[2,96,768]{2,1,0:T(8,128)(2,1)S(1)} %collective-permute-done.3.refs_2_), channel_id=1, source_target_pairs={{0,1},{1,0},{2,3},{3,2},{4,5},{5,4},{6,7},{7,6},{8,9},{9,8},{10,11... | collective-permute-start | bytes 884744 | tf_op jit(solution)/shard_map/ppermute | solution.py:493
  47.3 12.5 %collective-permute-start.8 = (bf16[2,96,768]{2,1,0:T(8,128)(2,1)S(1)}, bf16[2,96,768]{2,1,0:T(8,128)(2,1)S(1)}, u32[]{:S(2)}, u32[]{:S(2)}) collective-permute-start(bf16[2,96,768]{2,1,0:T(8,128)(2,1)S(1)} %collective-permute-done.6.refs_5_), channel_id=1, source_target_pairs={{0,4},{1,5},{2,6},{3,7},{4,0},{5,1},{6,2},{7,3},{8,12},{9,13},{10,... | collective-permute-start | bytes 884744 | tf_op jit(solution)/shard_map/ppermute | solution.py:493
  48.4 11.4 %collective-permute-start.13 = (bf16[2,96,768]{2,1,0:T(8,128)(2,1)S(1)}, bf16[2,96,768]{2,1,0:T(8,128)(2,1)S(1)}, u32[]{:S(2)}, u32[]{:S(2)}) collective-permute-start(bf16[2,96,768]{2,1,0:T(8,128)(2,1)S(1)} %collective-permute-done.5.refs_4_), channel_id=1, source_target_pairs={{0,1},{1,0},{2,3},{3,2},{4,5},{5,4},{6,7},{7,6},{8,9},{9,8},{10,11... | collective-permute-start | bytes 884744 | tf_op jit(solution)/shard_map/ppermute | solution.py:493
  59.8 31.2 %collective-permute-start.18 = (f32[768]{0:T(1024)S(1)}, f32[768]{0:T(1024)S(1)}, u32[]{:S(2)}, u32[]{:S(2)}) collective-permute-start(f32[768]{0:T(1024)S(1)} %copy-done.40), channel_id=1, source_target_pairs={{0,1},{1,0},{2,3},{3,2},{4,5},{5,4},{6,7},{7,6},{8,9},{9,8},{10,11... | collective-permute-start | bytes 9224 | tf_op jit(solution)/shard_map/ppermute | solution.py:493
  60.3 30.6 %collective-permute-start.17 = (f32[768]{0:T(1024)S(1)}, f32[768]{0:T(1024)S(1)}, u32[]{:S(2)}, u32[]{:S(2)}) collective-permute-start(f32[768]{0:T(1024)S(1)} %copy-done.40), channel_id=1, source_target_pairs={{0,2},{1,3},{2,0},{3,1},{4,6},{5,7},{6,4},{7,5},{8,10},{9,11},{10,... | collective-permute-start | bytes 9224 | tf_op jit(solution)/shard_map/ppermute | solution.py:493
  121.3 10.8 %collective-permute-start.20 = (bf16[2,8,192,768]{3,2,1,0:T(8,128)(2,1)S(1)}, bf16[2,8,192,768]{3,2,1,0:T(8,128)(2,1)S(1)}, u32[]{:S(2)}, u32[]{:S(2)}) collective-permute-start(bf16[2,8,192,768]{3,2,1,0:T(8,128)(2,1)S(1)} %get-tuple-element.81), channel_id=1, source_target_pairs={{0,1},{1,0},{2,3},{3,2},{4,5},{5,4},{6,7},{7,6},{8,9},{9,8},{10,11... | collective-permute-start | bytes 14155784 | tf_op jit(solution)/shard_map/ppermute | solution.py:493
  136.4 28.3 %collective-permute-start.22 = (bf16[2,2,192,768]{3,2,1,0:T(8,128)(2,1)}, bf16[2,2,192,768]{3,2,1,0:T(8,128)(2,1)S(1)}, u32[]{:S(2)}, u32[]{:S(2)}) collective-permute-start(bf16[2,2,192,768]{3,2,1,0:T(8,128)(2,1)} %get-tuple-element.83), channel_id=1, source_target_pairs={{0,4},{1,5},{2,6},{3,7},{4,0},{5,1},{6,2},{7,3},{8,12},{9,13},{10,... | collective-permute-start | bytes 3538952 | tf_op jit(solution)/shard_map/ppermute | solution.py:493
  137.9 28.1 %collective-permute-start.23 = (bf16[2,2,192,768]{3,2,1,0:T(8,128)(2,1)}, bf16[2,2,192,768]{3,2,1,0:T(8,128)(2,1)S(1)}, u32[]{:S(2)}, u32[]{:S(2)}) collective-permute-start(bf16[2,2,192,768]{3,2,1,0:T(8,128)(2,1)} %get-tuple-element.84), channel_id=1, source_target_pairs={{0,2},{1,3},{2,0},{3,1},{4,6},{5,7},{6,4},{7,5},{8,10},{9,11},{10,... | collective-permute-start | bytes 3538952 | tf_op jit(solution)/shard_map/ppermute | solution.py:493
  156.4 12.0 %collective-permute-start.24 = (bf16[1,8,96,768]{3,2,1,0:T(8,128)(2,1)S(1)}, bf16[1,8,96,768]{3,2,1,0:T(8,128)(2,1)S(1)}, u32[]{:S(2)}, u32[]{:S(2)}) collective-permute-start(bf16[1,8,96,768]{3,2,1,0:T(8,128)(2,1)S(1)} %get-tuple-element.95), channel_id=1, source_target_pairs={{0,1},{1,0},{2,3},{3,2},{4,5},{5,4},{6,7},{7,6},{8,9},{9,8},{10,11... | collective-permute-start | bytes 3538952 | tf_op jit(solution)/shard_map/ppermute | solution.py:493
  156.5 11.9 %collective-permute-start.25 = (bf16[1,8,96,768]{3,2,1,0:T(8,128)(2,1)S(1)}, bf16[1,8,96,768]{3,2,1,0:T(8,128)(2,1)S(1)}, u32[]{:S(2)}, u32[]{:S(2)}) collective-permute-start(bf16[1,8,96,768]{3,2,1,0:T(8,128)(2,1)S(1)} %get-tuple-element.96), channel_id=1, source_target_pairs={{0,1},{1,0},{2,3},{3,2},{4,5},{5,4},{6,7},{7,6},{8,9},{9,8},{10,11... | collective-permute-start | bytes 3538952 | tf_op jit(solution)/shard_map/ppermute | solution.py:493
  166.1 20.7 %collective-permute-start.28 = (bf16[2,192,768]{2,1,0:T(8,128)(2,1)S(1)}, bf16[2,192,768]{2,1,0:T(8,128)(2,1)S(1)}, u32[]{:S(2)}, u32[]{:S(2)}) collective-permute-start(bf16[2,192,768]{2,1,0:T(8,128)(2,1)S(1)} %fusion.2), channel_id=1, source_target_pairs={{0,4},{1,5},{2,6},{3,7},{4,0},{5,1},{6,2},{7,3},{8,12},{9,13},{10,... | collective-permute-start | bytes 1769480 | tf_op jit(solution)/shard_map/ppermute | solution.py:493
  166.9 19.9 %collective-permute-start.27 = (bf16[2,192,768]{2,1,0:T(8,128)(2,1)S(1)}, bf16[2,192,768]{2,1,0:T(8,128)(2,1)S(1)}, u32[]{:S(2)}, u32[]{:S(2)}) collective-permute-start(bf16[2,192,768]{2,1,0:T(8,128)(2,1)S(1)} %fusion.1), channel_id=1, source_target_pairs={{0,2},{1,3},{2,0},{3,1},{4,6},{5,7},{6,4},{7,5},{8,10},{9,11},{10,... | collective-permute-start | bytes 1769480 | tf_op jit(solution)/shard_map/ppermute | solution.py:493
  169.9 24.4 %collective-permute-start.30 = (bf16[2,2,96,768]{3,2,1,0:T(8,128)(2,1)S(1)}, bf16[2,2,96,768]{3,2,1,0:T(8,128)(2,1)S(1)}, u32[]{:S(2)}, u32[]{:S(2)}) collective-permute-start(bf16[2,2,96,768]{3,2,1,0:T(8,128)(2,1)S(1)} %get-tuple-element.99), channel_id=1, source_target_pairs={{0,4},{1,5},{2,6},{3,7},{4,0},{5,1},{6,2},{7,3},{8,12},{9,13},{10,... | collective-permute-start | bytes 1769480 | tf_op jit(solution)/shard_map/ppermute | solution.py:493
  170.5 23.8 %collective-permute-start.31 = (bf16[2,2,96,768]{3,2,1,0:T(8,128)(2,1)S(1)}, bf16[2,2,96,768]{3,2,1,0:T(8,128)(2,1)S(1)}, u32[]{:S(2)}, u32[]{:S(2)}) collective-permute-start(bf16[2,2,96,768]{3,2,1,0:T(8,128)(2,1)S(1)} %get-tuple-element.100), channel_id=1, source_target_pairs={{0,2},{1,3},{2,0},{3,1},{4,6},{5,7},{6,4},{7,5},{8,10},{9,11},{10,... | collective-permute-start | bytes 1769480 | tf_op jit(solution)/shard_map/ppermute | solution.py:493
  187.6 16.2 %collective-permute-start.35 = (bf16[2,192,768]{2,1,0:T(8,128)(2,1)S(1)}, bf16[2,192,768]{2,1,0:T(8,128)(2,1)S(1)}, u32[]{:S(2)}, u32[]{:S(2)}) collective-permute-start(bf16[2,192,768]{2,1,0:T(8,128)(2,1)S(1)} %fusion), channel_id=1, source_target_pairs={{0,8},{1,9},{2,10},{3,11},{4,12},{5,13},{6,14},{7,15},{8,0},{9,1},... | collective-permute-start | bytes 1769480 | tf_op jit(solution)/shard_map/ppermute | solution.py:493
  194.4 8.4 %collective-permute-start.32 = (f32[16,768]{1,0:T(8,128)S(1)}, f32[16,768]{1,0:T(8,128)S(1)}, u32[]{:S(2)}, u32[]{:S(2)}) collective-permute-start(f32[16,768]{1,0:T(8,128)S(1)} %add.132), channel_id=1, source_target_pairs={{0,16},{1,17},{2,18},{3,19},{4,20},{5,21},{6,22},{7,23},{8,24},{9,... | collective-permute-start | bytes 147464 | tf_op jit(solution)/shard_map/ppermute | solution.py:493
  196.4 10.7 %collective-permute-start.34 = (bf16[2,96,768]{2,1,0:T(8,128)(2,1)S(1)}, bf16[2,96,768]{2,1,0:T(8,128)(2,1)S(1)}, u32[]{:S(2)}, u32[]{:S(2)}) collective-permute-start(bf16[2,96,768]{2,1,0:T(8,128)(2,1)S(1)} %fusion.7), channel_id=1, source_target_pairs={{0,4},{1,5},{2,6},{3,7},{4,0},{5,1},{6,2},{7,3},{8,12},{9,13},{10,... | collective-permute-start | bytes 884744 | tf_op jit(solution)/shard_map/ppermute | solution.py:493
  197.3 9.8 %collective-permute-start.33 = (bf16[2,96,768]{2,1,0:T(8,128)(2,1)S(1)}, bf16[2,96,768]{2,1,0:T(8,128)(2,1)S(1)}, u32[]{:S(2)}, u32[]{:S(2)}) collective-permute-start(bf16[2,96,768]{2,1,0:T(8,128)(2,1)S(1)} %fusion.6), channel_id=1, source_target_pairs={{0,2},{1,3},{2,0},{3,1},{4,6},{5,7},{6,4},{7,5},{8,10},{9,11},{10,... | collective-permute-start | bytes 884744 | tf_op jit(solution)/shard_map/ppermute | solution.py:493
  204.0 15.4 %collective-permute-start.38 = (bf16[192,768]{1,0:T(8,128)(2,1)S(1)}, bf16[192,768]{1,0:T(8,128)(2,1)S(1)}, u32[]{:S(2)}, u32[]{:S(2)}) collective-permute-start(bf16[192,768]{1,0:T(8,128)(2,1)S(1)} %fusion.4), channel_id=1, source_target_pairs={{0,16},{1,17},{2,18},{3,19},{4,20},{5,21},{6,22},{7,23},{8,24},{9,... | collective-permute-start | bytes 884744 | tf_op jit(solution)/shard_map/ppermute | solution.py:493
  207.9 7.8 %collective-permute-start.36 = (f32[16,768]{1,0:T(8,128)}, f32[16,768]{1,0:T(8,128)}, u32[]{:S(2)}, u32[]{:S(2)}) collective-permute-start(f32[16,768]{1,0:T(8,128)} %add.135), channel_id=1, source_target_pairs={{0,8},{1,9},{2,10},{3,11},{4,12},{5,13},{6,14},{7,15},{8,0},{9,1},... | collective-permute-start | bytes 147464 | tf_op jit(solution)/shard_map/ppermute | solution.py:493
  208.0 13.2 %collective-permute-start.37 = (bf16[2,96,768]{2,1,0:T(8,128)(2,1)}, bf16[2,96,768]{2,1,0:T(8,128)(2,1)S(1)}, u32[]{:S(2)}, u32[]{:S(2)}) collective-permute-start(bf16[2,96,768]{2,1,0:T(8,128)(2,1)} %fusion.5), channel_id=1, source_target_pairs={{0,8},{1,9},{2,10},{3,11},{4,12},{5,13},{6,14},{7,15},{8,0},{9,1},... | collective-permute-start | bytes 884744 | tf_op jit(solution)/shard_map/ppermute | solution.py:493
  (53 other events, 564.0 us)
Sparse Core Ops, SparseCore 0:
  11.6 95.0 all-gather.2

commit v5 on v4

--- a/solution.py
+++ b/solution.py
@@ -377,26 +377,8 @@
         store_blocks(dat1_ref, value, info_ref[WIDE])
 
 
-def late_kernel(
-    info_ref,
-    dq_ref,
-    a_ref,
-    actm_ref,
-    actt_ref,
-    d_ref,
-    x_ref,
-    y_ref,
-    dy_ref,
-    vec_ref,
-    sums_ref,
-    dbm_ref,
-    dbt_ref,
-    out_ref,
-    grad_ref,
-    small_ref,
-    acc,
-    acc2,
-    left,
+def tokens_kernel(
+    info_ref, dq_ref, a_ref, x_ref, dy_ref, vec_ref, sums_ref, dbm_ref, dbt_ref, grad_ref, small_ref, acc
 ):
     n = pl.program_id(0)
     dh = nt(dq_ref[0], a_ref[0])
@@ -408,17 +390,6 @@
     @pl.when(n > 0)
     def _():
         acc[...] += dh
-
-    pick(actm_ref, actt_ref, left)
-    y2 = nt(left[...], d_ref[...].reshape(D, D))
-
-    @pl.when(n == 0)
-    def _():
-        acc2[...] = y_ref[...] + y2 + vec_ref[4:5, :]
-
-    @pl.when(n > 0)
-    def _():
-        acc2[...] += y2
 
     @pl.when(n == pl.num_programs(0) - 1)
     def _():
@@ -439,7 +410,24 @@
                 small_ref[5 + j : 6 + j, :] = dbt_ref[at - 2]
 
         gather_back(grad_ref, dy_ref[...] + ln_back(grad, normed, rstd, vec_ref[0:1, :]), info_ref[ODD])
-        gather_back(out_ref, acc2[...], info_ref[ODD])
+
+
+def result_kernel(info_ref, actm_ref, actt_ref, d_ref, y_ref, vec_ref, out_ref, acc, left):
+    n = pl.program_id(0)
+    pick(actm_ref, actt_ref, left)
+    y2 = nt(left[...], d_ref[...].reshape(D, D))
+
+    @pl.when(n == 0)
+    def _():
+        acc[...] = y_ref[...] + y2 + vec_ref[4:5, :]
+
+    @pl.when(n > 0)
+    def _():
+        acc[...] += y2
+
+    @pl.when(n == pl.num_programs(0) - 1)
+    def _():
+        gather_back(out_ref, acc[...], info_ref[ODD])
 
 
 WIDE, ODD, BACK, ORDER = 0, 1, 2, 6
@@ -747,19 +735,27 @@
         [turned, turned, pltpu.VMEM((ROWS + HALF_ROWS, 256), BF)],
         units=4,
     )
+    grad_x, small = call(
+        tokens_kernel,
+        info,
+        [(dq, "panel"), (a, "panel"), (x, "fixed"), (dy, "fixed"), (vecs, "fixed"), (sums2, "fixed")]
+        + [(db_m, "fixed"), (db_t, "fixed")],
+        [result32, ((16, D), F32, "fixed")],
+        [wide_row],
+        units=1,
+        vmem="late",
+    )
     if direct:
         sa = Scatter(swap, *da_t)
-        sent = sm.step(dq)
-        dq = after(dq, *sent, *sa.step(*sent, own=da_m))
-    out, grad_x, small = call(
-        late_kernel,
+        sent = sm.step(small)
+        act_m = after(act_m, *sent, *sa.step(*sent, own=da_m))
+    (out,) = call(
+        result_kernel,
         info,
-        [(dq, "panel"), (a, "panel"), (act_m, "mine"), (act_t, "theirs")]
-        + [(full, "down"), (x, "fixed"), (y, "fixed"), (dy, "fixed")]
-        + [(vecs, "fixed"), (sums2, "fixed"), (db_m, "fixed"), (db_t, "fixed")],
-        [result32, result32, ((16, D), F32, "fixed")],
-        [wide_row, wide_row, pltpu.VMEM((ROWS, D), BF)],
-        units=2,
+        [(act_m, "mine"), (act_t, "theirs"), (full, "down"), (y, "fixed"), (vecs, "fixed")],
+        [result32],
+        [wide_row, pltpu.VMEM((ROWS, D), BF)],
+        units=1,
         vmem="late",
     )
     if direct:
@@ -768,7 +764,7 @@
             small = after(small, *wait)
             return small + swap(small, bit)
 
-        near = sm.step(small)
+        near = sm.step(out)
         small = reduced(reduced(small, CORE), LINE_X, *near)
         small = reduced(small, FAR_Z, *sa.step(small))
         far = sm.step()

time: 239 us -> 237 us (level)
    unnamed x87 -> x81, local copies, waits for them, and re-layouts: 19.9 us -> 18.7 us
    pallas_call x6 -> x7, Pallas kernels: 73.4 us -> 74.3 us  [call(): pl.pallas_call(kernel, grid_spec=pltpu.PrefetchScalarGridSpec(num_scalar_...]
  transfers between devices with their start and end apart: 42 -> 42, of which waited for: 19 -> 21; matrix products, arithmetic and copies ran while one was open for 3% -> 3% of each run, Pallas kernels for 30% -> 30%
where the time goes in v5:
time: 237 us; the launch traced here: 236 us
  Pallas kernels  79.9 us (34%)
  waiting for transfers between devices  76.7 us (32%)
  starting transfers between devices  34.6 us (15%)
  local copies, waits for them, and re-layouts  21 us (9%)
  between operations  14.5 us (6%)
  other arithmetic  9.42 us (4%)
    pallas_call x7, Pallas kernels, call(): pl.pallas_call(kernel, grid_spec=pltpu.PrefetchScalarGridSpec(num_scalar_...  74.3 us
    ppermute x41, waiting for transfers between devices, swap(): lax.ppermute(value, ('wide', 'narrow'), [(i, i ^ bit) for i in range(devi...  62.3 us
    ppermute x41, starting transfers between devices, swap(): lax.ppermute(value, ('wide', 'narrow'), [(i, i ^ bit) for i in range(devi...  34.5 us
    unnamed x81, local copies, waits for them, and re-layouts  18.7 us
    all_gather x1, waiting for transfers between devices, body(): full = lax.all_gather(mlp, ('wide', 'narrow'), axis=0, tiled=False)  14.4 us
    pallas_call x2, Pallas kernels, merge(): pl.pallas_call(merge_kernel, grid=(2, 4), in_specs=[taken] + gots, out_sp...  5.36 us
  transfers between devices with their start and end apart: 42, of which 21 were waited for; matrix products, arithmetic and copies ran while one was open for 3% of the time, Pallas kernels for 30%

profile of v5, /device:TPU:0, one launch (start us, length us, event | category | flops | bytes accessed | tf_op | source)
XLA Modules:
  0.0 236.2 jit_solution(2184315543211029333)
XLA Ops:
  7.3 1.7 pad_maximum_fusion.1
  11.0 3.7 %collective-permute-start.1 = (bf16[96,768]{1,0:T(8,128)(2,1)S(1)}, bf16[96,768]{1,0:T(8,128)(2,1)S(1)}, u32[]{:S(2)}, u32[]{:S(2)}) collective-permute-start(bf16[96,768]{1,0:T(8,128)(2,1)S(1)} %shard_map.255), channel_id=1, source_target_pairs={{0,16},{1,17},{2,18},{3,19},{4,20},{5,21},{6,22},{7,23},{8,24},{9,... | collective-permute-start | bytes 442376 | tf_op jit(solution)/shard_map/ppermute | solution.py:481
  14.7 7.6 %collective-permute-done.1 = bf16[96,768]{1,0:T(8,128)(2,1)S(1)} collective-permute-done((bf16[96,768]{1,0:T(8,128)(2,1)S(1)}, bf16[96,768]{1,0:T(8,128)(2,1)S(1)}, u32[]{:S(2)}, u32[]{:S(2)}) %collective-permute-start.1) | collective-permute-done | bytes 147488 | tf_op jit(solution)/shard_map/ppermute | solution.py:481
  25.5 1.5 collective-permute-start.5
  30.0 1.6 shard_map.254
  32.5 4.0 %collective-permute-done.2.refs_1_ = bf16[2,96,768]{2,1,0:T(8,128)(2,1)} collective-permute-done((bf16[2,96,768]{2,1,0:T(8,128)(2,1)S(1)}, bf16[2,96,768]{2,1,0:T(8,128)(2,1)}, u32[]{:S(2)}, u32[]{:S(2)}) %collective-permute-start.2) | collective-permute-done | bytes 294944 | tf_op jit(solution)/shard_map/ppermute | solution.py:481
  40.3 7.0 %collective-permute-done.6.refs_5_ = bf16[2,96,768]{2,1,0:T(8,128)(2,1)S(1)} collective-permute-done((bf16[2,96,768]{2,1,0:T(8,128)(2,1)}, bf16[2,96,768]{2,1,0:T(8,128)(2,1)S(1)}, u32[]{:S(2)}, u32[]{:S(2)}) %collective-permute-start.6) | collective-permute-done | bytes 294944 | tf_op jit(solution)/shard_map/ppermute | solution.py:481
  48.4 6.3 %collective-permute-done.7.refs_6_ = bf16[2,96,768]{2,1,0:T(8,128)(2,1)S(1)} collective-permute-done((bf16[2,96,768]{2,1,0:T(8,128)(2,1)S(1)}, bf16[2,96,768]{2,1,0:T(8,128)(2,1)S(1)}, u32[]{:S(2)}, u32[]{:S(2)}) %collective-permute-start.7) | collective-permute-done | bytes 294944 | tf_op jit(solution)/shard_map/ppermute | solution.py:481
  55.3 4.5 %collective-permute-done.8.refs_7_ = bf16[2,96,768]{2,1,0:T(8,128)(2,1)S(1)} collective-permute-done((bf16[2,96,768]{2,1,0:T(8,128)(2,1)S(1)}, bf16[2,96,768]{2,1,0:T(8,128)(2,1)S(1)}, u32[]{:S(2)}, u32[]{:S(2)}) %collective-permute-start.8) | collective-permute-done | bytes 294944 | tf_op jit(solution)/shard_map/ppermute | solution.py:481
  61.4 23.6 %shard_map.256 = (bf16[4,624,768]{2,1,0:T(8,128)(2,1)S(1)}, bf16[4,512,256]{2,1,0:T(8,128)(2,1)S(1)}, bf16[4,768,768]{2,1,0:T(8,128)(2,1)S(1)}, f32[512,768]{1,0:T(8,128)S(1)}, bf16[512,768]{1,0:T(8,128)(2,1)S(1)}) custom-call(s32[10]{0:T(128)S(1)} %pad_add_fusion.info_ref, bf16[624,768]{1,0:T(8,128)(2,1)S(1)} %get-tuple-element.68.h_ref, ...), custom_call_target="tpu_custom_call" | custom-call | flops 4831838208 | bytes 14548992 | tf_op jit(solution)/shard_map/pallas_call | solution.py:459
  85.0 2.2 copy-done.2
  88.1 1.9 copy-done.22
  92.2 14.4 %all-gather.3.cloned.1.call-done = bf16[6144,768]{1,0:T(8,128)(2,1)} async-done(((bf16[192,768]{1,0:T(8,128)(2,1)}), bf16[6144,768]{1,0:T(8,128)(2,1)}) %all-gather.3.cloned.1.call-update) | async-done | bytes 9437200 | tf_op jit(solution)/shard_map/all_gather | solution.py:651
  106.6 3.7 %copy-done = bf16[6144,768]{1,0:T(8,128)(2,1)S(1)} copy-done((bf16[6144,768]{1,0:T(8,128)(2,1)S(1)}, bf16[6144,768]{1,0:T(8,128)(2,1)}, u32[]{:S(2)}) %copy-start) | copy-done | bytes 9437208
  112.6 10.2 %shard_map.257 = (bf16[2,512,768]{2,1,0:T(8,128)(2,1)S(1)}, bf16[2,8,192,768]{3,2,1,0:T(8,128)(2,1)}, f32[2,1,768]{2,1,0:T(1,128)S(1)}, f32[512,768]{1,0:T(8,128)S(1)}) custom-call(s32[10]{0:T(128)S(1)} %pad_add_fusion.info_ref, bf16[512,768]{1,0:T(8,128)(2,1)S(1)} %copy-done.11, bf16[512,768]{1,0:T(8,128)(2,1)S(1)} %copy-done.8, ...), custom_call_target="tpu_custom_call" | custom-call | flops 6039797760 | bytes 40919040 | tf_op jit(solution)/shard_map/pallas_call | solution.py:459
  123.0 10.1 %shard_map.258 = (bf16[2,512,768]{2,1,0:T(8,128)(2,1)S(1)}, bf16[2,8,192,768]{3,2,1,0:T(8,128)(2,1)S(1)}, f32[2,1,768]{2,1,0:T(1,128)S(1)}, f32[512,768]{1,0:T(8...) custom-call(s32[10]{0:T(128)S(1)} %pad_add_fusion.info_ref, bf16[512,768]{1,0:T(8,128)(2,1)S(1)} %copy-done.11, ...), custom_call_target="tpu_custom_call" | custom-call | flops 6039797760 | bytes 50405376 | tf_op jit(solution)/shard_map/pallas_call | solution.py:459
  133.4 3.9 %shard_map.259 = (bf16[2,2,192,768]{3,2,1,0:T(8,128)(2,1)S(1)}, bf16[2,2,192,768]{3,2,1,0:T(8,128)(2,1)}, bf16[2,2,192,768]{3,2,1,0:T(8,128)(2,1)S(1)}, bf16[2,2,192,768]{3,2,1,0:T(8,128)(2,1)S(1)}) custom-call(bf16[2,8,192,768]{3,2,1,0:T(8,128)(2,1)S(1)} %get-tuple-element.79.own_ref, bf16[2,8,192,768]{3,2,1,0:T(8,128)(2,1)S(1)} %collective-permute-done.20.refs_0_), custom_call_target="tpu_custom_call" | custom-call | bytes 14155776 | tf_op jit(solution)/shard_map/pallas_call | solution.py:559
  139.4 2.1 copy-done.23
  141.5 15.8 %shard_map.260 = (bf16[2,8,96,768]{3,2,1,0:T(8,128)(2,1)S(1)}, bf16[1,8,96,768]{3,2,1,0:T(8,128)(2,1)S(1)}, bf16[1,8,96,768]{3,2,1,0:T(8,128)(2,1)S(1)}, bf16[4,512,768]{2,1,0:T(8,128)(2,1)S(1)}) custom-call(s32[10]{0:T(128)S(1)} %pad_add_fusion.info_ref, bf16[512,768]{1,0:T(8,128)(2,1)S(1)} %get-tuple-element.86.dz_ref, ...), custom_call_target="tpu_custom_call" | custom-call | flops 9663676416 | bytes 23035904 | tf_op jit(solution)/shard_map/pallas_call | solution.py:459
  157.9 6.8 %shard_map.261 = (f32[490,768]{1,0:T(8,128)}, f32[16,768]{1,0:T(8,128)S(1)}) custom-call(s32[10]{0:T(128)S(1)} %pad_add_fusion.info_ref, bf16[4,512,768]{2,1,0:T(8,128)(2,1)S(1)} %get-tuple-element.90.dq_ref, bf16[4,768,768]{2,1,0:T(8,128)(2,1)S(1)} %bitcast.70, f32[512,768]{1,0:T(8,128)S(1)} %copy-done.4, f32[512,768]{1,0:T(8,128)S(1)} %get-tuple-element.91.dy_ref, ...), custom_call_target="tpu_custom_call" | custom-call | flops 2415919104 | bytes 22142976 | tf_op jit(solution)/shard_map/pallas_call | solution.py:459
  167.6 1.5 collective-permute-start.27
  172.6 6.3 %shard_map.263 = f32[490,768]{1,0:T(8,128)} custom-call(s32[10]{0:T(128)S(1)} %pad_add_fusion.info_ref, bf16[2,512,768]{2,1,0:T(8,128)(2,1)S(1)} %get-tuple-element.106.actm_ref, bf16[2,512,768]{2,1,0:T(8,128)(2,1)S(1)} %get-tuple-element.107.actt_ref, bf16[8,4,2,96,768]{4,3,2,1,0:T(8,128)(2,1)S(1)} %bitcast.68, ...), custom_call_target="tpu_custom_call" | custom-call | flops 2415919104 | bytes 28360704 | tf_op jit(solution)/shard_map/pallas_call | solution.py:459
  178.9 4.2 %collective-permute-done.28 = bf16[2,192,768]{2,1,0:T(8,128)(2,1)S(1)} collective-permute-done((bf16[2,192,768]{2,1,0:T(8,128)(2,1)S(1)}, bf16[2,192,768]{2,1,0:T(8,128)(2,1)S(1)}, u32[]{:S(2)}, u32[]{:S(2)}) %collective-permute-start.28) | collective-permute-done | bytes 589856 | tf_op jit(solution)/shard_map/ppermute | solution.py:481
  187.1 7.8 %collective-permute-done.29 = f32[16,768]{1,0:T(8,128)S(1)} collective-permute-done((f32[16,768]{1,0:T(8,128)S(1)}, f32[16,768]{1,0:T(8,128)S(1)}, u32[]{:S(2)}, u32[]{:S(2)}) %collective-permute-start.29) | collective-permute-done | bytes 49184 | tf_op jit(solution)/shard_map/ppermute | solution.py:481
  195.1 2.0 collective-permute-start.32
  200.4 2.0 collective-permute-start.38
  202.3 1.6 collective-permute-done.34
  207.5 3.8 %collective-permute-done.36 = f32[16,768]{1,0:T(8,128)S(1)} collective-permute-done((f32[16,768]{1,0:T(8,128)S(1)}, f32[16,768]{1,0:T(8,128)S(1)}, u32[]{:S(2)}, u32[]{:S(2)}) %collective-permute-start.36) | collective-permute-done | bytes 49184 | tf_op jit(solution)/shard_map/ppermute | solution.py:481
  211.3 2.6 %collective-permute-done.38 = bf16[192,768]{1,0:T(8,128)(2,1)} collective-permute-done((bf16[192,768]{1,0:T(8,128)(2,1)S(1)}, bf16[192,768]{1,0:T(8,128)(2,1)}, u32[]{:S(2)}, u32[]{:S(2)}) %collective-permute-start.38) | collective-permute-done | bytes 294944 | tf_op jit(solution)/shard_map/ppermute | solution.py:481
  215.3 2.6 %collective-permute-done.37 = bf16[2,96,768]{2,1,0:T(8,128)(2,1)} collective-permute-done((bf16[2,96,768]{2,1,0:T(8,128)(2,1)}, bf16[2,96,768]{2,1,0:T(8,128)(2,1)}, u32[]{:S(2)}, u32[]{:S(2)}) %collective-permute-start.37) | collective-permute-done | bytes 294944 | tf_op jit(solution)/shard_map/ppermute | solution.py:481
  220.9 2.2 collective-permute-done.39
  223.8 2.3 collective-permute-done.40
  (187 shorter events, 50.2 us)
Async XLA Ops:
  7.2 99.4 %all-gather.3.cloned.1.call-start = ((), (), s32[]{:S(2)}) async-start(), calls=%async_computation | async-start | bytes 9732096 | tf_op jit(solution)/shard_map/all_gather | solution.py:651
  10.2 16.9 %collective-permute-start = (bf16[98,768]{1,0:T(8,128)(2,1)S(1)}, bf16[98,768]{1,0:T(8,128)(2,1)S(1)}, u32[]{:S(2)}, u32[]{:S(2)}) collective-permute-start(bf16[98,768]{1,0:T(8,128)(2,1)S(1)} %slice_select_fusion), channel_id=1, source_target_pairs={{0,1},{1,0},{2,3},{3,2},{4,5},{5,4},{6,7},{7,6},{8,9},{9,8},{10,11... | collective-permute-start | bytes 451592 | tf_op jit(solution)/shard_map/ppermute | solution.py:481
  11.0 11.3 %collective-permute-start.1 = (bf16[96,768]{1,0:T(8,128)(2,1)S(1)}, bf16[96,768]{1,0:T(8,128)(2,1)S(1)}, u32[]{:S(2)}, u32[]{:S(2)}) collective-permute-start(bf16[96,768]{1,0:T(8,128)(2,1)S(1)} %shard_map.255), channel_id=1, source_target_pairs={{0,16},{1,17},{2,18},{3,19},{4,20},{5,21},{6,22},{7,23},{8,24},{9,... | collective-permute-start | bytes 442376 | tf_op jit(solution)/shard_map/ppermute | solution.py:481
  22.3 14.2 %collective-permute-start.2 = (bf16[2,96,768]{2,1,0:T(8,128)(2,1)S(1)}, bf16[2,96,768]{2,1,0:T(8,128)(2,1)}, u32[]{:S(2)}, u32[]{:S(2)}) collective-permute-start(bf16[2,96,768]{2,1,0:T(8,128)(2,1)S(1)} %pad_maximum_fusion.refs_0_), channel_id=1, source_target_pairs={{0,8},{1,9},{2,10},{3,11},{4,12},{5,13},{6,14},{7,15},{8,0},{9,1},... | collective-permute-start | bytes 884744 | tf_op jit(solution)/shard_map/ppermute | solution.py:481
  24.0 15.3 %collective-permute-start.3 = (bf16[2,96,768]{2,1,0:T(8,128)(2,1)S(1)}, bf16[2,96,768]{2,1,0:T(8,128)(2,1)S(1)}, u32[]{:S(2)}, u32[]{:S(2)}) collective-permute-start(bf16[2,96,768]{2,1,0:T(8,128)(2,1)S(1)} %pad_maximum_fusion.refs_0_), channel_id=1, source_target_pairs={{0,4},{1,5},{2,6},{3,7},{4,0},{5,1},{6,2},{7,3},{8,12},{9,13},{10,... | collective-permute-start | bytes 884744 | tf_op jit(solution)/shard_map/ppermute | solution.py:481
  25.5 14.3 %collective-permute-start.5 = (bf16[2,96,768]{2,1,0:T(8,128)(2,1)S(1)}, bf16[2,96,768]{2,1,0:T(8,128)(2,1)S(1)}, u32[]{:S(2)}, u32[]{:S(2)}) collective-permute-start(bf16[2,96,768]{2,1,0:T(8,128)(2,1)S(1)} %pad_maximum_fusion.refs_0_), channel_id=1, source_target_pairs={{0,2},{1,3},{2,0},{3,1},{4,6},{5,7},{6,4},{7,5},{8,10},{9,11},{10,... | collective-permute-start | bytes 884744 | tf_op jit(solution)/shard_map/ppermute | solution.py:481
  27.0 12.8 %collective-permute-start.9 = (bf16[2,96,768]{2,1,0:T(8,128)(2,1)S(1)}, bf16[2,96,768]{2,1,0:T(8,128)(2,1)S(1)}, u32[]{:S(2)}, u32[]{:S(2)}) collective-permute-start(bf16[2,96,768]{2,1,0:T(8,128)(2,1)S(1)} %pad_maximum_fusion.refs_0_), channel_id=1, source_target_pairs={{0,1},{1,0},{2,3},{3,2},{4,5},{5,4},{6,7},{7,6},{8,9},{9,8},{10,11... | collective-permute-start | bytes 884744 | tf_op jit(solution)/shard_map/ppermute | solution.py:481
  36.6 10.8 %collective-permute-start.6 = (bf16[2,96,768]{2,1,0:T(8,128)(2,1)}, bf16[2,96,768]{2,1,0:T(8,128)(2,1)S(1)}, u32[]{:S(2)}, u32[]{:S(2)}) collective-permute-start(bf16[2,96,768]{2,1,0:T(8,128)(2,1)} %collective-permute-done.2.refs_1_), channel_id=1, source_target_pairs={{0,2},{1,3},{2,0},{3,1},{4,6},{5,7},{6,4},{7,5},{8,10},{9,11},{10,... | collective-permute-start | bytes 884744 | tf_op jit(solution)/shard_map/ppermute | solution.py:481
  37.8 10.6 %collective-permute-start.4 = (bf16[2,96,768]{2,1,0:T(8,128)(2,1)}, bf16[2,96,768]{2,1,0:T(8,128)(2,1)S(1)}, u32[]{:S(2)}, u32[]{:S(2)}) collective-permute-start(bf16[2,96,768]{2,1,0:T(8,128)(2,1)} %collective-permute-done.2.refs_1_), channel_id=1, source_target_pairs={{0,4},{1,5},{2,6},{3,7},{4,0},{5,1},{6,2},{7,3},{8,12},{9,13},{10,... | collective-permute-start | bytes 884744 | tf_op jit(solution)/shard_map/ppermute | solution.py:481
  39.3 15.4 %collective-permute-start.7 = (bf16[2,96,768]{2,1,0:T(8,128)(2,1)S(1)}, bf16[2,96,768]{2,1,0:T(8,128)(2,1)S(1)}, u32[]{:S(2)}, u32[]{:S(2)}) collective-permute-start(bf16[2,96,768]{2,1,0:T(8,128)(2,1)S(1)} %collective-permute-done.3.refs_2_), channel_id=1, source_target_pairs={{0,2},{1,3},{2,0},{3,1},{4,6},{5,7},{6,4},{7,5},{8,10},{9,11},{10,... | collective-permute-start | bytes 884744 | tf_op jit(solution)/shard_map/ppermute | solution.py:481
  39.8 14.9 %collective-permute-start.10 = (bf16[2,96,768]{2,1,0:T(8,128)(2,1)}, bf16[2,96,768]{2,1,0:T(8,128)(2,1)S(1)}, u32[]{:S(2)}, u32[]{:S(2)}) collective-permute-start(bf16[2,96,768]{2,1,0:T(8,128)(2,1)} %collective-permute-done.2.refs_1_), channel_id=1, source_target_pairs={{0,1},{1,0},{2,3},{3,2},{4,5},{5,4},{6,7},{7,6},{8,9},{9,8},{10,11... | collective-permute-start | bytes 884744 | tf_op jit(solution)/shard_map/ppermute | solution.py:481
  39.8 15.4 %collective-permute-start.11 = (bf16[2,96,768]{2,1,0:T(8,128)(2,1)S(1)}, bf16[2,96,768]{2,1,0:T(8,128)(2,1)S(1)}, u32[]{:S(2)}, u32[]{:S(2)}) collective-permute-start(bf16[2,96,768]{2,1,0:T(8,128)(2,1)S(1)} %collective-permute-done.3.refs_2_), channel_id=1, source_target_pairs={{0,1},{1,0},{2,3},{3,2},{4,5},{5,4},{6,7},{7,6},{8,9},{9,8},{10,11... | collective-permute-start | bytes 884744 | tf_op jit(solution)/shard_map/ppermute | solution.py:481
  47.3 12.5 %collective-permute-start.8 = (bf16[2,96,768]{2,1,0:T(8,128)(2,1)S(1)}, bf16[2,96,768]{2,1,0:T(8,128)(2,1)S(1)}, u32[]{:S(2)}, u32[]{:S(2)}) collective-permute-start(bf16[2,96,768]{2,1,0:T(8,128)(2,1)S(1)} %collective-permute-done.6.refs_5_), channel_id=1, source_target_pairs={{0,4},{1,5},{2,6},{3,7},{4,0},{5,1},{6,2},{7,3},{8,12},{9,13},{10,... | collective-permute-start | bytes 884744 | tf_op jit(solution)/shard_map/ppermute | solution.py:481
  48.4 11.4 %collective-permute-start.13 = (bf16[2,96,768]{2,1,0:T(8,128)(2,1)S(1)}, bf16[2,96,768]{2,1,0:T(8,128)(2,1)S(1)}, u32[]{:S(2)}, u32[]{:S(2)}) collective-permute-start(bf16[2,96,768]{2,1,0:T(8,128)(2,1)S(1)} %collective-permute-done.5.refs_4_), channel_id=1, source_target_pairs={{0,1},{1,0},{2,3},{3,2},{4,5},{5,4},{6,7},{7,6},{8,9},{9,8},{10,11... | collective-permute-start | bytes 884744 | tf_op jit(solution)/shard_map/ppermute | solution.py:481
  59.8 31.3 %collective-permute-start.18 = (f32[768]{0:T(1024)S(1)}, f32[768]{0:T(1024)S(1)}, u32[]{:S(2)}, u32[]{:S(2)}) collective-permute-start(f32[768]{0:T(1024)S(1)} %copy-done.37), channel_id=1, source_target_pairs={{0,1},{1,0},{2,3},{3,2},{4,5},{5,4},{6,7},{7,6},{8,9},{9,8},{10,11... | collective-permute-start | bytes 9224 | tf_op jit(solution)/shard_map/ppermute | solution.py:481
  60.3 30.6 %collective-permute-start.17 = (f32[768]{0:T(1024)S(1)}, f32[768]{0:T(1024)S(1)}, u32[]{:S(2)}, u32[]{:S(2)}) collective-permute-start(f32[768]{0:T(1024)S(1)} %copy-done.37), channel_id=1, source_target_pairs={{0,2},{1,3},{2,0},{3,1},{4,6},{5,7},{6,4},{7,5},{8,10},{9,11},{10,... | collective-permute-start | bytes 9224 | tf_op jit(solution)/shard_map/ppermute | solution.py:481
  122.7 10.7 %collective-permute-start.20 = (bf16[2,8,192,768]{3,2,1,0:T(8,128)(2,1)}, bf16[2,8,192,768]{3,2,1,0:T(8,128)(2,1)S(1)}, u32[]{:S(2)}, u32[]{:S(2)}) collective-permute-start(bf16[2,8,192,768]{3,2,1,0:T(8,128)(2,1)} %get-tuple-element.80), channel_id=1, source_target_pairs={{0,1},{1,0},{2,3},{3,2},{4,5},{5,4},{6,7},{7,6},{8,9},{9,8},{10,11... | collective-permute-start | bytes 14155784 | tf_op jit(solution)/shard_map/ppermute | solution.py:481
  137.3 28.4 %collective-permute-start.21 = (bf16[2,2,192,768]{3,2,1,0:T(8,128)(2,1)}, bf16[2,2,192,768]{3,2,1,0:T(8,128)(2,1)S(1)}, u32[]{:S(2)}, u32[]{:S(2)}) collective-permute-start(bf16[2,2,192,768]{3,2,1,0:T(8,128)(2,1)} %get-tuple-element.84), channel_id=1, source_target_pairs={{0,4},{1,5},{2,6},{3,7},{4,0},{5,1},{6,2},{7,3},{8,12},{9,13},{10,... | collective-permute-start | bytes 3538952 | tf_op jit(solution)/shard_map/ppermute | solution.py:481
  138.8 27.9 %collective-permute-start.22 = (bf16[2,2,192,768]{3,2,1,0:T(8,128)(2,1)S(1)}, bf16[2,2,192,768]{3,2,1,0:T(8,128)(2,1)S(1)}, u32[]{:S(2)}, u32[]{:S(2)}) collective-permute-start(bf16[2,2,192,768]{3,2,1,0:T(8,128)(2,1)S(1)} %get-tuple-element.85), channel_id=1, source_target_pairs={{0,2},{1,3},{2,0},{3,1},{4,6},{5,7},{6,4},{7,5},{8,10},{9,11},{10,... | collective-permute-start | bytes 3538952 | tf_op jit(solution)/shard_map/ppermute | solution.py:481
  157.3 11.8 %collective-permute-start.24 = (bf16[1,8,96,768]{3,2,1,0:T(8,128)(2,1)S(1)}, bf16[1,8,96,768]{3,2,1,0:T(8,128)(2,1)S(1)}, u32[]{:S(2)}, u32[]{:S(2)}) collective-permute-start(bf16[1,8,96,768]{3,2,1,0:T(8,128)(2,1)S(1)} %get-tuple-element.100), channel_id=1, source_target_pairs={{0,1},{1,0},{2,3},{3,2},{4,5},{5,4},{6,7},{7,6},{8,9},{9,8},{10,11... | collective-permute-start | bytes 3538952 | tf_op jit(solution)/shard_map/ppermute | solution.py:481
  157.4 11.7 %collective-permute-start.25 = (bf16[1,8,96,768]{3,2,1,0:T(8,128)(2,1)S(1)}, bf16[1,8,96,768]{3,2,1,0:T(8,128)(2,1)S(1)}, u32[]{:S(2)}, u32[]{:S(2)}) collective-permute-start(bf16[1,8,96,768]{3,2,1,0:T(8,128)(2,1)S(1)} %get-tuple-element.101), channel_id=1, source_target_pairs={{0,1},{1,0},{2,3},{3,2},{4,5},{5,4},{6,7},{7,6},{8,9},{9,8},{10,11... | collective-permute-start | bytes 3538952 | tf_op jit(solution)/shard_map/ppermute | solution.py:481
  166.8 16.3 %collective-permute-start.28 = (bf16[2,192,768]{2,1,0:T(8,128)(2,1)S(1)}, bf16[2,192,768]{2,1,0:T(8,128)(2,1)S(1)}, u32[]{:S(2)}, u32[]{:S(2)}) collective-permute-start(bf16[2,192,768]{2,1,0:T(8,128)(2,1)S(1)} %fusion.2), channel_id=1, source_target_pairs={{0,4},{1,5},{2,6},{3,7},{4,0},{5,1},{6,2},{7,3},{8,12},{9,13},{10,... | collective-permute-start | bytes 1769480 | tf_op jit(solution)/shard_map/ppermute | solution.py:481
  167.6 16.3 %collective-permute-start.27 = (bf16[2,192,768]{2,1,0:T(8,128)(2,1)S(1)}, bf16[2,192,768]{2,1,0:T(8,128)(2,1)S(1)}, u32[]{:S(2)}, u32[]{:S(2)}) collective-permute-start(bf16[2,192,768]{2,1,0:T(8,128)(2,1)S(1)} %fusion.1), channel_id=1, source_target_pairs={{0,2},{1,3},{2,0},{3,1},{4,6},{5,7},{6,4},{7,5},{8,10},{9,11},{10,... | collective-permute-start | bytes 1769480 | tf_op jit(solution)/shard_map/ppermute | solution.py:481
  170.6 24.3 %collective-permute-start.30 = (bf16[2,2,96,768]{3,2,1,0:T(8,128)(2,1)S(1)}, bf16[2,2,96,768]{3,2,1,0:T(8,128)(2,1)S(1)}, u32[]{:S(2)}, u32[]{:S(2)}) collective-permute-start(bf16[2,2,96,768]{3,2,1,0:T(8,128)(2,1)S(1)} %get-tuple-element.104), channel_id=1, source_target_pairs={{0,4},{1,5},{2,6},{3,7},{4,0},{5,1},{6,2},{7,3},{8,12},{9,13},{10,... | collective-permute-start | bytes 1769480 | tf_op jit(solution)/shard_map/ppermute | solution.py:481
  171.2 23.7 %collective-permute-start.31 = (bf16[2,2,96,768]{3,2,1,0:T(8,128)(2,1)S(1)}, bf16[2,2,96,768]{3,2,1,0:T(8,128)(2,1)S(1)}, u32[]{:S(2)}, u32[]{:S(2)}) collective-permute-start(bf16[2,2,96,768]{3,2,1,0:T(8,128)(2,1)S(1)} %get-tuple-element.105), channel_id=1, source_target_pairs={{0,2},{1,3},{2,0},{3,1},{4,6},{5,7},{6,4},{7,5},{8,10},{9,11},{10,... | collective-permute-start | bytes 1769480 | tf_op jit(solution)/shard_map/ppermute | solution.py:481
  184.2 10.7 %collective-permute-start.29 = (f32[16,768]{1,0:T(8,128)S(1)}, f32[16,768]{1,0:T(8,128)S(1)}, u32[]{:S(2)}, u32[]{:S(2)}) collective-permute-start(f32[16,768]{1,0:T(8,128)S(1)} %add.128), channel_id=1, source_target_pairs={{0,4},{1,5},{2,6},{3,7},{4,0},{5,1},{6,2},{7,3},{8,12},{9,13},{10,... | collective-permute-start | bytes 147464 | tf_op jit(solution)/shard_map/ppermute | solution.py:481
  185.7 14.5 %collective-permute-start.35 = (bf16[2,192,768]{2,1,0:T(8,128)(2,1)S(1)}, bf16[2,192,768]{2,1,0:T(8,128)(2,1)S(1)}, u32[]{:S(2)}, u32[]{:S(2)}) collective-permute-start(bf16[2,192,768]{2,1,0:T(8,128)(2,1)S(1)} %fusion), channel_id=1, source_target_pairs={{0,8},{1,9},{2,10},{3,11},{4,12},{5,13},{6,14},{7,15},{8,0},{9,1},... | collective-permute-start | bytes 1769480 | tf_op jit(solution)/shard_map/ppermute | solution.py:481
  197.1 6.8 %collective-permute-start.34 = (bf16[2,96,768]{2,1,0:T(8,128)(2,1)S(1)}, bf16[2,96,768]{2,1,0:T(8,128)(2,1)S(1)}, u32[]{:S(2)}, u32[]{:S(2)}) collective-permute-start(bf16[2,96,768]{2,1,0:T(8,128)(2,1)S(1)} %fusion.7), channel_id=1, source_target_pairs={{0,4},{1,5},{2,6},{3,7},{4,0},{5,1},{6,2},{7,3},{8,12},{9,13},{10,... | collective-permute-start | bytes 884744 | tf_op jit(solution)/shard_map/ppermute | solution.py:481
  197.9 6.7 %collective-permute-start.33 = (bf16[2,96,768]{2,1,0:T(8,128)(2,1)S(1)}, bf16[2,96,768]{2,1,0:T(8,128)(2,1)S(1)}, u32[]{:S(2)}, u32[]{:S(2)}) collective-permute-start(bf16[2,96,768]{2,1,0:T(8,128)(2,1)S(1)} %fusion.6), channel_id=1, source_target_pairs={{0,2},{1,3},{2,0},{3,1},{4,6},{5,7},{6,4},{7,5},{8,10},{9,11},{10,... | collective-permute-start | bytes 884744 | tf_op jit(solution)/shard_map/ppermute | solution.py:481
  200.4 13.5 %collective-permute-start.38 = (bf16[192,768]{1,0:T(8,128)(2,1)S(1)}, bf16[192,768]{1,0:T(8,128)(2,1)}, u32[]{:S(2)}, u32[]{:S(2)}) collective-permute-start(bf16[192,768]{1,0:T(8,128)(2,1)S(1)} %fusion.4), channel_id=1, source_target_pairs={{0,16},{1,17},{2,18},{3,19},{4,20},{5,21},{6,22},{7,23},{8,24},{9,... | collective-permute-start | bytes 884744 | tf_op jit(solution)/shard_map/ppermute | solution.py:481
  206.1 11.8 %collective-permute-start.37 = (bf16[2,96,768]{2,1,0:T(8,128)(2,1)}, bf16[2,96,768]{2,1,0:T(8,128)(2,1)}, u32[]{:S(2)}, u32[]{:S(2)}) collective-permute-start(bf16[2,96,768]{2,1,0:T(8,128)(2,1)} %fusion.5), channel_id=1, source_target_pairs={{0,8},{1,9},{2,10},{3,11},{4,12},{5,13},{6,14},{7,15},{8,0},{9,1},... | collective-permute-start | bytes 884744 | tf_op jit(solution)/shard_map/ppermute | solution.py:481
  218.9 7.2 %collective-permute-start.40 = (bf16[96,768]{1,0:T(8,128)(2,1)S(1)}, bf16[96,768]{1,0:T(8,128)(2,1)S(1)}, u32[]{:S(2)}, u32[]{:S(2)}) collective-permute-start(bf16[96,768]{1,0:T(8,128)(2,1)S(1)} %fusion.9), channel_id=1, source_target_pairs={{0,16},{1,17},{2,18},{3,19},{4,20},{5,21},{6,22},{7,23},{8,24},{9,... | collective-permute-start | bytes 442376 | tf_op jit(solution)/shard_map/ppermute | solution.py:481
  (50 other events, 527.6 us)
Sparse Core Ops, SparseCore 0:
  11.6 95.0 all-gather.2
